TPU v7x, 32 devices: a whole 2x2x4 slice. The times are simulated.
32 devices in a mesh: sta: 8 (over z, x), evt: 4 (over y, core).
Axes of the slice: x: 2, y: 2, z: 4, core: 2. Of those that a mesh axis runs over, the one named last changes fastest.
Arguments:
- waveforms: bfloat16 [128, 64, 1024], P(('evt', 'sta')), may hold values from -18 to 18
- pair_events: int32 [4096, 2], P('evt'), may hold values from 0 to 127, as said below
- pair_valid: int32 [4096], P('evt'), may hold values from 0 to 1, as said below
- presence: int32 [128, 64], P(None, 'sta'), may hold values 0 or 1
Outputs:
- correlation: bfloat16 [4096, 64, 256], P('evt', 'sta')
- pair_peak: float32 [4096], P('evt')
Inputs may be any that keep to these rules, and one draw needn't show every extreme that they name: `pair_events`: slot rows p * 1024 to (p + 1) * 1024 - 1 belong to block p; each row names first an event of block p (events p * 32 to (p + 1) * 32 - 1), then a different event at most 16 positions away from it; in every block the first row names the block's first event and the second row the block's last event, each with an event exactly 16 away. `pair_valid`: in each block of 1024 slots the valid slots come first; in every draw some block is full.
All inputs are finite; a program needn't handle non-finite values. No bound on the sum of `presence` on one device may be relied on, other than what follows from the above.
Results may differ from a plain program's by a relative error of at most 0.0064.
Values may be sent and summed in bfloat16 or wider, within the bound.
No kernel may reach another device: no remote copies, remote signals or barrier semaphores. Data moves between devices by JAX's collectives and lax.ppermute only.
A program may use at most 64 MiB of HBM per device.

v0:
```python
import math

import jax
import jax.numpy as jnp
from jax import lax
from jax.sharding import PartitionSpec as P

LAGS = 256


def padded_2(block, sides, width):
    for axis, dim in sides:
        count = lax.axis_size(axis)
        forward = [(i, i + 1) for i in range(count - 1)]
        backward = [(target, source) for source, target in forward]
        low = lax.ppermute(
            lax.slice_in_dim(block, block.shape[dim] - width, None, axis=dim), axis, forward
        )
        high = lax.ppermute(lax.slice_in_dim(block, 0, width, axis=dim), axis, backward)
        block = jnp.concatenate([low, block, high], axis=dim)
    return block


def spectral_tables(window, lag_count):
    half_width = window // 2
    sample_index = jnp.arange(window, dtype=jnp.int32)
    bin_index = jnp.arange(half_width, dtype=jnp.int32)
    phase_angle = (sample_index[:, None] * bin_index[None, :] % window).astype(jnp.float32) * (
        2.0 * math.pi / window
    )
    forward = (
        jnp.concatenate([jnp.cos(phase_angle), -jnp.sin(phase_angle)], axis=1) / math.sqrt(window)
    ).astype(jnp.bfloat16)
    shifts = jnp.arange(lag_count, dtype=jnp.int32) - lag_count // 2
    lag_angle = (bin_index[:, None] * shifts[None, :] % window).astype(jnp.float32) * (
        2.0 * math.pi / window
    )
    factor = jnp.where(bin_index == 0, 1.0, 2.0).astype(jnp.float32)
    inverse = jnp.concatenate(
        [factor[:, None] * jnp.cos(lag_angle), -factor[:, None] * jnp.sin(lag_angle)], axis=0
    ).astype(jnp.bfloat16)
    energy_weights = jnp.concatenate([factor, factor])
    return (forward, inverse, energy_weights)


def to_spectra(traces, forward):
    flattened = traces.reshape(-1, traces.shape[-1])
    result = jnp.dot(flattened, forward, preferred_element_type=jnp.float32).astype(jnp.bfloat16)
    return result.reshape(traces.shape[:-1] + (forward.shape[1],))


def body(waveforms, pair_events, pair_valid, presence):
    sta_count = lax.axis_size("sta")
    local_events, stations, window = waveforms.shape
    station_share = stations // sta_count
    forward, inverse, energy_weights = spectral_tables(window, LAGS)
    arrived = lax.all_to_all(waveforms, "sta", split_axis=1, concat_axis=0, tiled=True)
    spectra = to_spectra(arrived, forward)
    block_rows = spectra.shape[0]
    band_rows = block_rows // 2
    padded = padded_2(spectra, (("evt", 0),), band_rows)
    energy = jnp.sum(energy_weights * jnp.square(padded.astype(jnp.float32)), axis=-1) + 1e-06
    anchor = lax.axis_index("evt") * block_rows - band_rows
    half_width = window // 2
    pair_count = pair_events.shape[0]
    group_rows = min(128, pair_count)
    event_groups = pair_events.reshape(pair_count // group_rows, group_rows, 2)
    valid_groups = pair_valid.reshape(pair_count // group_rows, group_rows)

    def one_group(group_item):
        events_here, valid_rows = group_item
        first_event = events_here[:, 0]
        second_event = events_here[:, 1]
        first_local = first_event - anchor
        second_local = second_event - anchor
        first_spec = jnp.take(padded, first_local, axis=0).astype(jnp.float32)
        second_spec = jnp.take(padded, second_local, axis=0).astype(jnp.float32)
        first_real, first_imag = (first_spec[..., :half_width], first_spec[..., half_width:])
        second_real, second_imag = (second_spec[..., :half_width], second_spec[..., half_width:])
        cross_spec = jnp.concatenate(
            [
                first_real * second_real + first_imag * second_imag,
                first_real * second_imag - first_imag * second_real,
            ],
            axis=-1,
        ).astype(jnp.bfloat16)
        lagged = jnp.dot(
            cross_spec.reshape(-1, window), inverse, preferred_element_type=jnp.float32
        )
        lagged = lagged.reshape(group_rows, station_share, inverse.shape[1])
        norm_factor = lax.rsqrt(
            jnp.take(energy, first_local, axis=0) * jnp.take(energy, second_local, axis=0)
        )
        weight_mask = (
            valid_rows[:, None].astype(jnp.float32)
            * jnp.take(presence, first_event, axis=0).astype(jnp.float32)
            * jnp.take(presence, second_event, axis=0).astype(jnp.float32)
        )
        normalized = lagged * (norm_factor * weight_mask)[:, :, None]
        peak_terms = jnp.sum(jnp.max(normalized, axis=-1) * weight_mask, axis=-1)
        present = jnp.sum(weight_mask, axis=-1)
        return (normalized.astype(jnp.bfloat16), peak_terms, present)

    correlation, peak_terms, present = lax.map(one_group, (event_groups, valid_groups))
    totals, counts = lax.psum((peak_terms.reshape(pair_count), present.reshape(pair_count)), "sta")
    pair_peak = totals / jnp.maximum(counts, 1.0)
    return (correlation.reshape(pair_count, station_share, LAGS), pair_peak)


def solution(mesh):
    return jax.shard_map(
        body,
        mesh=mesh,
        in_specs=(P(("evt", "sta"), None, None), P("evt", None), P("evt"), P(None, "sta")),
        out_specs=(P("evt", "sta", None), P("evt")),
        check_vma=False,
    )
```

profile of v0, /device:TPU:4, one launch (start us, length us, event | category | flops | bytes accessed | tf_op | source)
XLA Modules:
  0.0 189.2 jit_solution(14598306707098952834)
XLA Ops:
  0.6 2.2 %copy.35 = bf16[4,64,1024]{2,0,1:T(4,128)(2,1)} copy(bf16[4,64,1024]{2,1,0:T(8,128)(2,1)} %param.12) | data formatting | bytes 1048576 | tf_op args[0]
  2.9 5.8 %all-to-all-start = ((bf16[4,64,1024]{2,0,1:T(4,128)(2,1)}), bf16[4,64,1024]{2,0,1:T(4,128)(2,1)S(1)}, u32[]{:S(2)}, u32[]{:S(2)}) async-start(bf16[4,64,1024]{2,0,1:T(4,128)(2,1)} %copy.35), calls=%async_computation | async-start | bytes 1048576 | tf_op jit(solution)/shard_map/all_to_all | solution.py:57
  8.7 9.1 %sine_negate_fusion = (f32[1024,512]{1,0:T(8,128)S(1)}, f32[1024,512]{1,0:T(8,128)}) fusion(), kind=kLoop, calls=%fused_computation.58 | loop fusion | flops 7864320 | bytes 4194304 | tf_op jit(solution)/shard_map/neg | solution.py:32
  17.8 5.4 %all-to-all-done = bf16[4,64,1024]{2,0,1:T(4,128)(2,1)S(1)} async-done(((bf16[4,64,1024]{2,0,1:T(4,128)(2,1)}), bf16[4,64,1024]{2,0,1:T(4,128)(2,1)S(1)}, u32[]{:S(2)}, u32[]{:S(2)}) %all-to-all-start) | async-done | bytes 524320 | tf_op jit(solution)/shard_map/all_to_all | solution.py:57
  23.4 1.4 copy-done
  24.8 0.7 fusion.27
  25.5 1.9 %collective-permute-start = (bf16[16,8,1024]{2,1,0:T(8,128)(2,1)S(1)}, bf16[16,8,1024]{2,1,0:T(8,128)(2,1)S(1)}, u32[]{:S(2)}, u32[]{:S(2)}) collective-permute-start(bf16[16,8,1024]{2,1,0:T(8,128)(2,1)S(1)} %get-tuple-element.174), channel_id=1, source_target_pairs={{0,1},{1,2},{2,3},{4,5},{5,6},{6,7},{8,9},{9,10},{10,11},{12,13},{... | collective-permute-start | bytes 786440 | tf_op jit(solution)/shard_map/ppermute | solution.py:16
  27.4 3.8 %collective-permute-start.1 = (bf16[16,8,1024]{2,1,0:T(8,128)(2,1)S(1)}, bf16[16,8,1024]{2,1,0:T(8,128)(2,1)S(1)}, u32[]{:S(2)}, u32[]{:S(2)}) collective-permute-start(bf16[16,8,1024]{2,1,0:T(8,128)(2,1)S(1)} %get-tuple-element.175), channel_id=1, source_target_pairs={{1,0},{2,1},{3,2},{5,4},{6,5},{7,6},{9,8},{10,9},{11,10},{13,12},{... | collective-permute-start | bytes 786440 | tf_op jit(solution)/shard_map/ppermute | solution.py:19
  31.3 2.3 %multiply_convert_fusion.1 = (bf16[512,256]{1,0:T(8,128)(2,1)S(1)}, bf16[512,256]{1,0:T(8,128)(2,1)S(1)}) fusion(s32[256]{0:T(256)S(1)} %iota_add_fusion, f32[512]{0:T(512)S(1)} %fusion.37, f32[512]{0:T(512)S(1)} %fusion.38), kind=kLoop, calls=%fused_computation.74 | loop fusion | flops 2359296 | bytes 529408 | tf_op jit(solution)/shard_map/convert.2
  33.8 0.8 pad_maximum_fusion.1
  35.3 133.5 %while.14 = (s32[]{:T(128)}, bf16[8,128,8,256]{3,2,1,0:T(8,128)(2,1)}, f32[8,128]{1,0:T(8,128)S(1)}, f32[8,128]{1,0:T(8,128)S(1)}, s32[8,128,2]{1,2,0:T(2,128)},...) while((s32[]{:T(128)}, ...), condition=%wide.region_5.9_spmd, body=%wide.region_1.8_spmd.sunk | while | flops 550259840 | bytes 37887928 | solution.py:104
  35.3 0.7 fusion.58
  39.6 0.7 gather_fusion.4
  40.3 2.0 %gather_fusion.5 = bf16[128,8,1024]{2,1,0:T(8,128)(2,1)} fusion(bf16[64,8,1024]{2,1,0:T(8,128)(2,1)S(1)} %get-tuple-element.319, s32[1024]{0:T(1024)S(1)} %pad_clamp_fusion.8), kind=kCustom, calls=%fused_computation.clone.clone.1 | custom fusion | bytes 4194816 | tf_op jit(solution)/shard_map/while/body/eval_jaxpr/jit(_take)/gather | solution.py:76
  42.3 6.5 %fusion.60 = (f32[128,8,1024]{2,0,1:T(8,128)S(1)}, f32[128,8,1024]{2,0,1:T(8,128)S(1)}) fusion(bf16[128,8,1024]{2,1,0:T(8,128)(2,1)S(1)} %gather_fusion.4, pred[128]{0:T(512)(128)(4,1)S(1)} %get-tuple-element.269, bf16[128,8,1024]{2,1,0:T(8,128)(2,1)} %gather_fusion.5, pred[128]{0:T(512)(128)(4,1)S(1)} %get-tuple-element.270), kind=kLoop, calls=%fused_computation.11.clone.1 | loop fusion | flops 4194304 | bytes 12583168 | tf_op jit(solution)/shard_map/while/body/eval_jaxpr/convert_element_type | solution.py:77
  48.8 1.2 add_convert_fusion.2
  50.1 0.8 fusion.61
  50.9 1.1 copy_dynamic-update-slice_fusion.2
  52.0 0.7 fusion.58
  56.3 0.7 gather_fusion.4
  57.0 2.0 %gather_fusion.5 = bf16[128,8,1024]{2,1,0:T(8,128)(2,1)} fusion(bf16[64,8,1024]{2,1,0:T(8,128)(2,1)S(1)} %get-tuple-element.319, s32[1024]{0:T(1024)S(1)} %pad_clamp_fusion.8), kind=kCustom, calls=%fused_computation.clone.clone.1 | custom fusion | bytes 4194816 | tf_op jit(solution)/shard_map/while/body/eval_jaxpr/jit(_take)/gather | solution.py:76
  59.0 6.5 %fusion.60 = (f32[128,8,1024]{2,0,1:T(8,128)S(1)}, f32[128,8,1024]{2,0,1:T(8,128)S(1)}) fusion(bf16[128,8,1024]{2,1,0:T(8,128)(2,1)S(1)} %gather_fusion.4, pred[128]{0:T(512)(128)(4,1)S(1)} %get-tuple-element.269, bf16[128,8,1024]{2,1,0:T(8,128)(2,1)} %gather_fusion.5, pred[128]{0:T(512)(128)(4,1)S(1)} %get-tuple-element.270), kind=kLoop, calls=%fused_computation.11.clone.1 | loop fusion | flops 4194304 | bytes 12583168 | tf_op jit(solution)/shard_map/while/body/eval_jaxpr/convert_element_type | solution.py:77
  65.5 1.2 add_convert_fusion.2
  66.7 0.8 fusion.61
  67.6 1.1 copy_dynamic-update-slice_fusion.2
  68.7 0.7 fusion.58
  73.0 0.7 gather_fusion.4
  73.7 2.0 %gather_fusion.5 = bf16[128,8,1024]{2,1,0:T(8,128)(2,1)} fusion(bf16[64,8,1024]{2,1,0:T(8,128)(2,1)S(1)} %get-tuple-element.319, s32[1024]{0:T(1024)S(1)} %pad_clamp_fusion.8), kind=kCustom, calls=%fused_computation.clone.clone.1 | custom fusion | bytes 4194816 | tf_op jit(solution)/shard_map/while/body/eval_jaxpr/jit(_take)/gather | solution.py:76
  75.7 6.5 %fusion.60 = (f32[128,8,1024]{2,0,1:T(8,128)S(1)}, f32[128,8,1024]{2,0,1:T(8,128)S(1)}) fusion(bf16[128,8,1024]{2,1,0:T(8,128)(2,1)S(1)} %gather_fusion.4, pred[128]{0:T(512)(128)(4,1)S(1)} %get-tuple-element.269, bf16[128,8,1024]{2,1,0:T(8,128)(2,1)} %gather_fusion.5, pred[128]{0:T(512)(128)(4,1)S(1)} %get-tuple-element.270), kind=kLoop, calls=%fused_computation.11.clone.1 | loop fusion | flops 4194304 | bytes 12583168 | tf_op jit(solution)/shard_map/while/body/eval_jaxpr/convert_element_type | solution.py:77
  82.2 1.2 add_convert_fusion.2
  83.4 0.8 fusion.61
  84.3 1.1 copy_dynamic-update-slice_fusion.2
  85.4 0.7 fusion.58
  89.7 0.7 gather_fusion.4
  90.4 2.0 %gather_fusion.5 = bf16[128,8,1024]{2,1,0:T(8,128)(2,1)} fusion(bf16[64,8,1024]{2,1,0:T(8,128)(2,1)S(1)} %get-tuple-element.319, s32[1024]{0:T(1024)S(1)} %pad_clamp_fusion.8), kind=kCustom, calls=%fused_computation.clone.clone.1 | custom fusion | bytes 4194816 | tf_op jit(solution)/shard_map/while/body/eval_jaxpr/jit(_take)/gather | solution.py:76
  92.4 6.5 %fusion.60 = (f32[128,8,1024]{2,0,1:T(8,128)S(1)}, f32[128,8,1024]{2,0,1:T(8,128)S(1)}) fusion(bf16[128,8,1024]{2,1,0:T(8,128)(2,1)S(1)} %gather_fusion.4, pred[128]{0:T(512)(128)(4,1)S(1)} %get-tuple-element.269, bf16[128,8,1024]{2,1,0:T(8,128)(2,1)} %gather_fusion.5, pred[128]{0:T(512)(128)(4,1)S(1)} %get-tuple-element.270), kind=kLoop, calls=%fused_computation.11.clone.1 | loop fusion | flops 4194304 | bytes 12583168 | tf_op jit(solution)/shard_map/while/body/eval_jaxpr/convert_element_type | solution.py:77
  98.9 1.2 add_convert_fusion.2
  100.1 0.8 fusion.61
  101.0 1.1 copy_dynamic-update-slice_fusion.2
  102.1 0.7 fusion.58
  107.1 2.0 %gather_fusion.5 = bf16[128,8,1024]{2,1,0:T(8,128)(2,1)} fusion(bf16[64,8,1024]{2,1,0:T(8,128)(2,1)S(1)} %get-tuple-element.319, s32[1024]{0:T(1024)S(1)} %pad_clamp_fusion.8), kind=kCustom, calls=%fused_computation.clone.clone.1 | custom fusion | bytes 4194816 | tf_op jit(solution)/shard_map/while/body/eval_jaxpr/jit(_take)/gather | solution.py:76
  109.1 6.5 %fusion.60 = (f32[128,8,1024]{2,0,1:T(8,128)S(1)}, f32[128,8,1024]{2,0,1:T(8,128)S(1)}) fusion(bf16[128,8,1024]{2,1,0:T(8,128)(2,1)S(1)} %gather_fusion.4, pred[128]{0:T(512)(128)(4,1)S(1)} %get-tuple-element.269, bf16[128,8,1024]{2,1,0:T(8,128)(2,1)} %gather_fusion.5, pred[128]{0:T(512)(128)(4,1)S(1)} %get-tuple-element.270), kind=kLoop, calls=%fused_computation.11.clone.1 | loop fusion | flops 4194304 | bytes 12583168 | tf_op jit(solution)/shard_map/while/body/eval_jaxpr/convert_element_type | solution.py:77
  115.6 1.2 add_convert_fusion.2
  116.8 0.8 fusion.61
  117.7 1.1 copy_dynamic-update-slice_fusion.2
  118.8 0.7 fusion.58
  123.8 2.0 %gather_fusion.5 = bf16[128,8,1024]{2,1,0:T(8,128)(2,1)} fusion(bf16[64,8,1024]{2,1,0:T(8,128)(2,1)S(1)} %get-tuple-element.319, s32[1024]{0:T(1024)S(1)} %pad_clamp_fusion.8), kind=kCustom, calls=%fused_computation.clone.clone.1 | custom fusion | bytes 4194816 | tf_op jit(solution)/shard_map/while/body/eval_jaxpr/jit(_take)/gather | solution.py:76
  125.8 6.5 %fusion.60 = (f32[128,8,1024]{2,0,1:T(8,128)S(1)}, f32[128,8,1024]{2,0,1:T(8,128)S(1)}) fusion(bf16[128,8,1024]{2,1,0:T(8,128)(2,1)S(1)} %gather_fusion.4, pred[128]{0:T(512)(128)(4,1)S(1)} %get-tuple-element.269, bf16[128,8,1024]{2,1,0:T(8,128)(2,1)} %gather_fusion.5, pred[128]{0:T(512)(128)(4,1)S(1)} %get-tuple-element.270), kind=kLoop, calls=%fused_computation.11.clone.1 | loop fusion | flops 4194304 | bytes 12583168 | tf_op jit(solution)/shard_map/while/body/eval_jaxpr/convert_element_type | solution.py:77
  132.3 1.2 add_convert_fusion.2
  133.5 0.8 fusion.61
  134.4 1.1 copy_dynamic-update-slice_fusion.2
  135.5 0.7 fusion.58
  140.5 2.0 %gather_fusion.5 = bf16[128,8,1024]{2,1,0:T(8,128)(2,1)} fusion(bf16[64,8,1024]{2,1,0:T(8,128)(2,1)S(1)} %get-tuple-element.319, s32[1024]{0:T(1024)S(1)} %pad_clamp_fusion.8), kind=kCustom, calls=%fused_computation.clone.clone.1 | custom fusion | bytes 4194816 | tf_op jit(solution)/shard_map/while/body/eval_jaxpr/jit(_take)/gather | solution.py:76
  142.5 6.5 %fusion.60 = (f32[128,8,1024]{2,0,1:T(8,128)S(1)}, f32[128,8,1024]{2,0,1:T(8,128)S(1)}) fusion(bf16[128,8,1024]{2,1,0:T(8,128)(2,1)S(1)} %gather_fusion.4, pred[128]{0:T(512)(128)(4,1)S(1)} %get-tuple-element.269, bf16[128,8,1024]{2,1,0:T(8,128)(2,1)} %gather_fusion.5, pred[128]{0:T(512)(128)(4,1)S(1)} %get-tuple-element.270), kind=kLoop, calls=%fused_computation.11.clone.1 | loop fusion | flops 4194304 | bytes 12583168 | tf_op jit(solution)/shard_map/while/body/eval_jaxpr/convert_element_type | solution.py:77
  149.0 1.2 add_convert_fusion.2
  150.2 0.8 fusion.61
  151.1 1.1 copy_dynamic-update-slice_fusion.2
  152.2 0.7 fusion.58
  157.2 2.0 %gather_fusion.5 = bf16[128,8,1024]{2,1,0:T(8,128)(2,1)} fusion(bf16[64,8,1024]{2,1,0:T(8,128)(2,1)S(1)} %get-tuple-element.319, s32[1024]{0:T(1024)S(1)} %pad_clamp_fusion.8), kind=kCustom, calls=%fused_computation.clone.clone.1 | custom fusion | bytes 4194816 | tf_op jit(solution)/shard_map/while/body/eval_jaxpr/jit(_take)/gather | solution.py:76
  159.2 6.5 %fusion.60 = (f32[128,8,1024]{2,0,1:T(8,128)S(1)}, f32[128,8,1024]{2,0,1:T(8,128)S(1)}) fusion(bf16[128,8,1024]{2,1,0:T(8,128)(2,1)S(1)} %gather_fusion.4, pred[128]{0:T(512)(128)(4,1)S(1)} %get-tuple-element.269, bf16[128,8,1024]{2,1,0:T(8,128)(2,1)} %gather_fusion.5, pred[128]{0:T(512)(128)(4,1)S(1)} %get-tuple-element.270), kind=kLoop, calls=%fused_computation.11.clone.1 | loop fusion | flops 4194304 | bytes 12583168 | tf_op jit(solution)/shard_map/while/body/eval_jaxpr/convert_element_type | solution.py:77
  165.7 1.2 add_convert_fusion.2
  166.9 0.8 fusion.61
  167.8 1.1 copy_dynamic-update-slice_fusion.2
  168.9 19.7 %all-reduce = (f32[1024]{0:T(1024)S(1)}, f32[1024]{0:T(1024)S(1)}) all-reduce(f32[1024]{0:T(1024)S(1)} %bitcast.63, f32[1024]{0:T(1024)S(1)} %bitcast.62), channel_id=1, replica_groups=mesh['sta'=8,'evt'=4] {'sta'}, use_global_device_ids=true, to_apply=%region_6.10 | all-reduce | flops 2048 | bytes 16384 | tf_op jit(solution)/shard_map/psum | solution.py:105
  (175 shorter events, 33.8 us)
Async XLA Ops:
  2.9 20.3 %all-to-all-start = ((bf16[4,64,1024]{2,0,1:T(4,128)(2,1)}), bf16[4,64,1024]{2,0,1:T(4,128)(2,1)S(1)}, u32[]{:S(2)}, u32[]{:S(2)}) async-start(bf16[4,64,1024]{2,0,1:T(4,128)(2,1)} %copy.35), calls=%async_computation | async-start | bytes 1048576 | tf_op jit(solution)/shard_map/all_to_all | solution.py:57
  23.2 1.6 copy-start
  24.7 8.9 %copy-start.2 = (s32[128,8]{0,1:T(8,128)S(1)}, s32[128,8]{0,1:T(8,128)}, u32[]{:S(2)}) copy-start(s32[128,8]{0,1:T(8,128)} %param.15) | copy-start | bytes 12292
  25.5 9.1 %collective-permute-start = (bf16[16,8,1024]{2,1,0:T(8,128)(2,1)S(1)}, bf16[16,8,1024]{2,1,0:T(8,128)(2,1)S(1)}, u32[]{:S(2)}, u32[]{:S(2)}) collective-permute-start(bf16[16,8,1024]{2,1,0:T(8,128)(2,1)S(1)} %get-tuple-element.174), channel_id=1, source_target_pairs={{0,1},{1,2},{2,3},{4,5},{5,6},{6,7},{8,9},{9,10},{10,11},{12,13},{... | collective-permute-start | bytes 786440 | tf_op jit(solution)/shard_map/ppermute | solution.py:16
  27.4 7.5 %collective-permute-start.1 = (bf16[16,8,1024]{2,1,0:T(8,128)(2,1)S(1)}, bf16[16,8,1024]{2,1,0:T(8,128)(2,1)S(1)}, u32[]{:S(2)}, u32[]{:S(2)}) collective-permute-start(bf16[16,8,1024]{2,1,0:T(8,128)(2,1)S(1)} %get-tuple-element.175), channel_id=1, source_target_pairs={{1,0},{2,1},{3,2},{5,4},{6,5},{7,6},{9,8},{10,9},{11,10},{13,12},{... | collective-permute-start | bytes 786440 | tf_op jit(solution)/shard_map/ppermute | solution.py:19
  48.8 1.2 copy-start.1
  65.5 1.2 copy-start.1
  82.2 1.2 copy-start.1
  98.9 1.2 copy-start.1
  115.6 1.2 copy-start.1
  132.3 1.2 copy-start.1
  149.0 1.2 copy-start.1
  165.7 1.2 copy-start.1
where the time goes:
time: 190 us; the launch traced here: 189 us
  other arithmetic  80.9 us (43%)
  local copies, waits for them, and re-layouts  63 us (33%)
  blocking collectives  19.7 us (10%)
  starting transfers between devices  11.5 us (6%)
  matrix products  7.01 us (4%)
  waiting for transfers between devices  5.74 us (3%)
    convert_element_type x8, other arithmetic, one_group(): second_spec = jnp.take(padded, second_local, axis=0).astype(jnp.float32)  51.6 us
    psum x1, blocking collectives, body(): lax.psum((peak_terms.reshape(pair_count), present.reshape(pair_count)), '...  19.7 us
    gather x8, local copies, waits for them, and re-layouts, one_group(): first_spec = jnp.take(padded, first_local, axis=0).astype(jnp.float32)  16.2 us
    another operation x11, other arithmetic  12.1 us
    dynamic_update_slice x24, local copies, waits for them, and re-layouts, body(): lax.map(one_group, (event_groups, valid_groups))  9.29 us
    neg x1, other arithmetic, spectral_tables(): -jnp.sin(phase_angle)  9.11 us
    dot_general x8, matrix products, one_group(): jnp.dot(cross_spec.reshape(-1, window), inverse, preferred_element_type=j...  6.29 us
    all_to_all x1, starting transfers between devices, body(): lax.all_to_all(waveforms, 'sta', split_axis=1, concat_axis=0, tiled=True)  5.81 us
  transfers between devices with their start and end apart: 3, of which 2 were waited for; matrix products, arithmetic and copies ran while one was open for 7% of the time, Pallas kernels for 0%

commit v1 on v0

v1 whole, which is shorter than its diff:
```python
import functools
import math

import jax
import jax.numpy as jnp
import numpy as np
from jax import lax
from jax.experimental import pallas as pl
from jax.experimental.pallas import tpu as pltpu
from jax.sharding import PartitionSpec as P

LAGS = 256
LANES = 128


def spectral_tables(window, lag_count):
    half = window // 2
    sample = np.arange(window, dtype=np.int64)
    bins = np.arange(half, dtype=np.int64)
    angle = (sample[:, None] * bins[None, :] % window) * (2.0 * math.pi / window)
    forward = np.concatenate([np.cos(angle), -np.sin(angle)], axis=1) / math.sqrt(window)
    shifts = np.arange(lag_count, dtype=np.int64) - lag_count // 2
    lag_angle = (bins[:, None] * shifts[None, :] % window) * (2.0 * math.pi / window)
    factor = np.where(bins == 0, 1.0, 2.0)[:, None]
    inverse = np.concatenate([factor * np.cos(lag_angle), -factor * np.sin(lag_angle)], axis=0)
    weights = np.concatenate([factor[:, 0], factor[:, 0]])[None, :]
    return (
        jnp.asarray(forward.astype(jnp.bfloat16)),
        jnp.asarray(inverse.astype(jnp.bfloat16)),
        jnp.asarray(weights.astype(np.float32)),
    )


def pair_kernel(
    group, chunk, parts, slots_ref, *refs
):
    traces = refs[:parts]
    (
        presence_ref, forward_ref, inverse_ref, weights_ref,
        out_ref, peak_ref,
        spec_ref, gain_ref, lhs_ref,
    ) = refs[parts:]
    stations, window = spec_ref.shape[1:]
    half = window // 2
    events = spec_ref.shape[0]

    @pl.when(pl.program_id(0) == 0)
    def _():
        start = 0
        for ref in traces:
            rows = ref.shape[0]
            count = rows // stations
            result = jnp.dot(ref[...], forward_ref[...], preferred_element_type=jnp.float32)
            rounded = result.astype(jnp.bfloat16).astype(jnp.float32)
            spec_ref[pl.ds(start, count)] = rounded.reshape(count, stations, window)
            power = jnp.square(rounded) * weights_ref[...]
            energy = jnp.sum(power, axis=1, keepdims=True) + 1e-06
            gain = jnp.broadcast_to(lax.rsqrt(energy), (rows, LANES))
            gain = gain.reshape(count, stations, LANES) * presence_ref[pl.ds(start, count)]
            gain_ref[pl.ds(start, count)] = gain
            start += count
        gain_ref[events] = jnp.zeros((stations, LANES), jnp.float32)

    base = pl.program_id(0) * group
    lane = lax.broadcasted_iota(jnp.int32, (stations, LANES), 1)

    def cross(pair):
        first = spec_ref[slots_ref[0, pair]]
        second = spec_ref[slots_ref[1, pair]]
        ra, ia = first[:, :half], first[:, half:]
        rb, ib = second[:, :half], second[:, half:]
        return jnp.concatenate([ra * rb + ia * ib, ra * ib - ia * rb], axis=1)

    def one_chunk(index, peaks):
        first_pair = base + index * chunk
        for j in range(0, chunk, 2):
            both = jnp.concatenate([cross(first_pair + j), cross(first_pair + j + 1)], axis=0)
            lhs_ref[pl.ds(j * stations, 2 * stations), :] = both.astype(jnp.bfloat16)
        lagged = jnp.dot(lhs_ref[...], inverse_ref[...], preferred_element_type=jnp.float32)
        for j in range(0, chunk, 2):
            rows = []
            for i in (j, j + 1):
                pair = first_pair + i
                gain = gain_ref[slots_ref[2, pair]] * gain_ref[slots_ref[1, pair]]
                scaled = lagged[i * stations:(i + 1) * stations] * jnp.concatenate([gain, gain], axis=1)
                rows.append(scaled)
                top = jnp.max(scaled, axis=1, keepdims=True)
                peaks = jnp.where(lane == index * chunk + i, top, peaks)
            block = jnp.concatenate(rows, axis=0).astype(jnp.bfloat16)
            start = pl.multiple_of(index * chunk * stations, chunk * stations) + j * stations
            out_ref[pl.ds(start, 2 * stations), :] = block
        return peaks

    peaks = lax.fori_loop(0, group // chunk, one_chunk, jnp.zeros((stations, LANES), jnp.float32))
    peak_ref[0] = jnp.sum(peaks, axis=0, keepdims=True)


def pair_call(slots, traces, presence, tables):
    forward, inverse, weights = tables
    window = forward.shape[0]
    lags = inverse.shape[1]
    pairs = slots.shape[1]
    events, stations = presence.shape[:2]
    group = LANES
    chunk = 32
    vmem = pl.BlockSpec(memory_space=pltpu.VMEM)
    return pl.pallas_call(
        functools.partial(pair_kernel, group, chunk, len(traces)),
        grid=(pairs // group,),
        out_shape=(
            jax.ShapeDtypeStruct((pairs * stations, lags), jnp.bfloat16),
            jax.ShapeDtypeStruct((pairs // group, 1, group), jnp.float32),
        ),
        in_specs=[pl.BlockSpec(memory_space=pltpu.SMEM)] + [vmem] * (len(traces) + 4),
        out_specs=(
            pl.BlockSpec((group * stations, lags), lambda i: (i, 0)),
            pl.BlockSpec((1, 1, group), lambda i: (i, 0, 0)),
        ),
        scratch_shapes=[
            pltpu.VMEM((events, stations, window), jnp.float32),
            pltpu.VMEM((events + 1, stations, LANES), jnp.float32),
            pltpu.VMEM((chunk * stations, window), jnp.bfloat16),
        ],
        compiler_params=pltpu.CompilerParams(vmem_limit_bytes=56 * 1024 * 1024),
        cost_estimate=pl.CostEstimate(flops=4_500_000_000, bytes_accessed=8_000_000, transcendentals=0),
    )(slots, *traces, presence, forward, inverse, weights)


def exchange(waveforms, sta_count):
    events, stations, window = waveforms.shape
    share = stations // sta_count
    blocks = waveforms.reshape(events, sta_count, share, window)
    me = lax.axis_index("sta")
    half = sta_count // 2
    evt_count = lax.axis_size("evt")
    toward, away = [], []
    for e in range(evt_count):
        for s in range(sta_count):
            step = -1 if s < half else 1
            for pairs, target in ((toward, e + step), (away, e - step)):
                if 0 <= target < evt_count:
                    pairs.append((s * evt_count + e, s * evt_count + target))
    pieces = [lax.dynamic_index_in_dim(blocks, me, axis=1, keepdims=False)]
    for j in range(1, sta_count):
        piece = lax.dynamic_index_in_dim(blocks, me ^ j, axis=1, keepdims=False)
        pieces.append(lax.ppermute(piece, "sta", [(i, i ^ j) for i in range(sta_count)]))
    rows = half * events * share
    near = jnp.concatenate(pieces[:half], axis=0).reshape(rows, window)
    far = jnp.concatenate(pieces[half:], axis=0).reshape(rows, window)
    near_halo = lax.ppermute(near, ("sta", "evt"), toward)
    far_halo = lax.ppermute(far, ("sta", "evt"), away)
    return (near, far, near_halo, far_halo), me


def exchange_whole(waveforms, sta_count):
    events, stations, window = waveforms.shape
    share = stations // sta_count
    arrived = lax.all_to_all(waveforms, "sta", split_axis=1, concat_axis=0, tiled=True)
    arrived = arrived.reshape(-1, window)
    half = arrived.shape[0] // 2
    count = lax.axis_size("evt")
    down = [(i, i - 1) for i in range(1, count)]
    up = [(i, i + 1) for i in range(count - 1)]
    next_low = lax.ppermute(arrived[:half], "evt", down)
    last_high = lax.ppermute(arrived[half:], "evt", up)
    return (arrived, next_low, last_high), jnp.int32(0)


def body(waveforms, pair_events, pair_valid, presence):
    sta_count = lax.axis_size("sta")
    local_events, stations, window = waveforms.shape
    share = stations // sta_count
    block = sta_count * local_events
    tables = spectral_tables(window, LAGS)
    direct = sta_count <= 8 and sta_count & (sta_count - 1) == 0
    traces, me = (exchange if direct else exchange_whole)(waveforms, sta_count)

    start = lax.axis_index("evt") * block
    offset = pair_events - start
    inside = (offset >= 0) & (offset < block)
    flip = me * local_events
    slot = jnp.where(inside, 0, block) + ((offset % block) ^ flip)
    first, second = slot[:, 0], slot[:, 1]
    gained = jnp.where(pair_valid > 0, first, 2 * block)
    slots = jnp.stack([first, second, gained]).astype(jnp.int32)

    place = jnp.arange(2 * block, dtype=jnp.int32)
    relative = (place % block) ^ flip
    relative = jnp.where(
        place < block, relative, jnp.where(relative < block // 2, relative + block, relative - block)
    )
    held = jnp.clip(start + relative, 0, presence.shape[0] - 1)
    present = presence.astype(jnp.float32)
    slot_presence = jnp.broadcast_to(
        jnp.take(present, held, axis=0)[:, :, None], (2 * block, share, LANES)
    )
    both = jnp.take(present, pair_events[:, 0], axis=0) * jnp.take(present, pair_events[:, 1], axis=0)
    counts = jnp.sum(both, axis=1) * pair_valid.astype(jnp.float32)

    correlation, peaks = pair_call(slots, traces, slot_presence, tables)
    sums = jnp.stack([peaks.reshape(-1), counts])
    if direct:
        step = sta_count // 2
        while step:
            sums = sums + lax.ppermute(sums, "sta", [(i, i ^ step) for i in range(sta_count)])
            step //= 2
    else:
        sums = lax.psum(sums, "sta")
    pair_peak = sums[0] / jnp.maximum(sums[1], 1.0)
    return correlation.reshape(-1, share, LAGS), pair_peak


def solution(mesh):
    return jax.shard_map(
        body,
        mesh=mesh,
        in_specs=(P(("evt", "sta"), None, None), P("evt", None), P("evt"), P(None, "sta")),
        out_specs=(P("evt", "sta", None), P("evt")),
        check_vma=False,
    )
```

time: 190 us -> 70.8 us (0.37)
  other arithmetic: 80.9 us -> 4.78 us
  local copies, waits for them, and re-layouts: 63 us -> 9.81 us
  blocking collectives: 19.7 us -> 0 us
  Pallas kernels: 0 us -> 18.9 us
  waiting for transfers between devices: 5.74 us -> 20.3 us
  matrix products: 7.01 us -> 0 us
  starting transfers between devices: 11.5 us -> 15.7 us
    convert_element_type x16 -> x1, other arithmetic: 57.2 us -> 0.01 us  [body(): present = presence.astype(jnp.float32)]
    gather x80 -> x3, local copies, waits for them, and re-layouts: 44.3 us -> 6.22 us  [the longest x1 2.81 us: body(): jnp.take(present, pair_events[:, 0], axis=0)]
    ppermute x2 -> x12, waiting for transfers between devices: 0.39 us -> 20.3 us  [the longest x3 11.1 us: body(): lax.ppermute(sums, 'sta', [(i, i ^ step) for i in range(sta_count)])]
    psum x1 -> x0, blocking collectives: 19.7 us -> none  [body(): lax.psum((peak_terms.reshape(pair_count), present.reshape(pair_count)), '...]
    pallas_call x0 -> x1, Pallas kernels: none -> 18.9 us  [pair_call(): pl.pallas_call(functools.partial(pair_kernel, group, chunk, len(traces)),...]
    another operation x11 -> x2, other arithmetic: 12.1 us -> 1.31 us  [the longest x1 0.7 us: body(): sums = jnp.stack([peaks.reshape(-1), counts])]
    ppermute x2 -> x12, starting transfers between devices: 5.74 us -> 15.7 us  [the longest x7 11 us: exchange(): lax.ppermute(piece, 'sta', [(i, i ^ j) for i in range(sta_count)])]
    dynamic_update_slice x24 -> x0, local copies, waits for them, and re-layouts: 9.29 us -> none  [body(): lax.map(one_group, (event_groups, valid_groups))]
  transfers between devices with their start and end apart: 3 -> 12, of which waited for: 2 -> 6; matrix products, arithmetic and copies ran while one was open for 7% -> 14% of each run, Pallas kernels for 0% -> 0%
where the time goes in v1:
time: 70.8 us; the launch traced here: 70.3 us
  waiting for transfers between devices  20.3 us (29%)
  Pallas kernels  18.9 us (27%)
  starting transfers between devices  15.7 us (22%)
  local copies, waits for them, and re-layouts  9.81 us (14%)
  other arithmetic  4.78 us (7%)
  between operations  0.9 us (1%)
    pallas_call x1, Pallas kernels, pair_call(): pl.pallas_call(functools.partial(pair_kernel, group, chunk, len(traces)),...  18.9 us
    ppermute x3, waiting for transfers between devices, body(): lax.ppermute(sums, 'sta', [(i, i ^ step) for i in range(sta_count)])  11.1 us
    ppermute x7, starting transfers between devices, exchange(): lax.ppermute(piece, 'sta', [(i, i ^ j) for i in range(sta_count)])  11 us
    ppermute x1, waiting for transfers between devices, exchange(): far_halo = lax.ppermute(far, ('sta', 'evt'), away)  5.05 us
    ppermute x7, waiting for transfers between devices, exchange(): lax.ppermute(piece, 'sta', [(i, i ^ j) for i in range(sta_count)])  4.06 us
    gather x1, local copies, waits for them, and re-layouts, body(): jnp.take(present, pair_events[:, 0], axis=0)  2.81 us
    gather x1, local copies, waits for them, and re-layouts, body(): jnp.take(present, pair_events[:, 1], axis=0)  2.81 us
    ppermute x1, starting transfers between devices, exchange(): near_halo = lax.ppermute(near, ('sta', 'evt'), toward)  1.92 us
  transfers between devices with their start and end apart: 12, of which 6 were waited for; matrix products, arithmetic and copies ran while one was open for 14% of the time, Pallas kernels for 0%

profile of v1, /device:TPU:4, one launch (start us, length us, event | category | flops | bytes accessed | tf_op | source)
XLA Modules:
  0.0 70.3 jit_solution(15871875470441461196)
XLA Ops:
  0.7 1.1 %dynamic-slice_bitcast_fusion.3 = (bf16[4,8,1024]{2,1,0:T(8,128)(2,1)S(1)}, bf16[4,8,1024]{2,1,0:T(8,128)(2,1)S(1)}, bf16[4,8,1024]{2,1,0:T(8,128)(2,1)S(1)}, bf...) fusion(bf16[4,8,8,1024]{3,2,1,0:T(8,128)(2,1)} %bitcast.35, ...), kind=kLoop, calls=%fused_computation.10 | loop fusion | bytes 1048608 | tf_op jit(solution)/shard_map/jit(dynamic_index_in_dim)/squeeze | solution.py:145
  1.8 2.7 %collective-permute-start.3 = (bf16[4,8,1024]{2,1,0:T(8,128)(2,1)S(1)}, bf16[4,8,1024]{2,1,0:T(8,128)(2,1)S(1)}, u32[]{:S(2)}, u32[]{:S(2)}) collective-permute-start(bf16[4,8,1024]{2,1,0:T(8,128)(2,1)S(1)} %get-tuple-element.7), channel_id=1, source_target_pairs={{0,16},{4,20},{8,24},{12,28},{16,0},{20,4},{24,8},{28,12},{1,17},{... | collective-permute-start | bytes 196616 | tf_op jit(solution)/shard_map/ppermute | solution.py:146
  4.5 2.3 %collective-permute-start.6 = (bf16[4,8,1024]{2,1,0:T(8,128)(2,1)S(1)}, bf16[4,8,1024]{2,1,0:T(8,128)(2,1)S(1)}, u32[]{:S(2)}, u32[]{:S(2)}) collective-permute-start(bf16[4,8,1024]{2,1,0:T(8,128)(2,1)S(1)} %get-tuple-element.8), channel_id=1, source_target_pairs={{0,28},{4,24},{8,20},{12,16},{16,12},{20,8},{24,4},{28,0},{1,29},{... | collective-permute-start | bytes 196616 | tf_op jit(solution)/shard_map/ppermute | solution.py:146
  6.7 0.2 collective-permute-start.2
  7.0 1.8 %collective-permute-start.1 = (bf16[4,8,1024]{2,1,0:T(8,128)(2,1)S(1)}, bf16[4,8,1024]{2,1,0:T(8,128)(2,1)S(1)}, u32[]{:S(2)}, u32[]{:S(2)}) collective-permute-start(bf16[4,8,1024]{2,1,0:T(8,128)(2,1)S(1)} %get-tuple-element.12), channel_id=1, source_target_pairs={{0,8},{4,12},{8,0},{12,4},{16,24},{20,28},{24,16},{28,20},{1,9},{5... | collective-permute-start | bytes 196616 | tf_op jit(solution)/shard_map/ppermute | solution.py:146
  8.7 1.5 %collective-permute-start = (bf16[4,8,1024]{2,1,0:T(8,128)(2,1)S(1)}, bf16[4,8,1024]{2,1,0:T(8,128)(2,1)S(1)}, u32[]{:S(2)}, u32[]{:S(2)}) collective-permute-start(bf16[4,8,1024]{2,1,0:T(8,128)(2,1)S(1)} %get-tuple-element.13), channel_id=1, source_target_pairs={{0,4},{4,0},{8,12},{12,8},{16,20},{20,16},{24,28},{28,24},{1,5},{5... | collective-permute-start | bytes 196616 | tf_op jit(solution)/shard_map/ppermute | solution.py:146
  10.2 0.7 %fusion.1 = s32[1024,2]{0,1:T(2,128)S(1)} fusion(s32[1024,2]{0,1:T(2,128)} %param.10, s32[]{:T(128)S(6)} %mul.13, s32[]{:T(128)S(6)} %mul.12), kind=kLoop, calls=%fused_computation.23 | loop fusion | flops 36864 | bytes 16392 | tf_op jit(solution)/shard_map/add | solution.py:182
  11.0 0.8 %fusion.11 = (s32[1024,1]{0,1:T(1,128)S(1)}, s32[1024,1]{0,1:T(1,128)S(1)}) fusion(s32[1024,2]{0,1:T(2,128)} %param.10), kind=kLoop, calls=%fused_computation.51 | loop fusion | bytes 16384 | tf_op jit(solution)/shard_map/slice | solution.py:197
  11.8 0.8 %copy.9 = s32[128,8]{1,0:T(8,128)S(1)} copy(s32[128,8]{0,1:T(8,128)} %param.12) | data formatting | bytes 8192 | tf_op args[3]
  12.6 0.0 copy-start.2
  12.6 2.8 %gather_fusion.2 = f32[1024,8]{1,0:T(8,128)S(1)} fusion(f32[128,8]{1,0:T(8,128)S(1)} %convert_element_type.6, s32[1024]{0:T(1024)S(1)} %fusion.6), kind=kCustom, calls=%fused_computation.1.clone | custom fusion | bytes 69632 | tf_op jit(solution)/shard_map/jit(_take)/gather | solution.py:197
  15.4 2.8 %gather_fusion.1 = f32[1024,8]{1,0:T(8,128)S(1)} fusion(f32[128,8]{1,0:T(8,128)S(1)} %convert_element_type.6, s32[1024]{0:T(1024)S(1)} %fusion.5), kind=kCustom, calls=%fused_computation.clone | custom fusion | bytes 69632 | tf_op jit(solution)/shard_map/jit(_take)/gather | solution.py:197
  18.3 0.0 copy-done.2
  18.3 0.5 fusion
  18.8 0.6 pad_add_fusion.slots_ref
  19.4 0.0 collective-permute-done.2
  19.4 2.5 %collective-permute-start.5 = (bf16[4,8,1024]{2,1,0:T(8,128)(2,1)S(1)}, bf16[4,8,1024]{2,1,0:T(8,128)(2,1)S(1)}, u32[]{:S(2)}, u32[]{:S(2)}) collective-permute-start(bf16[4,8,1024]{2,1,0:T(8,128)(2,1)S(1)} %get-tuple-element.9), channel_id=1, source_target_pairs={{0,24},{4,28},{8,16},{12,20},{16,8},{20,12},{24,0},{28,4},{1,25},{... | collective-permute-start | bytes 196616 | tf_op jit(solution)/shard_map/ppermute | solution.py:146
  22.0 0.0 collective-permute-done.1
  22.0 0.0 collective-permute-start.4
  22.0 0.0 collective-permute-done
  22.0 0.0 copy-start
  22.1 1.9 %collective-permute-start.7 = (bf16[128,1024]{1,0:T(8,128)(2,1)S(1)}, bf16[128,1024]{1,0:T(8,128)(2,1)S(1)}, u32[]{:S(2)}, u32[]{:S(2)}) collective-permute-start(bf16[128,1024]{1,0:T(8,128)(2,1)S(1)} %maximum_bitcast_fusion.refs_0_), channel_id=1, source_target_pairs={{16,17},{20,21},{24,25},{28,29},{1,0},{5,4},{9,8},{13,12},{17,18},... | collective-permute-start | bytes 786440 | tf_op jit(solution)/shard_map/ppermute | solution.py:150
  24.0 0.0 collective-permute-done.3
  24.0 0.0 collective-permute-done.6
  24.0 1.7 %collective-permute-done.5 = bf16[4,8,1024]{2,1,0:T(8,128)(2,1)S(1)} collective-permute-done((bf16[4,8,1024]{2,1,0:T(8,128)(2,1)S(1)}, bf16[4,8,1024]{2,1,0:T(8,128)(2,1)S(1)}, u32[]{:S(2)}, u32[]{:S(2)}) %collective-permute-start.5) | collective-permute-done | bytes 65568 | tf_op jit(solution)/shard_map/ppermute | solution.py:146
  25.7 2.4 %collective-permute-done.4 = bf16[4,8,1024]{2,1,0:T(8,128)(2,1)S(1)} collective-permute-done((bf16[4,8,1024]{2,1,0:T(8,128)(2,1)S(1)}, bf16[4,8,1024]{2,1,0:T(8,128)(2,1)S(1)}, u32[]{:S(2)}, u32[]{:S(2)}) %collective-permute-start.4) | collective-permute-done | bytes 65568 | tf_op jit(solution)/shard_map/ppermute | solution.py:146
  28.1 0.0 copy-start.1
  28.1 1.9 %collective-permute-start.8 = (bf16[128,1024]{1,0:T(8,128)(2,1)S(1)}, bf16[128,1024]{1,0:T(8,128)(2,1)S(1)}, u32[]{:S(2)}, u32[]{:S(2)}) collective-permute-start(bf16[128,1024]{1,0:T(8,128)(2,1)S(1)} %maximum_bitcast_fusion.1.refs_1_), channel_id=1, source_target_pairs={{0,1},{4,5},{8,9},{12,13},{1,2},{5,6},{9,10},{13,14},{17,16},{21,2... | collective-permute-start | bytes 786440 | tf_op jit(solution)/shard_map/ppermute | solution.py:151
  30.0 0.6 gather_fusion
  30.6 0.1 broadcast_select_fusion
  30.7 0.0 collective-permute-done.7.refs_2_
  30.7 0.0 copy-start.3
  30.7 5.0 %collective-permute-done.8.refs_3_ = bf16[128,1024]{1,0:T(8,128)(2,1)S(1)} collective-permute-done((bf16[128,1024]{1,0:T(8,128)(2,1)S(1)}, bf16[128,1024]{1,0:T(8,128)(2,1)S(1)}, u32[]{:S(2)}, u32[]{:S(2)}) %collective-permute-start.8) | collective-permute-done | bytes 262176 | tf_op jit(solution)/shard_map/ppermute | solution.py:151
  35.8 0.0 copy-start.4
  35.8 0.9 %broadcast_in_dim.36.refs_4_ = f32[64,8,128]{2,1,0:T(8,128)} broadcast(f32[64,8]{1,0:T(8,128)S(1)} %broadcast_select_fusion), dimensions={0,1} | broadcast | bytes 264192 | tf_op jit(solution)/shard_map/broadcast_in_dim | solution.py:194
  36.6 0.0 copy-done
  36.7 0.0 copy-done.1
  36.7 0.0 copy-done.3
  36.7 0.0 copy-done.4
  36.7 18.9 %shard_map.86 = (bf16[8192,256]{1,0:T(8,128)(2,1)}, f32[8,1,128]{2,1,0:T(1,128)}) custom-call(s32[3,1024]{1,0:T(4,128)} %pad_add_fusion.slots_ref, bf16[128,1024]{1,0:T(8,128)(2,1)} %copy-done, bf16[128,1024]{1,0:T(8,128)(2,1)} %copy-done.1, bf16[128,1024]{1,0:T(8,128)(2,1)} %copy-done.3, bf16[128,1024]{1,0:T(8,128)(2,1)} %copy-done.4, ...), custom_call_target="tpu_custom_call" | custom-call | flops 4499999744 | bytes 8000000 | tf_op jit(solution)/shard_map/pallas_call | solution.py:107
  55.5 0.7 pad_maximum_fusion
  56.2 0.1 collective-permute-start.9
  56.3 4.5 %collective-permute-done.9 = f32[2,1024]{1,0:T(2,128)S(1)} collective-permute-done((f32[2,1024]{1,0:T(2,128)S(1)}, f32[2,1024]{1,0:T(2,128)S(1)}, u32[]{:S(2)}, u32[]{:S(2)}) %collective-permute-start.9) | collective-permute-done | bytes 8224 | tf_op jit(solution)/shard_map/ppermute | solution.py:205
  60.9 0.7 fusion.10
  61.6 0.1 collective-permute-start.10
  61.6 3.6 %collective-permute-done.10 = f32[2,1024]{1,0:T(2,128)S(1)} collective-permute-done((f32[2,1024]{1,0:T(2,128)S(1)}, f32[2,1024]{1,0:T(2,128)S(1)}, u32[]{:S(2)}, u32[]{:S(2)}) %collective-permute-start.10) | collective-permute-done | bytes 8224 | tf_op jit(solution)/shard_map/ppermute | solution.py:205
  65.3 0.7 fusion.12
  66.0 0.7 %collective-permute-start.11 = (f32[2,1024]{1,0:T(2,128)S(1)}, f32[2,1024]{1,0:T(2,128)S(1)}, u32[]{:S(2)}, u32[]{:S(2)}) collective-permute-start(f32[2,1024]{1,0:T(2,128)S(1)} %fusion.12), channel_id=1, source_target_pairs={{0,4},{4,0},{8,12},{12,8},{16,20},{20,16},{24,28},{28,24},{1,5},{5... | collective-permute-start | bytes 24584 | tf_op jit(solution)/shard_map/ppermute | solution.py:205
  66.7 3.0 %collective-permute-done.11 = f32[2,1024]{1,0:T(2,128)S(1)} collective-permute-done((f32[2,1024]{1,0:T(2,128)S(1)}, f32[2,1024]{1,0:T(2,128)S(1)}, u32[]{:S(2)}, u32[]{:S(2)}) %collective-permute-start.11) | collective-permute-done | bytes 8224 | tf_op jit(solution)/shard_map/ppermute | solution.py:205
  69.7 0.6 fusion.4
  (13 shorter events, 0.2 us)
Async XLA Ops:
  1.8 22.2 %collective-permute-start.3 = (bf16[4,8,1024]{2,1,0:T(8,128)(2,1)S(1)}, bf16[4,8,1024]{2,1,0:T(8,128)(2,1)S(1)}, u32[]{:S(2)}, u32[]{:S(2)}) collective-permute-start(bf16[4,8,1024]{2,1,0:T(8,128)(2,1)S(1)} %get-tuple-element.7), channel_id=1, source_target_pairs={{0,16},{4,20},{8,24},{12,28},{16,0},{20,4},{24,8},{28,12},{1,17},{... | collective-permute-start | bytes 196616 | tf_op jit(solution)/shard_map/ppermute | solution.py:146
  4.5 19.5 %collective-permute-start.6 = (bf16[4,8,1024]{2,1,0:T(8,128)(2,1)S(1)}, bf16[4,8,1024]{2,1,0:T(8,128)(2,1)S(1)}, u32[]{:S(2)}, u32[]{:S(2)}) collective-permute-start(bf16[4,8,1024]{2,1,0:T(8,128)(2,1)S(1)} %get-tuple-element.8), channel_id=1, source_target_pairs={{0,28},{4,24},{8,20},{12,16},{16,12},{20,8},{24,4},{28,0},{1,29},{... | collective-permute-start | bytes 196616 | tf_op jit(solution)/shard_map/ppermute | solution.py:146
  6.7 12.7 %collective-permute-start.2 = (bf16[4,8,1024]{2,1,0:T(8,128)(2,1)S(1)}, bf16[4,8,1024]{2,1,0:T(8,128)(2,1)S(1)}, u32[]{:S(2)}, u32[]{:S(2)}) collective-permute-start(bf16[4,8,1024]{2,1,0:T(8,128)(2,1)S(1)} %get-tuple-element.11), channel_id=1, source_target_pairs={{0,12},{4,8},{8,4},{12,0},{16,28},{20,24},{24,20},{28,16},{1,13},{... | collective-permute-start | bytes 196616 | tf_op jit(solution)/shard_map/ppermute | solution.py:146
  7.0 15.0 %collective-permute-start.1 = (bf16[4,8,1024]{2,1,0:T(8,128)(2,1)S(1)}, bf16[4,8,1024]{2,1,0:T(8,128)(2,1)S(1)}, u32[]{:S(2)}, u32[]{:S(2)}) collective-permute-start(bf16[4,8,1024]{2,1,0:T(8,128)(2,1)S(1)} %get-tuple-element.12), channel_id=1, source_target_pairs={{0,8},{4,12},{8,0},{12,4},{16,24},{20,28},{24,16},{28,20},{1,9},{5... | collective-permute-start | bytes 196616 | tf_op jit(solution)/shard_map/ppermute | solution.py:146
  8.7 13.3 %collective-permute-start = (bf16[4,8,1024]{2,1,0:T(8,128)(2,1)S(1)}, bf16[4,8,1024]{2,1,0:T(8,128)(2,1)S(1)}, u32[]{:S(2)}, u32[]{:S(2)}) collective-permute-start(bf16[4,8,1024]{2,1,0:T(8,128)(2,1)S(1)} %get-tuple-element.13), channel_id=1, source_target_pairs={{0,4},{4,0},{8,12},{12,8},{16,20},{20,16},{24,28},{28,24},{1,5},{5... | collective-permute-start | bytes 196616 | tf_op jit(solution)/shard_map/ppermute | solution.py:146
  12.6 5.7 %copy-start.2 = (s32[1024]{0:T(1024)S(1)}, s32[1024]{0:T(1024)}, u32[]{:S(2)}) copy-start(s32[1024]{0:T(1024)} %param.11) | copy-start | bytes 12292
  19.4 6.2 %collective-permute-start.5 = (bf16[4,8,1024]{2,1,0:T(8,128)(2,1)S(1)}, bf16[4,8,1024]{2,1,0:T(8,128)(2,1)S(1)}, u32[]{:S(2)}, u32[]{:S(2)}) collective-permute-start(bf16[4,8,1024]{2,1,0:T(8,128)(2,1)S(1)} %get-tuple-element.9), channel_id=1, source_target_pairs={{0,24},{4,28},{8,16},{12,20},{16,8},{20,12},{24,0},{28,4},{1,25},{... | collective-permute-start | bytes 196616 | tf_op jit(solution)/shard_map/ppermute | solution.py:146
  22.0 6.1 %collective-permute-start.4 = (bf16[4,8,1024]{2,1,0:T(8,128)(2,1)S(1)}, bf16[4,8,1024]{2,1,0:T(8,128)(2,1)S(1)}, u32[]{:S(2)}, u32[]{:S(2)}) collective-permute-start(bf16[4,8,1024]{2,1,0:T(8,128)(2,1)S(1)} %get-tuple-element.10), channel_id=1, source_target_pairs={{0,20},{4,16},{8,28},{12,24},{16,4},{20,0},{24,12},{28,8},{1,21},{... | collective-permute-start | bytes 196616 | tf_op jit(solution)/shard_map/ppermute | solution.py:146
  22.0 14.6 %copy-start = (bf16[128,1024]{1,0:T(8,128)(2,1)}, bf16[128,1024]{1,0:T(8,128)(2,1)S(1)}, u32[]{:S(2)}) copy-start(bf16[128,1024]{1,0:T(8,128)(2,1)S(1)} %maximum_bitcast_fusion.refs_0_) | copy-start | bytes 786436
  22.1 8.7 %collective-permute-start.7 = (bf16[128,1024]{1,0:T(8,128)(2,1)S(1)}, bf16[128,1024]{1,0:T(8,128)(2,1)S(1)}, u32[]{:S(2)}, u32[]{:S(2)}) collective-permute-start(bf16[128,1024]{1,0:T(8,128)(2,1)S(1)} %maximum_bitcast_fusion.refs_0_), channel_id=1, source_target_pairs={{16,17},{20,21},{24,25},{28,29},{1,0},{5,4},{9,8},{13,12},{17,18},... | collective-permute-start | bytes 786440 | tf_op jit(solution)/shard_map/ppermute | solution.py:150
  28.1 8.6 %copy-start.1 = (bf16[128,1024]{1,0:T(8,128)(2,1)}, bf16[128,1024]{1,0:T(8,128)(2,1)S(1)}, u32[]{:S(2)}) copy-start(bf16[128,1024]{1,0:T(8,128)(2,1)S(1)} %maximum_bitcast_fusion.1.refs_1_) | copy-start | bytes 786436
  28.1 7.7 %collective-permute-start.8 = (bf16[128,1024]{1,0:T(8,128)(2,1)S(1)}, bf16[128,1024]{1,0:T(8,128)(2,1)S(1)}, u32[]{:S(2)}, u32[]{:S(2)}) collective-permute-start(bf16[128,1024]{1,0:T(8,128)(2,1)S(1)} %maximum_bitcast_fusion.1.refs_1_), channel_id=1, source_target_pairs={{0,1},{4,5},{8,9},{12,13},{1,2},{5,6},{9,10},{13,14},{17,16},{21,2... | collective-permute-start | bytes 786440 | tf_op jit(solution)/shard_map/ppermute | solution.py:151
  30.7 5.9 %copy-start.3 = (bf16[128,1024]{1,0:T(8,128)(2,1)}, bf16[128,1024]{1,0:T(8,128)(2,1)S(1)}, u32[]{:S(2)}) copy-start(bf16[128,1024]{1,0:T(8,128)(2,1)S(1)} %collective-permute-done.7.refs_2_) | copy-start | bytes 786436
  35.8 0.9 %copy-start.4 = (bf16[128,1024]{1,0:T(8,128)(2,1)}, bf16[128,1024]{1,0:T(8,128)(2,1)S(1)}, u32[]{:S(2)}) copy-start(bf16[128,1024]{1,0:T(8,128)(2,1)S(1)} %collective-permute-done.8.refs_3_) | copy-start | bytes 786436
  56.2 4.6 %collective-permute-start.9 = (f32[2,1024]{1,0:T(2,128)S(1)}, f32[2,1024]{1,0:T(2,128)S(1)}, u32[]{:S(2)}, u32[]{:S(2)}) collective-permute-start(f32[2,1024]{1,0:T(2,128)S(1)} %pad_maximum_fusion), channel_id=1, source_target_pairs={{0,16},{4,20},{8,24},{12,28},{16,0},{20,4},{24,8},{28,12},{1,17},{... | collective-permute-start | bytes 24584 | tf_op jit(solution)/shard_map/ppermute | solution.py:205
  61.6 3.7 %collective-permute-start.10 = (f32[2,1024]{1,0:T(2,128)S(1)}, f32[2,1024]{1,0:T(2,128)S(1)}, u32[]{:S(2)}, u32[]{:S(2)}) collective-permute-start(f32[2,1024]{1,0:T(2,128)S(1)} %fusion.10), channel_id=1, source_target_pairs={{0,8},{4,12},{8,0},{12,4},{16,24},{20,28},{24,16},{28,20},{1,9},{5... | collective-permute-start | bytes 24584 | tf_op jit(solution)/shard_map/ppermute | solution.py:205
  66.0 3.7 %collective-permute-start.11 = (f32[2,1024]{1,0:T(2,128)S(1)}, f32[2,1024]{1,0:T(2,128)S(1)}, u32[]{:S(2)}, u32[]{:S(2)}) collective-permute-start(f32[2,1024]{1,0:T(2,128)S(1)} %fusion.12), channel_id=1, source_target_pairs={{0,4},{4,0},{8,12},{12,8},{16,20},{20,16},{24,28},{28,24},{1,5},{5... | collective-permute-start | bytes 24584 | tf_op jit(solution)/shard_map/ppermute | solution.py:205

commit v2 on v1

--- a/solution.py
+++ b/solution.py
@@ -152,9 +152,8 @@
     return (near, far, near_halo, far_halo), me
 
 
-def exchange_whole(waveforms, sta_count):
-    events, stations, window = waveforms.shape
-    share = stations // sta_count
+def exchange_whole(waveforms):
+    window = waveforms.shape[2]
     arrived = lax.all_to_all(waveforms, "sta", split_axis=1, concat_axis=0, tiled=True)
     arrived = arrived.reshape(-1, window)
     half = arrived.shape[0] // 2
@@ -163,7 +162,302 @@
     up = [(i, i + 1) for i in range(count - 1)]
     next_low = lax.ppermute(arrived[:half], "evt", down)
     last_high = lax.ppermute(arrived[half:], "evt", up)
-    return (arrived, next_low, last_high), jnp.int32(0)
+    return arrived, next_low, last_high
+
+
+def triangle(count):
+    return count * (count + 1) // 2
+
+
+def own_list(block):
+    band = block // 2
+    return [(x, y) for x in range(block) for y in range(x + 1, min(x + band, block - 1) + 1)]
+
+
+def lane_rows(count):
+    return -(-count // LANES) * LANES
+
+
+def own_rows(block):
+    return lane_rows(2 * len(own_list(block)) + 1)
+
+
+def halo_rows(block):
+    return lane_rows(triangle(block // 2))
+
+
+def cross_spectra(first, second):
+    half = first.shape[1] // 2
+    ra, ia = first[:, :half], first[:, half:]
+    rb, ib = second[:, :half], second[:, half:]
+    return jnp.concatenate([ra * rb + ia * ib, ra * ib - ia * rb], axis=1)
+
+
+def scaled_spectra(traces_ref, me, each, place, presence_ref, present, forward_ref, weights_ref, spec_ref):
+    stations, window = spec_ref.shape[1:]
+    events = traces_ref.shape[0] // stations
+    pieces = events // each
+    result = jnp.dot(traces_ref[...], forward_ref[...], preferred_element_type=jnp.float32)
+    rounded = result.astype(jnp.bfloat16).astype(jnp.float32)
+    energy = jnp.sum(jnp.square(rounded) * weights_ref[...], axis=1, keepdims=True) + 1e-06
+    gain = jnp.broadcast_to(lax.rsqrt(energy), (events * stations, LANES)).reshape(events, stations, LANES)
+    rounded = rounded.reshape(events, stations, window)
+    for j in range(pieces):
+        shift = ((me ^ j) & (pieces - 1)) * each
+        piece = slice(j * each, (j + 1) * each)
+        scale = gain[piece] * presence_ref[pl.ds(present + shift, each)]
+        scale = jnp.concatenate([scale] * (window // LANES), axis=2)
+        spec_ref[pl.ds(place + shift, each)] = rounded[piece] * scale
+
+
+def build(lhs_ref, low, pairs, first_of, second_of):
+    for i in range(0, len(pairs), 2):
+        both = [cross_spectra(first_of(x), second_of(y)) for x, y in pairs[i:i + 2]]
+        rows = 2 * both[0].shape[0]
+        lhs_ref[pl.ds((low + i) * rows // 2, rows), :] = jnp.concatenate(both, axis=0).astype(jnp.bfloat16)
+
+
+def keep(table_ref, peaks, values, row):
+    stations = peaks[0].shape[0]
+    lane = lax.broadcasted_iota(jnp.int32, peaks[0].shape, 1)
+    for i in range(values.shape[0] // stations):
+        top = jnp.max(values[i * stations:(i + 1) * stations], axis=1, keepdims=True)
+        at, within = divmod(row + i, LANES)
+        peaks[at] = jnp.where(lane == within, top, peaks[at])
+    table_ref[pl.ds(row * stations, values.shape[0]), :] = values.astype(jnp.bfloat16)
+
+
+def no_peaks(peak_ref):
+    stations, count = peak_ref.shape
+    return [jnp.zeros((stations, LANES), jnp.float32) for _ in range(count // LANES)]
+
+
+def own_kernel(
+    each, me_ref, near_ref, far_ref, presence_ref, forward_ref, inverse_ref, weights_ref,
+    spec_ref, table_ref, peak_ref, lhs_ref,
+):
+    block, stations, window = spec_ref.shape
+    band = block // 2
+    half = window // 2
+    me = me_ref[0]
+    mine = jnp.where(me * each < band, 0, band)
+    for ref, place in ((near_ref, mine), (far_ref, band - mine)):
+        scaled_spectra(
+            ref, me, each, place, presence_ref, band + place, forward_ref, weights_ref, spec_ref
+        )
+    pairs = own_list(block)
+    peaks = no_peaks(peak_ref)
+    chunk = 64
+    for low in range(0, len(pairs), chunk):
+        some = pairs[low:low + chunk]
+        held = {x: spec_ref[x] for x, _ in some}
+        build(lhs_ref, low, some, lambda x: held[x], lambda y: spec_ref[y])
+        rows = pl.ds(low * stations, len(some) * stations)
+        even = jnp.dot(lhs_ref[rows, :half], inverse_ref[:half], preferred_element_type=jnp.float32)
+        odd = jnp.dot(lhs_ref[rows, half:], inverse_ref[half:], preferred_element_type=jnp.float32)
+        keep(table_ref, peaks, even + odd, low)
+        keep(table_ref, peaks, even - odd, len(pairs) + low)
+    peak_ref[...] = jnp.concatenate(peaks, axis=1)
+
+
+def halo_kernel(
+    each, is_far, me_ref, traces_ref, own_ref, presence_ref, forward_ref, inverse_ref, weights_ref,
+    table_ref, peak_ref, spec_ref, lhs_ref,
+):
+    band, stations, window = spec_ref.shape
+    me = me_ref[0]
+    high = (me * each < band) != is_far
+    scaled_spectra(
+        traces_ref, me, each, 0, presence_ref, jnp.where(high, 3 * band, 0), forward_ref, weights_ref, spec_ref
+    )
+
+    def own(u):
+        return own_ref[jnp.where(high, band + u, band - 1 - u)]
+
+    def other(h):
+        return spec_ref[jnp.where(high, h, band - 1 - h)]
+
+    pairs = [(u, h) for u in range(band) for h in range(u + 1)]
+    peaks = no_peaks(peak_ref)
+    chunk = 68
+    for low in range(0, len(pairs), chunk):
+        some = pairs[low:low + chunk]
+        held = {u: own(u) for u, _ in some}
+        build(lhs_ref, low, some, lambda u: held[u], other)
+        rows = pl.ds(low * stations, len(some) * stations)
+        lagged = jnp.dot(lhs_ref[rows, :], inverse_ref[...], preferred_element_type=jnp.float32)
+        keep(table_ref, peaks, lagged, low)
+    peak_ref[...] = jnp.concatenate(peaks, axis=1)
+
+
+def sum_kernel(own_ref, near_ref, far_ref, row_ref, out_ref):
+    rows = row_ref[...]
+    lanes = rows & (LANES - 1)
+    total = jnp.zeros(rows.shape, jnp.float32)
+    at = 0
+    for ref in (own_ref, near_ref, far_ref):
+        sums = jnp.sum(ref[...], axis=0, keepdims=True)
+        for low in range(0, ref.shape[1], LANES):
+            line = jnp.broadcast_to(sums[:, low:low + LANES], rows.shape)
+            picked = jnp.take_along_axis(line, lanes, axis=1)
+            total = jnp.where(rows // LANES == at, picked, total)
+            at += 1
+    out_ref[...] = total
+
+
+def pick_kernel(group, starts, row_ref, *refs):
+    tables, (out_ref, table_ref) = refs[:len(starts)], refs[len(starts):]
+    stations, lags = table_ref.shape[1:]
+
+    @pl.when(pl.program_id(0) == 0)
+    def _():
+        for ref, start in zip(tables, starts, strict=True):
+            count = ref.shape[0] // stations
+            wide = ref[...].astype(jnp.float32)
+            table_ref[pl.ds(start, count)] = wide.reshape(count, stations, lags)
+        zero = tables[0].shape[0] // stations
+        table_ref[zero] = jnp.zeros((stations, lags), jnp.float32)
+
+    base = pl.program_id(0) * group
+    for j in range(0, group, 2):
+        both = [table_ref[row_ref[base + i]] for i in (j, j + 1)]
+        out_ref[pl.ds(j * stations, 2 * stations), :] = jnp.concatenate(both, axis=0).astype(jnp.bfloat16)
+
+
+VMEM = pl.BlockSpec(memory_space=pltpu.VMEM)
+SMEM = pl.BlockSpec(memory_space=pltpu.SMEM)
+PARAMS = pltpu.CompilerParams(vmem_limit_bytes=40 * 1024 * 1024)
+
+
+def cost(rows, lags, window, traces, moved):
+    return pl.CostEstimate(
+        flops=2 * window * (rows * lags + traces * window), bytes_accessed=moved, transcendentals=0
+    )
+
+
+def own_call(me, near, far, presence, tables, each):
+    forward, inverse, weights = tables
+    window, lags = inverse.shape
+    block, stations = presence.shape[0] // 2, presence.shape[1]
+    count = len(own_list(block))
+    return pl.pallas_call(
+        functools.partial(own_kernel, each),
+        out_shape=(
+            jax.ShapeDtypeStruct((block, stations, window), jnp.float32),
+            jax.ShapeDtypeStruct((2 * count * stations, lags), jnp.bfloat16),
+            jax.ShapeDtypeStruct((stations, own_rows(block)), jnp.float32),
+        ),
+        in_specs=[SMEM] + [VMEM] * 6,
+        out_specs=(VMEM,) * 3,
+        scratch_shapes=[pltpu.VMEM((count * stations, window), jnp.bfloat16)],
+        compiler_params=PARAMS,
+        cost_estimate=cost(count * stations, lags, window, near.shape[0] * 2, 8_000_000),
+    )(me, near, far, presence, forward, inverse, weights)
+
+
+def halo_call(me, traces, own, presence, tables, each, is_far):
+    forward, inverse, weights = tables
+    window, lags = inverse.shape
+    block, stations = own.shape[:2]
+    count = triangle(block // 2)
+    return pl.pallas_call(
+        functools.partial(halo_kernel, each, is_far),
+        out_shape=(
+            jax.ShapeDtypeStruct((count * stations, lags), jnp.bfloat16),
+            jax.ShapeDtypeStruct((stations, halo_rows(block)), jnp.float32),
+        ),
+        in_specs=[SMEM] + [VMEM] * 6,
+        out_specs=(VMEM,) * 2,
+        scratch_shapes=[
+            pltpu.VMEM((block // 2, stations, window), jnp.float32),
+            pltpu.VMEM((count * stations, window), jnp.bfloat16),
+        ],
+        compiler_params=PARAMS,
+        cost_estimate=cost(count * stations, lags, window, traces.shape[0], 4_000_000),
+    )(me, traces, own, presence, forward, inverse, weights)
+
+
+def sum_call(peaks, rows):
+    return pl.pallas_call(
+        sum_kernel,
+        out_shape=jax.ShapeDtypeStruct(rows.shape, jnp.float32),
+        in_specs=[VMEM] * 4,
+        out_specs=VMEM,
+        cost_estimate=pl.CostEstimate(flops=100_000, bytes_accessed=100_000, transcendentals=0),
+    )(*peaks, rows)
+
+
+def pick_call(rows, tables, starts, stations, held):
+    lags = tables[0].shape[1]
+    pairs = rows.shape[0]
+    group = LANES
+    return pl.pallas_call(
+        functools.partial(pick_kernel, group, starts),
+        grid=(pairs // group,),
+        out_shape=jax.ShapeDtypeStruct((pairs * stations, lags), jnp.bfloat16),
+        in_specs=[SMEM] + [VMEM] * len(tables),
+        out_specs=pl.BlockSpec((group * stations, lags), lambda i: (i, 0)),
+        scratch_shapes=[pltpu.VMEM((held, stations, lags), jnp.float32)],
+        compiler_params=PARAMS,
+        cost_estimate=pl.CostEstimate(flops=10_000_000, bytes_accessed=10_000_000, transcendentals=0),
+    )(rows, *tables)
+
+
+def table_row(first, second, me, each, block):
+    band = block // 2
+    low, apart = jnp.minimum(first, second), jnp.abs(first - second)
+    past = jnp.maximum(low - band, 0)
+    index = jnp.minimum(low, band) * band + past * (band - 1) - past * (past - 1) // 2 + apart - 1
+    inside = jnp.where(second > first, index, len(own_list(block)) + index)
+    high = second >= block
+    u = jnp.where(high, first - band, band - 1 - first)
+    h = jnp.where(high, second - block, -1 - second)
+    near = high == (me * each < band)
+    outside = jnp.where(near, own_rows(block), own_rows(block) + halo_rows(block)) + u * (u + 1) // 2 + h
+    return jnp.where(high | (second < 0), outside, inside)
+
+
+def banded(waveforms, pair_events, pair_valid, presence, start, block, tables):
+    sta_count = lax.axis_size("sta")
+    each = waveforms.shape[0]
+    share = waveforms.shape[1] // sta_count
+    (near, far, near_halo, far_halo), me = exchange(waveforms, sta_count)
+    band = block // 2
+    window_presence = lax.dynamic_slice_in_dim(
+        jnp.pad(presence, ((band, band), (0, 0))), start, 2 * block, axis=0
+    )
+    held = jnp.broadcast_to(window_presence.astype(jnp.float32)[:, :, None], (2 * block, share, LANES))
+    place = pair_events - start
+    row = table_row(place[:, 0], place[:, 1], me, each, block)
+    zero = 2 * len(own_list(block))
+    starts = (0, own_rows(block), own_rows(block) + halo_rows(block))
+    last = starts[2] + triangle(band)
+    row = jnp.clip(jnp.where(pair_valid > 0, row, zero), 0, last - 1).astype(jnp.int32)
+
+    at = me.reshape(1).astype(jnp.int32)
+    own, own_table, own_peaks = own_call(at, near, far, held, tables, each)
+    near_table, near_peaks = halo_call(at, near_halo, own, held, tables, each, False)
+    far_table, far_peaks = halo_call(at, far_halo, own, held, tables, each, True)
+    peaks = sum_call((own_peaks, near_peaks, far_peaks), row.reshape(-1, LANES))
+    correlation = pick_call(row, (own_table, near_table, far_table), starts, share, last)
+    return correlation, peaks.reshape(-1)
+
+
+def by_slot(waveforms, pair_events, pair_valid, presence, start, block, tables):
+    share = presence.shape[1]
+    traces = exchange_whole(waveforms)
+    place = pair_events - start
+    slot = jnp.where((place >= 0) & (place < block), 0, block) + place % block
+    gained = jnp.where(pair_valid > 0, slot[:, 0], 2 * block)
+    slots = jnp.stack([slot[:, 0], slot[:, 1], gained]).astype(jnp.int32)
+    held = jnp.arange(2 * block, dtype=jnp.int32)
+    held = jnp.where(held < block, held, jnp.where(held < block + block // 2, held, held - 2 * block))
+    held = jnp.clip(start + held, 0, presence.shape[0] - 1)
+    slot_presence = jnp.broadcast_to(
+        jnp.take(presence.astype(jnp.float32), held, axis=0)[:, :, None], (2 * block, share, LANES)
+    )
+    correlation, peaks = pair_call(slots, traces, slot_presence, tables)
+    return correlation, peaks.reshape(-1)
 
 
 def body(waveforms, pair_events, pair_valid, presence):
@@ -171,35 +465,22 @@
     local_events, stations, window = waveforms.shape
     share = stations // sta_count
     block = sta_count * local_events
+    start = lax.axis_index("evt") * block
     tables = spectral_tables(window, LAGS)
-    direct = sta_count <= 8 and sta_count & (sta_count - 1) == 0
-    traces, me = (exchange if direct else exchange_whole)(waveforms, sta_count)
-
-    start = lax.axis_index("evt") * block
-    offset = pair_events - start
-    inside = (offset >= 0) & (offset < block)
-    flip = me * local_events
-    slot = jnp.where(inside, 0, block) + ((offset % block) ^ flip)
-    first, second = slot[:, 0], slot[:, 1]
-    gained = jnp.where(pair_valid > 0, first, 2 * block)
-    slots = jnp.stack([first, second, gained]).astype(jnp.int32)
-
-    place = jnp.arange(2 * block, dtype=jnp.int32)
-    relative = (place % block) ^ flip
-    relative = jnp.where(
-        place < block, relative, jnp.where(relative < block // 2, relative + block, relative - block)
-    )
-    held = jnp.clip(start + relative, 0, presence.shape[0] - 1)
-    present = presence.astype(jnp.float32)
-    slot_presence = jnp.broadcast_to(
-        jnp.take(present, held, axis=0)[:, :, None], (2 * block, share, LANES)
-    )
-    both = jnp.take(present, pair_events[:, 0], axis=0) * jnp.take(present, pair_events[:, 1], axis=0)
-    counts = jnp.sum(both, axis=1) * pair_valid.astype(jnp.float32)
-
-    correlation, peaks = pair_call(slots, traces, slot_presence, tables)
-    sums = jnp.stack([peaks.reshape(-1), counts])
-    if direct:
+
+    few = presence.astype(jnp.bfloat16)
+    event = jnp.arange(presence.shape[0], dtype=jnp.int32)
+    first, second = (
+        jnp.dot((pair_events[:, i:i + 1] == event).astype(jnp.bfloat16), few, preferred_element_type=jnp.float32)
+        for i in (0, 1)
+    )
+    counts = jnp.sum(first * second, axis=1) * pair_valid.astype(jnp.float32)
+
+    dense = sta_count == 8 and block * block <= pair_events.shape[0]
+    plan = banded if dense else by_slot
+    correlation, peaks = plan(waveforms, pair_events, pair_valid, presence, start, block, tables)
+    sums = jnp.stack([peaks, counts])
+    if dense:
         step = sta_count // 2
         while step:
             sums = sums + lax.ppermute(sums, "sta", [(i, i ^ step) for i in range(sta_count)])

time: 70.8 us -> 60.1 us (0.85)
  the two profiles are of different devices: /device:TPU:4 before, /device:TPU:0 now
where the time goes in v2:
time: 60.1 us; the launch traced here: 59.3 us
  starting transfers between devices  20.7 us (34%)
  Pallas kernels  12.5 us (21%)
  local copies, waits for them, and re-layouts  10.3 us (17%)
  waiting for transfers between devices  6.61 us (11%)
  other arithmetic  6.3 us (10%)
  matrix products  2.03 us (3%)
  between operations  0.88 us (1%)
    ppermute x7, starting transfers between devices, exchange(): lax.ppermute(piece, 'sta', [(i, i ^ j) for i in range(sta_count)])  12.5 us
    unnamed x26, local copies, waits for them, and re-layouts  8.22 us
    ppermute x3, starting transfers between devices, body(): lax.ppermute(sums, 'sta', [(i, i ^ step) for i in range(sta_count)])  5.58 us
    pallas_call x1, Pallas kernels, pick_call(): pl.pallas_call(functools.partial(pick_kernel, group, starts), grid=(pairs...  5.07 us
    ppermute x3, waiting for transfers between devices, body(): lax.ppermute(sums, 'sta', [(i, i ^ step) for i in range(sta_count)])  4.52 us
    pallas_call x1, Pallas kernels, own_call(): pl.pallas_call(functools.partial(own_kernel, each), out_shape=(jax.ShapeD...  3.16 us
    pallas_call x2, Pallas kernels, halo_call(): pl.pallas_call(functools.partial(halo_kernel, each, is_far), out_shape=(j...  2.8 us
    ppermute x7, waiting for transfers between devices, exchange(): lax.ppermute(piece, 'sta', [(i, i ^ j) for i in range(sta_count)])  2.09 us
  transfers between devices with their start and end apart: 12, of which 4 were waited for; matrix products, arithmetic and copies ran while one was open for 11% of the time, Pallas kernels for 16%

profile of v2, /device:TPU:0, one launch (start us, length us, event | category | flops | bytes accessed | tf_op | source)
XLA Modules:
  0.0 59.3 jit_solution(4039515068337064890)
XLA Ops:
  0.7 1.1 %dynamic-slice_bitcast_fusion.3 = (bf16[4,8,1024]{2,1,0:T(8,128)(2,1)S(1)}, bf16[4,8,1024]{2,1,0:T(8,128)(2,1)S(1)}, bf16[4,8,1024]{2,1,0:T(8,128)(2,1)S(1)}, bf...) fusion(bf16[4,8,8,1024]{3,2,1,0:T(8,128)(2,1)} %bitcast.37, ...), kind=kLoop, calls=%fused_computation.12 | loop fusion | bytes 1048608 | tf_op jit(solution)/shard_map/jit(dynamic_index_in_dim)/squeeze | solution.py:145
  1.8 4.1 %collective-permute-start.3 = (bf16[4,8,1024]{2,1,0:T(8,128)(2,1)S(1)}, bf16[4,8,1024]{2,1,0:T(8,128)(2,1)S(1)}, u32[]{:S(2)}, u32[]{:S(2)}) collective-permute-start(bf16[4,8,1024]{2,1,0:T(8,128)(2,1)S(1)} %get-tuple-element.18), channel_id=1, source_target_pairs={{0,16},{4,20},{8,24},{12,28},{16,0},{20,4},{24,8},{28,12},{1,17},{... | collective-permute-start | bytes 196616 | tf_op jit(solution)/shard_map/ppermute | solution.py:146
  5.9 1.3 %collective-permute-start.4 = (bf16[4,8,1024]{2,1,0:T(8,128)(2,1)S(1)}, bf16[4,8,1024]{2,1,0:T(8,128)(2,1)S(1)}, u32[]{:S(2)}, u32[]{:S(2)}) collective-permute-start(bf16[4,8,1024]{2,1,0:T(8,128)(2,1)S(1)} %get-tuple-element.21), channel_id=1, source_target_pairs={{0,20},{4,16},{8,28},{12,24},{16,4},{20,0},{24,12},{28,8},{1,21},{... | collective-permute-start | bytes 196616 | tf_op jit(solution)/shard_map/ppermute | solution.py:146
  7.2 3.6 %collective-permute-start.5 = (bf16[4,8,1024]{2,1,0:T(8,128)(2,1)S(1)}, bf16[4,8,1024]{2,1,0:T(8,128)(2,1)S(1)}, u32[]{:S(2)}, u32[]{:S(2)}) collective-permute-start(bf16[4,8,1024]{2,1,0:T(8,128)(2,1)S(1)} %get-tuple-element.20), channel_id=1, source_target_pairs={{0,24},{4,28},{8,16},{12,20},{16,8},{20,12},{24,0},{28,4},{1,25},{... | collective-permute-start | bytes 196616 | tf_op jit(solution)/shard_map/ppermute | solution.py:146
  10.8 0.0 collective-permute-start.6
  10.8 1.7 %collective-permute-start = (bf16[4,8,1024]{2,1,0:T(8,128)(2,1)S(1)}, bf16[4,8,1024]{2,1,0:T(8,128)(2,1)S(1)}, u32[]{:S(2)}, u32[]{:S(2)}) collective-permute-start(bf16[4,8,1024]{2,1,0:T(8,128)(2,1)S(1)} %get-tuple-element.24), channel_id=1, source_target_pairs={{0,4},{4,0},{8,12},{12,8},{16,20},{20,16},{24,28},{28,24},{1,5},{5... | collective-permute-start | bytes 196616 | tf_op jit(solution)/shard_map/ppermute | solution.py:146
  12.5 0.7 %broadcast_subtract_fusion = s32[1024,2]{0,1:T(2,128)S(1)} fusion(s32[1024,2]{0,1:T(2,128)} %param.8, s32[]{:T(128)S(6)} %mul.27), kind=kLoop, calls=%fused_computation.52 | loop fusion | flops 2048 | bytes 16388 | tf_op jit(solution)/shard_map/sub | solution.py:430
  13.2 0.8 %fusion.20 = (s32[1024,1]{0,1:T(1,128)S(1)}, s32[1024,1]{0,1:T(1,128)S(1)}) fusion(s32[1024,2]{0,1:T(2,128)} %param.8), kind=kLoop, calls=%fused_computation.59 | loop fusion | bytes 16384 | tf_op jit(solution)/shard_map/slice | solution.py:474
  14.0 1.0 %fusion.1 = f32[1024,8]{0,1:T(8,128)S(1)} fusion(s32[1024]{0:T(1024)S(1)} %bitcast.52, s32[128,8]{0,1:T(8,128)} %param.10), kind=kOutput, calls=%fused_computation.4 | convolution fusion | flops 2229248 | bytes 40960 | tf_op jit(solution)/shard_map/dot_general | solution.py:474
  15.0 1.0 %fusion = f32[1024]{0:T(1024)S(1)} fusion(f32[1024,8]{0,1:T(8,128)S(1)} %fusion.1, s32[1024]{0:T(1024)S(1)} %bitcast.51, s32[128,8]{0,1:T(8,128)} %param.10), kind=kOutput, calls=%fused_computation.1 | convolution fusion | flops 2244608 | bytes 45056 | tf_op jit(solution)/shard_map/dot_general | solution.py:474
  16.1 0.7 %convert_multiply_fusion = f32[1024]{0:T(1024)S(1)} fusion(f32[1024]{0:T(1024)S(1)} %fusion, s32[1024]{0:T(1024)} %param.9), kind=kLoop, calls=%fused_computation.44 | loop fusion | flops 2048 | bytes 12288 | tf_op jit(solution)/shard_map/mul | solution.py:477
  16.8 1.3 %fusion.9.row_ref = s32[1024]{0:T(1024)} fusion(pred[1024]{0:T(1024)(128)(4,1)S(1)} %get-tuple-element.17, s32[1024]{0:T(1024)S(1)} %bitcast.45, s32[1024]{0:T(1024)S(1)} %bitcast.49, pred[1024]{0:T(1024)(128)(4,1)S(1)} %get-tuple-element.16, s32[1024]{0:T(1024)S(1)} %bitcast.48, s32[1024]{0:T(1024)S(1)} %bitcast.46, s32[1024]{0:T(1024)S(1)} %bitcast.47, ...), kind=kLoop, calls=%fused_computation.37 | loop fusion | flops 48128 | bytes 34816 | tf_op jit(solution)/shard_map/jit(clip)/min | solution.py:435
  18.0 0.8 %fusion.13 = f32[64,8]{0,1:T(8,128)S(1)} fusion(s32[]{:T(128)S(6)} %select_n.84, s32[128,8]{0,1:T(8,128)} %param.10), kind=kLoop, calls=%fused_computation.41 | loop fusion | flops 512 | bytes 6148 | tf_op jit(solution)/shard_map/convert_element_type | solution.py:429
  18.8 0.1 copy.9
  18.9 0.0 collective-permute-done.3
  18.9 0.1 collective-permute-start.1
  19.0 0.0 collective-permute-done.4
  19.0 1.8 %collective-permute-start.2 = (bf16[4,8,1024]{2,1,0:T(8,128)(2,1)S(1)}, bf16[4,8,1024]{2,1,0:T(8,128)(2,1)S(1)}, u32[]{:S(2)}, u32[]{:S(2)}) collective-permute-start(bf16[4,8,1024]{2,1,0:T(8,128)(2,1)S(1)} %get-tuple-element.22), channel_id=1, source_target_pairs={{0,12},{4,8},{8,4},{12,0},{16,28},{20,24},{24,20},{28,16},{1,13},{... | collective-permute-start | bytes 196616 | tf_op jit(solution)/shard_map/ppermute | solution.py:146
  20.8 0.0 collective-permute-done.5
  20.8 0.0 collective-permute-done.6
  20.8 1.3 %collective-permute-start.8 = (bf16[128,1024]{1,0:T(8,128)(2,1)S(1)}, bf16[128,1024]{1,0:T(8,128)(2,1)S(1)}, u32[]{:S(2)}, u32[]{:S(2)}) collective-permute-start(bf16[128,1024]{1,0:T(8,128)(2,1)S(1)} %maximum_bitcast_fusion.1.far_ref), channel_id=1, source_target_pairs={{0,1},{4,5},{8,9},{12,13},{1,2},{5,6},{9,10},{13,14},{17,16},{21,2... | collective-permute-start | bytes 786440 | tf_op jit(solution)/shard_map/ppermute | solution.py:151
  22.1 0.0 collective-permute-done
  22.1 1.1 %collective-permute-done.1 = bf16[4,8,1024]{2,1,0:T(8,128)(2,1)S(1)} collective-permute-done((bf16[4,8,1024]{2,1,0:T(8,128)(2,1)S(1)}, bf16[4,8,1024]{2,1,0:T(8,128)(2,1)S(1)}, u32[]{:S(2)}, u32[]{:S(2)}) %collective-permute-start.1) | collective-permute-done | bytes 65568 | tf_op jit(solution)/shard_map/ppermute | solution.py:146
  23.2 1.0 %collective-permute-done.2 = bf16[4,8,1024]{2,1,0:T(8,128)(2,1)S(1)} collective-permute-done((bf16[4,8,1024]{2,1,0:T(8,128)(2,1)S(1)}, bf16[4,8,1024]{2,1,0:T(8,128)(2,1)S(1)}, u32[]{:S(2)}, u32[]{:S(2)}) %collective-permute-start.2) | collective-permute-done | bytes 65568 | tf_op jit(solution)/shard_map/ppermute | solution.py:146
  24.3 1.3 %collective-permute-start.7 = (bf16[128,1024]{1,0:T(8,128)(2,1)S(1)}, bf16[128,1024]{1,0:T(8,128)(2,1)S(1)}, u32[]{:S(2)}, u32[]{:S(2)}) collective-permute-start(bf16[128,1024]{1,0:T(8,128)(2,1)S(1)} %maximum_bitcast_fusion.near_ref), channel_id=1, source_target_pairs={{16,17},{20,21},{24,25},{28,29},{1,0},{5,4},{9,8},{13,12},{17,18},... | collective-permute-start | bytes 786440 | tf_op jit(solution)/shard_map/ppermute | solution.py:150
  25.6 0.1 broadcast_in_dim.23.presence_ref
  25.7 0.0 copy-start
  25.7 1.6 %copy-done = bf16[1024,1024]{1,0:T(8,128)(2,1)S(1)} copy-done((bf16[1024,1024]{1,0:T(8,128)(2,1)S(1)}, bf16[1024,1024]{1,0:T(8,128)(2,1)}, u32[]{:S(2)}) %copy-start) | copy-done | bytes 2097176
  27.3 0.0 copy-start.2
  27.3 1.0 %copy-done.2 = bf16[1024,256]{1,0:T(8,128)(2,1)S(1)} copy-done((bf16[1024,256]{1,0:T(8,128)(2,1)S(1)}, bf16[1024,256]{1,0:T(8,128)(2,1)}, u32[]{:S(2)}) %copy-start.2) | copy-done | bytes 524312
  28.3 0.0 copy-start.10
  28.3 0.7 %copy-done.10 = f32[1,1024]{1,0:T(1,128)S(1)} copy-done((f32[1,1024]{1,0:T(1,128)S(1)}, f32[1,1024]{1,0:T(1,128)}, u32[]{:S(2)}) %copy-start.10) | copy-done | bytes 4120
  29.0 0.0 copy-start.1
  29.0 0.0 copy-start.3
  29.0 3.2 %shard_map.86 = (f32[32,8,1024]{2,1,0:T(8,128)S(1)}, bf16[6016,256]{1,0:T(8,128)(2,1)S(1)}, f32[8,768]{1,0:T(8,128)S(1)}) custom-call(s32[1]{0:T(128)} %bitcast.6.me_ref, bf16[128,1024]{1,0:T(8,128)(2,1)S(1)} %maximum_bitcast_fusion.near_ref, bf16[128,1024]{1,0:T(8,128)(2,1)S(1)} %maximum_bitcast_fusion.1.far_ref, ...), custom_call_target="tpu_custom_call" | custom-call | flops 2113929216 | bytes 8000000 | tf_op jit(solution)/shard_map/pallas_call | solution.py:343
  32.2 0.0 copy-start.9
  32.2 0.0 collective-permute-done.8.traces_ref
  32.2 0.0 copy-done.1
  32.2 0.0 copy-done.3
  32.2 1.4 %shard_map.88 = (bf16[1088,256]{1,0:T(8,128)(2,1)S(1)}, f32[8,256]{1,0:T(8,128)S(1)}) custom-call(s32[1]{0:T(128)} %bitcast.6.me_ref, bf16[128,1024]{1,0:T(8,128)(2,1)S(1)} %collective-permute-done.8.traces_ref, f32[32,8,1024]{2,1,0:T(8,128)S(1)} %get-tuple-element.10.own_ref, f32[64,8,128]{2,1,0:T(8,128)S(1)} %broadcast_in_dim.23.presence_ref, ...), custom_call_target="tpu_custom_call" | custom-call | flops 838860800 | bytes 4000000 | tf_op jit(solution)/shard_map/pallas_call | solution.py:363
  33.6 0.0 copy-start.4
  33.6 0.8 %copy-done.4 = bf16[1088,256]{1,0:T(8,128)(2,1)} copy-done((bf16[1088,256]{1,0:T(8,128)(2,1)}, bf16[1088,256]{1,0:T(8,128)(2,1)S(1)}, u32[]{:S(2)}) %copy-start.4) | copy-done | bytes 557080
  34.5 0.6 copy-done.11
  35.0 0.0 collective-permute-done.7.traces_ref
  35.0 1.4 %shard_map.87 = (bf16[1088,256]{1,0:T(8,128)(2,1)S(1)}, f32[8,256]{1,0:T(8,128)S(1)}) custom-call(s32[1]{0:T(128)} %bitcast.6.me_ref, bf16[128,1024]{1,0:T(8,128)(2,1)S(1)} %collective-permute-done.7.traces_ref, f32[32,8,1024]{2,1,0:T(8,128)S(1)} %get-tuple-element.10.own_ref, f32[64,8,128]{2,1,0:T(8,128)S(1)} %broadcast_in_dim.23.presence_ref, ...), custom_call_target="tpu_custom_call" | custom-call | flops 838860800 | bytes 4000000 | tf_op jit(solution)/shard_map/pallas_call | solution.py:363
  36.5 0.0 copy-done.9
  36.5 0.0 copy-start.6
  36.5 0.8 %copy-done.6 = bf16[1088,256]{1,0:T(8,128)(2,1)} copy-done((bf16[1088,256]{1,0:T(8,128)(2,1)}, bf16[1088,256]{1,0:T(8,128)(2,1)S(1)}, u32[]{:S(2)}) %copy-start.6) | copy-done | bytes 557080
  37.3 0.6 copy-done.12
  37.9 1.4 %shard_map.90 = f32[8,128]{1,0:T(8,128)} custom-call(f32[8,768]{1,0:T(8,128)} %copy-done.9, f32[8,256]{1,0:T(8,128)} %copy-done.12, f32[8,256]{1,0:T(8,128)} %copy-done.11, s32[8,128]{1,0:T(8,128)} %bitcast.35), custom_call_target="tpu_custom_call" | custom-call | flops 100000 | bytes 100000 | tf_op jit(solution)/shard_map/pallas_call | solution.py:381
  39.3 0.7 %pad_maximum_fusion = f32[2,1024]{1,0:T(2,128)S(1)} fusion(f32[1,1024]{1,0:T(1,128)S(1)} %bitcast.38, f32[1,1024]{1,0:T(1,128)} %bitcast.41), kind=kLoop, calls=%fused_computation.20 | loop fusion | flops 2048 | bytes 16384 | tf_op jit(solution)/shard_map/stack | solution.py:482
  40.0 4.2 %collective-permute-start.9 = (f32[2,1024]{1,0:T(2,128)S(1)}, f32[2,1024]{1,0:T(2,128)S(1)}, u32[]{:S(2)}, u32[]{:S(2)}) collective-permute-start(f32[2,1024]{1,0:T(2,128)S(1)} %pad_maximum_fusion), channel_id=1, source_target_pairs={{0,16},{4,20},{8,24},{12,28},{16,0},{20,4},{24,8},{28,12},{1,17},{... | collective-permute-start | bytes 24584 | tf_op jit(solution)/shard_map/ppermute | solution.py:486
  44.2 1.6 %collective-permute-done.9 = f32[2,1024]{1,0:T(2,128)S(1)} collective-permute-done((f32[2,1024]{1,0:T(2,128)S(1)}, f32[2,1024]{1,0:T(2,128)S(1)}, u32[]{:S(2)}, u32[]{:S(2)}) %collective-permute-start.9) | collective-permute-done | bytes 8224 | tf_op jit(solution)/shard_map/ppermute | solution.py:486
  45.8 0.7 %fusion.19 = f32[2,1024]{1,0:T(2,128)S(1)} fusion(f32[2,1024]{1,0:T(2,128)S(1)} %collective-permute-done.9, f32[1,1024]{1,0:T(1,128)S(1)} %bitcast.39, f32[1,1024]{1,0:T(1,128)} %bitcast.42), kind=kLoop, calls=%fused_computation.58 | loop fusion | flops 4096 | bytes 24576 | tf_op jit(solution)/shard_map/add | solution.py:486
  46.5 0.8 %collective-permute-start.10 = (f32[2,1024]{1,0:T(2,128)S(1)}, f32[2,1024]{1,0:T(2,128)S(1)}, u32[]{:S(2)}, u32[]{:S(2)}) collective-permute-start(f32[2,1024]{1,0:T(2,128)S(1)} %fusion.19), channel_id=1, source_target_pairs={{0,8},{4,12},{8,0},{12,4},{16,24},{20,28},{24,16},{28,20},{1,9},{5... | collective-permute-start | bytes 24584 | tf_op jit(solution)/shard_map/ppermute | solution.py:486
  47.3 2.9 %collective-permute-done.10 = f32[2,1024]{1,0:T(2,128)S(1)} collective-permute-done((f32[2,1024]{1,0:T(2,128)S(1)}, f32[2,1024]{1,0:T(2,128)S(1)}, u32[]{:S(2)}, u32[]{:S(2)}) %collective-permute-start.10) | collective-permute-done | bytes 8224 | tf_op jit(solution)/shard_map/ppermute | solution.py:486
  50.2 0.7 %fusion.21 = f32[2,1024]{1,0:T(2,128)S(1)} fusion(f32[2,1024]{1,0:T(2,128)S(1)} %collective-permute-done.10, f32[2,1024]{1,0:T(2,128)S(1)} %collective-permute-done.9, f32[1,1024]{1,0:T(1,128)S(1)} %bitcast.40, f32[1,1024]{1,0:T(1,128)} %bitcast.43), kind=kLoop, calls=%fused_computation.60 | loop fusion | flops 6144 | bytes 32768 | tf_op jit(solution)/shard_map/add | solution.py:486
  50.9 0.6 %collective-permute-start.11 = (f32[2,1024]{1,0:T(2,128)S(1)}, f32[2,1024]{1,0:T(2,128)S(1)}, u32[]{:S(2)}, u32[]{:S(2)}) collective-permute-start(f32[2,1024]{1,0:T(2,128)S(1)} %fusion.21), channel_id=1, source_target_pairs={{0,4},{4,0},{8,12},{12,8},{16,20},{20,16},{24,28},{28,24},{1,5},{5... | collective-permute-start | bytes 24584 | tf_op jit(solution)/shard_map/ppermute | solution.py:486
  51.5 0.0 copy-done.8
  51.5 1.1 %copy-done.5 = bf16[1088,256]{1,0:T(8,128)(2,1)S(1)} copy-done((bf16[1088,256]{1,0:T(8,128)(2,1)S(1)}, bf16[1088,256]{1,0:T(8,128)(2,1)}, u32[]{:S(2)}) %copy-start.5) | copy-done | bytes 557080
  52.6 1.1 %copy-done.7 = bf16[1088,256]{1,0:T(8,128)(2,1)S(1)} copy-done((bf16[1088,256]{1,0:T(8,128)(2,1)S(1)}, bf16[1088,256]{1,0:T(8,128)(2,1)}, u32[]{:S(2)}) %copy-start.7) | copy-done | bytes 557080
  53.6 5.1 %shard_map.89 = bf16[8192,256]{1,0:T(8,128)(2,1)} custom-call(s32[1024]{0:T(1024)S(1)} %copy-done.8, bf16[6016,256]{1,0:T(8,128)(2,1)S(1)} %get-tuple-element.9.refs_0_, bf16[1088,256]{1,0:T(8,128)(2,1)S(1)} %copy-done.7, bf16[1088,256]{1,0:T(8,128)(2,1)S(1)} %copy-done.5), custom_call_target="tpu_custom_call" | custom-call | flops 10000000 | bytes 10000000 | tf_op jit(solution)/shard_map/pallas_call | solution.py:394
  58.7 0.0 collective-permute-done.11
  58.7 0.6 %fusion.14 = f32[1,1024]{1,0:T(1,128)} fusion(f32[2,1024]{1,0:T(2,128)S(1)} %add.90), kind=kLoop, calls=%fused_computation.43 | loop fusion | flops 2048 | bytes 12288 | tf_op jit(solution)/shard_map/div | solution.py:490
  (10 shorter events, 0.2 us)
Async XLA Ops:
  1.8 17.1 %collective-permute-start.3 = (bf16[4,8,1024]{2,1,0:T(8,128)(2,1)S(1)}, bf16[4,8,1024]{2,1,0:T(8,128)(2,1)S(1)}, u32[]{:S(2)}, u32[]{:S(2)}) collective-permute-start(bf16[4,8,1024]{2,1,0:T(8,128)(2,1)S(1)} %get-tuple-element.18), channel_id=1, source_target_pairs={{0,16},{4,20},{8,24},{12,28},{16,0},{20,4},{24,8},{28,12},{1,17},{... | collective-permute-start | bytes 196616 | tf_op jit(solution)/shard_map/ppermute | solution.py:146
  5.9 13.1 %collective-permute-start.4 = (bf16[4,8,1024]{2,1,0:T(8,128)(2,1)S(1)}, bf16[4,8,1024]{2,1,0:T(8,128)(2,1)S(1)}, u32[]{:S(2)}, u32[]{:S(2)}) collective-permute-start(bf16[4,8,1024]{2,1,0:T(8,128)(2,1)S(1)} %get-tuple-element.21), channel_id=1, source_target_pairs={{0,20},{4,16},{8,28},{12,24},{16,4},{20,0},{24,12},{28,8},{1,21},{... | collective-permute-start | bytes 196616 | tf_op jit(solution)/shard_map/ppermute | solution.py:146
  7.2 13.6 %collective-permute-start.5 = (bf16[4,8,1024]{2,1,0:T(8,128)(2,1)S(1)}, bf16[4,8,1024]{2,1,0:T(8,128)(2,1)S(1)}, u32[]{:S(2)}, u32[]{:S(2)}) collective-permute-start(bf16[4,8,1024]{2,1,0:T(8,128)(2,1)S(1)} %get-tuple-element.20), channel_id=1, source_target_pairs={{0,24},{4,28},{8,16},{12,20},{16,8},{20,12},{24,0},{28,4},{1,25},{... | collective-permute-start | bytes 196616 | tf_op jit(solution)/shard_map/ppermute | solution.py:146
  10.8 10.0 %collective-permute-start.6 = (bf16[4,8,1024]{2,1,0:T(8,128)(2,1)S(1)}, bf16[4,8,1024]{2,1,0:T(8,128)(2,1)S(1)}, u32[]{:S(2)}, u32[]{:S(2)}) collective-permute-start(bf16[4,8,1024]{2,1,0:T(8,128)(2,1)S(1)} %get-tuple-element.19), channel_id=1, source_target_pairs={{0,28},{4,24},{8,20},{12,16},{16,12},{20,8},{24,4},{28,0},{1,29},{... | collective-permute-start | bytes 196616 | tf_op jit(solution)/shard_map/ppermute | solution.py:146
  10.8 11.4 %collective-permute-start = (bf16[4,8,1024]{2,1,0:T(8,128)(2,1)S(1)}, bf16[4,8,1024]{2,1,0:T(8,128)(2,1)S(1)}, u32[]{:S(2)}, u32[]{:S(2)}) collective-permute-start(bf16[4,8,1024]{2,1,0:T(8,128)(2,1)S(1)} %get-tuple-element.24), channel_id=1, source_target_pairs={{0,4},{4,0},{8,12},{12,8},{16,20},{20,16},{24,28},{28,24},{1,5},{5... | collective-permute-start | bytes 196616 | tf_op jit(solution)/shard_map/ppermute | solution.py:146
  18.9 4.3 %collective-permute-start.1 = (bf16[4,8,1024]{2,1,0:T(8,128)(2,1)S(1)}, bf16[4,8,1024]{2,1,0:T(8,128)(2,1)S(1)}, u32[]{:S(2)}, u32[]{:S(2)}) collective-permute-start(bf16[4,8,1024]{2,1,0:T(8,128)(2,1)S(1)} %get-tuple-element.23), channel_id=1, source_target_pairs={{0,8},{4,12},{8,0},{12,4},{16,24},{20,28},{24,16},{28,20},{1,9},{5... | collective-permute-start | bytes 196616 | tf_op jit(solution)/shard_map/ppermute | solution.py:146
  19.0 5.2 %collective-permute-start.2 = (bf16[4,8,1024]{2,1,0:T(8,128)(2,1)S(1)}, bf16[4,8,1024]{2,1,0:T(8,128)(2,1)S(1)}, u32[]{:S(2)}, u32[]{:S(2)}) collective-permute-start(bf16[4,8,1024]{2,1,0:T(8,128)(2,1)S(1)} %get-tuple-element.22), channel_id=1, source_target_pairs={{0,12},{4,8},{8,4},{12,0},{16,28},{20,24},{24,20},{28,16},{1,13},{... | collective-permute-start | bytes 196616 | tf_op jit(solution)/shard_map/ppermute | solution.py:146
  20.8 11.4 %collective-permute-start.8 = (bf16[128,1024]{1,0:T(8,128)(2,1)S(1)}, bf16[128,1024]{1,0:T(8,128)(2,1)S(1)}, u32[]{:S(2)}, u32[]{:S(2)}) collective-permute-start(bf16[128,1024]{1,0:T(8,128)(2,1)S(1)} %maximum_bitcast_fusion.1.far_ref), channel_id=1, source_target_pairs={{0,1},{4,5},{8,9},{12,13},{1,2},{5,6},{9,10},{13,14},{17,16},{21,2... | collective-permute-start | bytes 786440 | tf_op jit(solution)/shard_map/ppermute | solution.py:151
  24.3 10.8 %collective-permute-start.7 = (bf16[128,1024]{1,0:T(8,128)(2,1)S(1)}, bf16[128,1024]{1,0:T(8,128)(2,1)S(1)}, u32[]{:S(2)}, u32[]{:S(2)}) collective-permute-start(bf16[128,1024]{1,0:T(8,128)(2,1)S(1)} %maximum_bitcast_fusion.near_ref), channel_id=1, source_target_pairs={{16,17},{20,21},{24,25},{28,29},{1,0},{5,4},{9,8},{13,12},{17,18},... | collective-permute-start | bytes 786440 | tf_op jit(solution)/shard_map/ppermute | solution.py:150
  25.7 1.6 %copy-start = (bf16[1024,1024]{1,0:T(8,128)(2,1)S(1)}, bf16[1024,1024]{1,0:T(8,128)(2,1)}, u32[]{:S(2)}) copy-start(bf16[1024,1024]{1,0:T(8,128)(2,1)} %constant.103.clone.forward_ref) | copy-start | bytes 6291460
  27.3 1.0 %copy-start.2 = (bf16[1024,256]{1,0:T(8,128)(2,1)S(1)}, bf16[1024,256]{1,0:T(8,128)(2,1)}, u32[]{:S(2)}) copy-start(bf16[1024,256]{1,0:T(8,128)(2,1)} %constant.104.clone.inverse_ref) | copy-start | bytes 1572868
  28.3 0.7 %copy-start.10 = (f32[1,1024]{1,0:T(1,128)S(1)}, f32[1,1024]{1,0:T(1,128)}, u32[]{:S(2)}) copy-start(f32[1,1024]{1,0:T(1,128)} %constant.105.clone.weights_ref) | copy-start | bytes 12292
  29.0 3.2 %copy-start.1 = (bf16[1024,1024]{1,0:T(8,128)(2,1)S(1)}, bf16[1024,1024]{1,0:T(8,128)(2,1)}, u32[]{:S(2)}) copy-start(bf16[1024,1024]{1,0:T(8,128)(2,1)} %constant.103.clone.forward_ref) | copy-start | bytes 6291460
  29.0 3.2 %copy-start.3 = (bf16[1024,256]{1,0:T(8,128)(2,1)S(1)}, bf16[1024,256]{1,0:T(8,128)(2,1)}, u32[]{:S(2)}) copy-start(bf16[1024,256]{1,0:T(8,128)(2,1)} %constant.104.clone.inverse_ref) | copy-start | bytes 1572868
  32.2 4.3 %copy-start.9 = (f32[8,768]{1,0:T(8,128)}, f32[8,768]{1,0:T(8,128)S(1)}, u32[]{:S(2)}) copy-start(f32[8,768]{1,0:T(8,128)S(1)} %get-tuple-element.13.own_ref) | copy-start | bytes 73732
  33.6 0.8 %copy-start.4 = (bf16[1088,256]{1,0:T(8,128)(2,1)}, bf16[1088,256]{1,0:T(8,128)(2,1)S(1)}, u32[]{:S(2)}) copy-start(bf16[1088,256]{1,0:T(8,128)(2,1)S(1)} %get-tuple-element.12.refs_2_) | copy-start | bytes 1671172
  34.4 0.6 copy-start.11
  35.0 16.5 %copy-start.8 = (s32[1024]{0:T(1024)S(1)}, s32[1024]{0:T(1024)}, u32[]{:S(2)}) copy-start(s32[1024]{0:T(1024)} %fusion.9.row_ref) | copy-start | bytes 12292
  36.5 0.8 %copy-start.6 = (bf16[1088,256]{1,0:T(8,128)(2,1)}, bf16[1088,256]{1,0:T(8,128)(2,1)S(1)}, u32[]{:S(2)}) copy-start(bf16[1088,256]{1,0:T(8,128)(2,1)S(1)} %get-tuple-element.11.refs_1_) | copy-start | bytes 1671172
  37.3 0.6 copy-start.12
  40.0 5.8 %collective-permute-start.9 = (f32[2,1024]{1,0:T(2,128)S(1)}, f32[2,1024]{1,0:T(2,128)S(1)}, u32[]{:S(2)}, u32[]{:S(2)}) collective-permute-start(f32[2,1024]{1,0:T(2,128)S(1)} %pad_maximum_fusion), channel_id=1, source_target_pairs={{0,16},{4,20},{8,24},{12,28},{16,0},{20,4},{24,8},{28,12},{1,17},{... | collective-permute-start | bytes 24584 | tf_op jit(solution)/shard_map/ppermute | solution.py:486
  46.5 3.7 %collective-permute-start.10 = (f32[2,1024]{1,0:T(2,128)S(1)}, f32[2,1024]{1,0:T(2,128)S(1)}, u32[]{:S(2)}, u32[]{:S(2)}) collective-permute-start(f32[2,1024]{1,0:T(2,128)S(1)} %fusion.19), channel_id=1, source_target_pairs={{0,8},{4,12},{8,0},{12,4},{16,24},{20,28},{24,16},{28,20},{1,9},{5... | collective-permute-start | bytes 24584 | tf_op jit(solution)/shard_map/ppermute | solution.py:486
  50.9 7.8 %collective-permute-start.11 = (f32[2,1024]{1,0:T(2,128)S(1)}, f32[2,1024]{1,0:T(2,128)S(1)}, u32[]{:S(2)}, u32[]{:S(2)}) collective-permute-start(f32[2,1024]{1,0:T(2,128)S(1)} %fusion.21), channel_id=1, source_target_pairs={{0,4},{4,0},{8,12},{12,8},{16,20},{20,16},{24,28},{28,24},{1,5},{5... | collective-permute-start | bytes 24584 | tf_op jit(solution)/shard_map/ppermute | solution.py:486
  51.5 1.1 %copy-start.5 = (bf16[1088,256]{1,0:T(8,128)(2,1)S(1)}, bf16[1088,256]{1,0:T(8,128)(2,1)}, u32[]{:S(2)}) copy-start(bf16[1088,256]{1,0:T(8,128)(2,1)} %copy-done.4) | copy-start | bytes 1671172
  52.6 1.1 %copy-start.7 = (bf16[1088,256]{1,0:T(8,128)(2,1)S(1)}, bf16[1088,256]{1,0:T(8,128)(2,1)}, u32[]{:S(2)}) copy-start(bf16[1088,256]{1,0:T(8,128)(2,1)} %copy-done.6) | copy-start | bytes 1671172

commit v3 on v1

--- a/solution.py
+++ b/solution.py
@@ -152,9 +152,8 @@
     return (near, far, near_halo, far_halo), me
 
 
-def exchange_whole(waveforms, sta_count):
-    events, stations, window = waveforms.shape
-    share = stations // sta_count
+def exchange_whole(waveforms):
+    window = waveforms.shape[2]
     arrived = lax.all_to_all(waveforms, "sta", split_axis=1, concat_axis=0, tiled=True)
     arrived = arrived.reshape(-1, window)
     half = arrived.shape[0] // 2
@@ -163,51 +162,377 @@
     up = [(i, i + 1) for i in range(count - 1)]
     next_low = lax.ppermute(arrived[:half], "evt", down)
     last_high = lax.ppermute(arrived[half:], "evt", up)
-    return (arrived, next_low, last_high), jnp.int32(0)
+    return arrived, next_low, last_high
+
+
+def triangle(count):
+    return count * (count + 1) // 2
+
+
+def own_list(block):
+    band = block // 2
+    return [(x, y) for x in range(block) for y in range(x + 1, min(x + band, block - 1) + 1)]
+
+
+class Rows:
+    def __init__(self, block):
+        self.own = len(own_list(block))
+        self.zero = 2 * self.own
+        self.near = self.zero + 8
+        self.far = self.near + triangle(block // 2)
+        self.end = self.far + triangle(block // 2)
+        self.lanes = -(-self.end // LANES) * LANES
+
+
+def cross_spectra(first, second):
+    half = first.shape[1] // 2
+    ra, ia = first[:, :half], first[:, half:]
+    rb, ib = second[:, :half], second[:, half:]
+    return jnp.concatenate([ra * rb + ia * ib, ra * ib - ia * rb], axis=1)
+
+
+def scaled_spectra(traces_ref, me, each, place, presence_ref, present, forward_ref, weights_ref, spec_ref):
+    stations, window = spec_ref.shape[1:]
+    events = traces_ref.shape[0] // stations
+    pieces = events // each
+    result = jnp.dot(traces_ref[...], forward_ref[...], preferred_element_type=jnp.float32)
+    rounded = result.astype(jnp.bfloat16).astype(jnp.float32)
+    energy = jnp.sum(jnp.square(rounded) * weights_ref[...], axis=1, keepdims=True) + 1e-06
+    gain = jnp.broadcast_to(lax.rsqrt(energy), (events * stations, LANES)).reshape(events, stations, LANES)
+    rounded = rounded.reshape(events, stations, window)
+    for j in range(pieces):
+        shift = ((me ^ j) & (pieces - 1)) * each
+        piece = slice(j * each, (j + 1) * each)
+        scale = gain[piece] * presence_ref[pl.ds(present + shift, each)]
+        scale = jnp.concatenate([scale] * (window // LANES), axis=2)
+        spec_ref[pl.ds(place + shift, each)] = rounded[piece] * scale
+
+
+def build(lhs_ref, low, pairs, first_of, second_of):
+    for i in range(0, len(pairs), 2):
+        both = [cross_spectra(first_of(x), second_of(y)) for x, y in pairs[i:i + 2]]
+        rows = 2 * both[0].shape[0]
+        lhs_ref[pl.ds((low + i) * rows // 2, rows), :] = jnp.concatenate(both, axis=0).astype(jnp.bfloat16)
+
+
+def keep(table_ref, peaks, values, row):
+    stations, lags = table_ref.shape[1:]
+    lane = lax.broadcasted_iota(jnp.int32, (stations, LANES), 1)
+    count = values.shape[0] // stations
+    for i in range(count):
+        top = jnp.max(values[i * stations:(i + 1) * stations], axis=1, keepdims=True)
+        at, within = divmod(row + i, LANES)
+        peaks[at] = jnp.where(lane == within, top, peaks[at])
+    table_ref[pl.ds(row, count)] = values.reshape(count, stations, lags).astype(jnp.bfloat16)
+
+
+def no_peaks(rows, stations):
+    return [jnp.zeros((stations, LANES), jnp.float32) for _ in range(rows.lanes // LANES)]
+
+
+def prepare_kernel(
+    each, block, at_ref, events_ref, valid_ref, presence_ref, forward_ref, inverse_ref,
+    row_ref, count_ref, held_ref, forward_out, inverse_out, sems,
+):
+    copies = [
+        pltpu.make_async_copy(forward_ref, forward_out, sems.at[0]),
+        pltpu.make_async_copy(inverse_ref, inverse_out, sems.at[1]),
+    ]
+    for copy in copies:
+        copy.start()
+    me, start = at_ref[0], at_ref[1]
+    lines = row_ref.shape[0]
+
+    def stacked(ref, line):
+        return jnp.concatenate([ref[line:line + 1, i * LANES:(i + 1) * LANES] for i in range(lines)], axis=0)
+
+    first, second, valid = stacked(events_ref, 0), stacked(events_ref, 1), stacked(valid_ref, 0)
+    rows = Rows(block)
+    row = table_row(first - start, second - start, me, each, block, rows)
+    row = jnp.where(valid > 0, row, rows.zero)
+    row_ref[...] = jnp.clip(row, 0, rows.end - 1)
+
+    presence = presence_ref[...]
+    stations, events = presence.shape
+    bits = jnp.zeros((1, events), jnp.int32)
+    for s in range(stations):
+        bits = bits + presence[s:s + 1] * (1 << s)
+    bits = jnp.broadcast_to(bits, (lines, events))
+    both = jnp.take_along_axis(bits, first, axis=1) & jnp.take_along_axis(bits, second, axis=1)
+    count = jnp.zeros_like(both)
+    for s in range(stations):
+        count = count + (lax.shift_right_logical(both, s) & 1)
+    count_ref[...] = (count * valid).astype(jnp.float32)
+
+    lane = lax.broadcasted_iota(jnp.int32, presence.shape, 1)
+    present = presence.astype(jnp.float32)
+    for i in range(held_ref.shape[0]):
+        mine = jnp.where(lane == start - block // 2 + i, present, 0.0)
+        held_ref[i] = jnp.broadcast_to(jnp.sum(mine, axis=1, keepdims=True), (stations, LANES))
+    for copy in copies:
+        copy.wait()
+
+
+def own_pairs(spec_ref, inverse_ref, table_ref, peaks, lhs_ref):
+    block, stations, window = spec_ref.shape
+    half = window // 2
+    pairs = own_list(block)
+    chunk = 64
+    for low in range(0, len(pairs), chunk):
+        some = pairs[low:low + chunk]
+        held = {x: spec_ref[x] for x, _ in some}
+        build(lhs_ref, low, some, lambda x: held[x], lambda y: spec_ref[y])
+        rows = pl.ds(low * stations, len(some) * stations)
+        even = jnp.dot(lhs_ref[rows, :half], inverse_ref[:half], preferred_element_type=jnp.float32)
+        odd = jnp.dot(lhs_ref[rows, half:], inverse_ref[half:], preferred_element_type=jnp.float32)
+        keep(table_ref, peaks, even + odd, low)
+        keep(table_ref, peaks, even - odd, len(pairs) + low)
+
+
+def halo_pairs(high, own_ref, spec_ref, inverse_ref, table_ref, peaks, lhs_ref, row):
+    band, stations = spec_ref.shape[:2]
+
+    def own(u):
+        return own_ref[jnp.where(high, band + u, band - 1 - u)]
+
+    def other(h):
+        return spec_ref[jnp.where(high, h, band - 1 - h)]
+
+    pairs = [(u, h) for u in range(band) for h in range(u + 1)]
+    chunk = 68
+    for low in range(0, len(pairs), chunk):
+        some = pairs[low:low + chunk]
+        held = {u: own(u) for u, _ in some}
+        build(lhs_ref, low, some, lambda u: held[u], other)
+        rows = pl.ds(low * stations, len(some) * stations)
+        lagged = jnp.dot(lhs_ref[rows, :], inverse_ref[...], preferred_element_type=jnp.float32)
+        keep(table_ref, peaks, lagged, row + low)
+
+
+def first_kernel(
+    each, at_ref, near_ref, far_ref, halo_ref, presence_ref, forward_ref, inverse_ref, weights_ref,
+    spec_ref, table_ref, peak_ref, other_ref, lhs_ref,
+):
+    block, stations, window = spec_ref.shape
+    band = block // 2
+    me = at_ref[0]
+    low_half = me * each < band
+    mine = jnp.where(low_half, 0, band)
+    for ref, place in ((near_ref, mine), (far_ref, band - mine)):
+        scaled_spectra(
+            ref, me, each, place, presence_ref, band + place, forward_ref, weights_ref, spec_ref
+        )
+    edge = jnp.where(low_half, 3 * band, 0)
+    scaled_spectra(halo_ref, me, each, 0, presence_ref, edge, forward_ref, weights_ref, other_ref)
+    rows = Rows(block)
+    peaks = no_peaks(rows, stations)
+    own_pairs(spec_ref, inverse_ref, table_ref, peaks, lhs_ref)
+    halo_pairs(low_half, spec_ref, other_ref, inverse_ref, table_ref, peaks, lhs_ref, rows.near)
+    table_ref[rows.zero] = jnp.zeros(table_ref.shape[1:], table_ref.dtype)
+    peak_ref[...] = jnp.concatenate(peaks, axis=1)
+
+
+def last_kernel(
+    each, at_ref, halo_ref, own_ref, presence_ref, forward_ref, inverse_ref, weights_ref, peak_ref, row_ref, count_ref,
+    held_table_ref, table_ref, sums_ref, other_ref, lhs_ref,
+):
+    del held_table_ref
+    block, stations, window = own_ref.shape
+    band = block // 2
+    me = at_ref[0]
+    high = me * each >= band
+    edge = jnp.where(high, 3 * band, 0)
+    scaled_spectra(halo_ref, me, each, 0, presence_ref, edge, forward_ref, weights_ref, other_ref)
+    rows = Rows(block)
+    peaks = no_peaks(rows, stations)
+    halo_pairs(high, own_ref, other_ref, inverse_ref, table_ref, peaks, lhs_ref, rows.far)
+    row = row_ref[...]
+    lanes = row & (LANES - 1)
+    total = jnp.zeros(row.shape, jnp.float32)
+    for at, late in enumerate(peaks):
+        line = jnp.sum(peak_ref[:, at * LANES:(at + 1) * LANES] + late, axis=0, keepdims=True)
+        picked = jnp.take_along_axis(jnp.broadcast_to(line, row.shape), lanes, axis=1)
+        total = jnp.where(lax.shift_right_logical(row, 7) == at, picked, total)
+    sums_ref[0] = total
+    sums_ref[1] = count_ref[...]
+
+
+def pick_kernel(group, skip, row_ref, table_ref, *refs):
+    out_ref = refs[-1]
+    base = (pl.program_id(0) + skip) * group
+    for j in range(group):
+        out_ref[j] = table_ref[row_ref[base + j]]
+
+
+VMEM = pl.BlockSpec(memory_space=pltpu.VMEM)
+SMEM = pl.BlockSpec(memory_space=pltpu.SMEM)
+PARAMS = pltpu.CompilerParams(vmem_limit_bytes=20 * 1024 * 1024)
+
+
+def cost(rows, lags, window, traces, moved):
+    return pl.CostEstimate(
+        flops=2 * window * (rows * lags + traces * window), bytes_accessed=moved, transcendentals=0
+    )
+
+
+def prepare_call(at, pair_events, pair_valid, presence, tables, each, block):
+    forward, inverse = tables[:2]
+    pairs = pair_events.shape[0]
+    stations = presence.shape[1]
+    line = (pairs // LANES, LANES)
+    anywhere = pl.BlockSpec(memory_space=pl.ANY)
+    return pl.pallas_call(
+        functools.partial(prepare_kernel, each, block),
+        out_shape=(
+            jax.ShapeDtypeStruct(line, jnp.int32),
+            jax.ShapeDtypeStruct(line, jnp.float32),
+            jax.ShapeDtypeStruct((2 * block, stations, LANES), jnp.float32),
+            jax.ShapeDtypeStruct(forward.shape, forward.dtype),
+            jax.ShapeDtypeStruct(inverse.shape, inverse.dtype),
+        ),
+        in_specs=[SMEM] + [VMEM] * 3 + [anywhere] * 2,
+        out_specs=(VMEM,) * 5,
+        scratch_shapes=[pltpu.SemaphoreType.DMA((2,))],
+        compiler_params=PARAMS,
+        cost_estimate=pl.CostEstimate(flops=1_000_000, bytes_accessed=5_000_000, transcendentals=0),
+    )(at, pair_events.T, pair_valid.reshape(1, pairs), presence.T, forward, inverse)
+
+
+def first_call(at, near, far, halo, presence, tables, each, block):
+    forward, inverse, weights = tables
+    window, lags = inverse.shape
+    stations = presence.shape[1]
+    rows = Rows(block)
+    return pl.pallas_call(
+        functools.partial(first_kernel, each),
+        out_shape=(
+            jax.ShapeDtypeStruct((block, stations, window), jnp.float32),
+            jax.ShapeDtypeStruct((rows.end, stations, lags), jnp.bfloat16),
+            jax.ShapeDtypeStruct((stations, rows.lanes), jnp.float32),
+        ),
+        in_specs=[SMEM] + [VMEM] * 7,
+        out_specs=(VMEM,) * 3,
+        scratch_shapes=[
+            pltpu.VMEM((block // 2, stations, window), jnp.float32),
+            pltpu.VMEM((rows.own * stations, window), jnp.bfloat16),
+        ],
+        compiler_params=PARAMS,
+        cost_estimate=cost(rows.far * stations, lags, window, near.shape[0] * 3, 8_000_000),
+    )(at, near, far, halo, presence, forward, inverse, weights)
+
+
+def last_call(at, halo, own, presence, tables, peaks, row, count, table, each):
+    forward, inverse, weights = tables
+    window, lags = inverse.shape
+    block, stations = own.shape[:2]
+    pairs = triangle(block // 2)
+    return pl.pallas_call(
+        functools.partial(last_kernel, each),
+        out_shape=(
+            jax.ShapeDtypeStruct(table.shape, table.dtype),
+            jax.ShapeDtypeStruct((2,) + row.shape, jnp.float32),
+        ),
+        in_specs=[SMEM] + [VMEM] * 10,
+        out_specs=(VMEM,) * 2,
+        scratch_shapes=[
+            pltpu.VMEM((block // 2, stations, window), jnp.float32),
+            pltpu.VMEM((pairs * stations, window), jnp.bfloat16),
+        ],
+        input_output_aliases={10: 0},
+        compiler_params=PARAMS,
+        cost_estimate=cost(pairs * stations, lags, window, halo.shape[0], 4_000_000),
+    )(at, halo, own, presence, forward, inverse, weights, peaks, row, count, table)
+
+
+def pick_call(row, table, held, skip, steps):
+    pairs = row.shape[0]
+    block = (LANES,) + table.shape[1:]
+    return pl.pallas_call(
+        functools.partial(pick_kernel, LANES, skip),
+        grid=(steps,),
+        out_shape=jax.ShapeDtypeStruct((pairs,) + table.shape[1:], table.dtype),
+        in_specs=[SMEM, VMEM] + [pl.BlockSpec(memory_space=pl.ANY)] * len(held),
+        out_specs=pl.BlockSpec(block, lambda i: (i + skip, 0, 0)),
+        input_output_aliases={2: 0} if held else {},
+        compiler_params=PARAMS,
+        cost_estimate=pl.CostEstimate(flops=1_000_000, bytes_accessed=3_000_000 * steps, transcendentals=0),
+    )(row, table, *held)
+
+
+def table_row(first, second, me, each, block, rows):
+    band = block // 2
+    low, apart = jnp.minimum(first, second), jnp.abs(first - second)
+    past = jnp.maximum(low - band, 0)
+    index = jnp.minimum(low, band) * band + past * (band - 1) - (past * (past - 1) >> 1) + apart - 1
+    inside = jnp.where(second > first, index, rows.own + index)
+    high = second >= block
+    u = jnp.where(high, first - band, band - 1 - first)
+    h = jnp.where(high, second - block, -1 - second)
+    near = jnp.where(high, 1, 0) == jnp.where(me * each < band, 1, 0)
+    outside = jnp.where(near, rows.near, rows.far) + (u * (u + 1) >> 1) + h
+    return jnp.where(high | (second < 0), outside, inside)
+
+
+def banded(waveforms, pair_events, pair_valid, presence, start, block, tables):
+    each = waveforms.shape[0]
+    (near, far, near_halo, far_halo), me = exchange(waveforms, lax.axis_size("sta"))
+    at = jnp.stack([me, start]).astype(jnp.int32)
+    near, at = lax.optimization_barrier((near, at))
+    row, count, held, forward, inverse = prepare_call(at, pair_events, pair_valid, presence, tables, each, block)
+    tables = (forward, inverse, tables[2])
+    own, table, peaks = first_call(at, near, far, near_halo, held, tables, each, block)
+    table, sums = last_call(at, far_halo, own, held, tables, peaks, row, count, table, each)
+
+    row = row.reshape(-1)
+    groups = row.shape[0] // LANES
+    correlation = ()
+    step, skip = lax.axis_size("sta") // 2, 0
+    while step:
+        arrived = lax.ppermute(sums, "sta", [(i, i ^ step) for i in range(lax.axis_size("sta"))])
+        steps = -(-(groups - skip) // step.bit_length())
+        correlation = (pick_call(row, table, correlation, skip, steps),)
+        sums, correlation = lax.optimization_barrier((sums + arrived, correlation))
+        skip += steps
+        step //= 2
+    return correlation[0], sums
+
+
+def by_slot(waveforms, pair_events, pair_valid, presence, start, block, tables):
+    share = presence.shape[1]
+    traces = exchange_whole(waveforms)
+    place = pair_events - start
+    slot = jnp.where((place >= 0) & (place < block), 0, block) + place % block
+    gained = jnp.where(pair_valid > 0, slot[:, 0], 2 * block)
+    slots = jnp.stack([slot[:, 0], slot[:, 1], gained]).astype(jnp.int32)
+    held = jnp.arange(2 * block, dtype=jnp.int32)
+    held = jnp.where(held < block, held, jnp.where(held < block + block // 2, held, held - 2 * block))
+    held = jnp.clip(start + held, 0, presence.shape[0] - 1)
+    slot_presence = jnp.broadcast_to(
+        jnp.take(presence.astype(jnp.float32), held, axis=0)[:, :, None], (2 * block, share, LANES)
+    )
+    few = presence.astype(jnp.bfloat16)
+    event = jnp.arange(presence.shape[0], dtype=jnp.int32)
+    first, second = (
+        jnp.dot((pair_events[:, i:i + 1] == event).astype(jnp.bfloat16), few, preferred_element_type=jnp.float32)
+        for i in (0, 1)
+    )
+    counts = jnp.sum(first * second, axis=1) * pair_valid.astype(jnp.float32)
+    correlation, peaks = pair_call(slots, traces, slot_presence, tables)
+    sums = lax.psum(jnp.stack([peaks.reshape(-1), counts]), "sta")
+    return correlation.reshape(-1, share, correlation.shape[1]), sums
 
 
 def body(waveforms, pair_events, pair_valid, presence):
     sta_count = lax.axis_size("sta")
     local_events, stations, window = waveforms.shape
-    share = stations // sta_count
     block = sta_count * local_events
+    start = lax.axis_index("evt") * block
     tables = spectral_tables(window, LAGS)
-    direct = sta_count <= 8 and sta_count & (sta_count - 1) == 0
-    traces, me = (exchange if direct else exchange_whole)(waveforms, sta_count)
-
-    start = lax.axis_index("evt") * block
-    offset = pair_events - start
-    inside = (offset >= 0) & (offset < block)
-    flip = me * local_events
-    slot = jnp.where(inside, 0, block) + ((offset % block) ^ flip)
-    first, second = slot[:, 0], slot[:, 1]
-    gained = jnp.where(pair_valid > 0, first, 2 * block)
-    slots = jnp.stack([first, second, gained]).astype(jnp.int32)
-
-    place = jnp.arange(2 * block, dtype=jnp.int32)
-    relative = (place % block) ^ flip
-    relative = jnp.where(
-        place < block, relative, jnp.where(relative < block // 2, relative + block, relative - block)
-    )
-    held = jnp.clip(start + relative, 0, presence.shape[0] - 1)
-    present = presence.astype(jnp.float32)
-    slot_presence = jnp.broadcast_to(
-        jnp.take(present, held, axis=0)[:, :, None], (2 * block, share, LANES)
-    )
-    both = jnp.take(present, pair_events[:, 0], axis=0) * jnp.take(present, pair_events[:, 1], axis=0)
-    counts = jnp.sum(both, axis=1) * pair_valid.astype(jnp.float32)
-
-    correlation, peaks = pair_call(slots, traces, slot_presence, tables)
-    sums = jnp.stack([peaks.reshape(-1), counts])
-    if direct:
-        step = sta_count // 2
-        while step:
-            sums = sums + lax.ppermute(sums, "sta", [(i, i ^ step) for i in range(sta_count)])
-            step //= 2
-    else:
-        sums = lax.psum(sums, "sta")
+    args = (waveforms, pair_events, pair_valid, presence, start, block, tables)
+    dense = sta_count == 8 and presence.shape[0] == LANES and block * block <= pair_events.shape[0]
+    correlation, sums = (banded if dense else by_slot)(*args)
     pair_peak = sums[0] / jnp.maximum(sums[1], 1.0)
-    return correlation.reshape(-1, share, LAGS), pair_peak
+    return correlation, pair_peak.reshape(-1)
 
 
 def solution(mesh):

time: 70.8 us -> 55.5 us (0.78)
  the two profiles are of different devices: /device:TPU:4 before, /device:TPU:0 now
where the time goes in v3:
time: 55.5 us; the launch traced here: 55.1 us
  waiting for transfers between devices  17.1 us (31%)
  starting transfers between devices  16.3 us (29%)
  Pallas kernels  14.3 us (26%)
  local copies, waits for them, and re-layouts  5.83 us (11%)
  between operations  0.78 us (1%)
  other arithmetic  0.76 us (1%)
    ppermute x7, waiting for transfers between devices, exchange(): lax.ppermute(piece, 'sta', [(i, i ^ j) for i in range(sta_count)])  13.1 us
    ppermute x7, starting transfers between devices, exchange(): lax.ppermute(piece, 'sta', [(i, i ^ j) for i in range(sta_count)])  11.3 us
    pallas_call x3, Pallas kernels, pick_call(): pl.pallas_call(functools.partial(pick_kernel, LANES, skip), grid=(steps,)...  6.67 us
    unnamed x12, local copies, waits for them, and re-layouts  4.7 us
    pallas_call x1, Pallas kernels, first_call(): pl.pallas_call(functools.partial(first_kernel, each), out_shape=(jax.Shap...  4.65 us
    ppermute x3, waiting for transfers between devices, banded(): lax.ppermute(sums, 'sta', [(i, i ^ step) for i in range(lax.axis_size('st...  4.03 us
    ppermute x1, starting transfers between devices, exchange(): far_halo = lax.ppermute(far, ('sta', 'evt'), away)  2.62 us
    pallas_call x1, Pallas kernels, last_call(): pl.pallas_call(functools.partial(last_kernel, each), out_shape=(jax.Shape...  2.06 us
  transfers between devices with their start and end apart: 12, of which 9 were waited for; matrix products, arithmetic and copies ran while one was open for 0% of the time, Pallas kernels for 22%

profile of v3, /device:TPU:0, one launch (start us, length us, event | category | flops | bytes accessed | tf_op | source)
XLA Modules:
  0.0 55.1 jit_solution(17671106198614820556)
XLA Ops:
  0.6 0.0 copy-start.5
  0.7 1.1 %dynamic-slice_bitcast_fusion.3 = (bf16[4,8,1024]{2,1,0:T(8,128)(2,1)S(1)}, bf16[4,8,1024]{2,1,0:T(8,128)(2,1)S(1)}, bf16[4,8,1024]{2,1,0:T(8,128)(2,1)S(1)}, bf...) fusion(bf16[4,8,8,1024]{3,2,1,0:T(8,128)(2,1)} %bitcast.35, ...), kind=kLoop, calls=%fused_computation.5 | loop fusion | bytes 1048608 | tf_op jit(solution)/shard_map/jit(dynamic_index_in_dim)/squeeze | solution.py:145
  1.8 4.0 %collective-permute-start.2 = (bf16[4,8,1024]{2,1,0:T(8,128)(2,1)S(1)}, bf16[4,8,1024]{2,1,0:T(8,128)(2,1)S(1)}, u32[]{:S(2)}, u32[]{:S(2)}) collective-permute-start(bf16[4,8,1024]{2,1,0:T(8,128)(2,1)S(1)} %get-tuple-element.42), channel_id=1, source_target_pairs={{0,12},{4,8},{8,4},{12,0},{16,28},{20,24},{24,20},{28,16},{1,13},{... | collective-permute-start | bytes 196616 | tf_op jit(solution)/shard_map/ppermute | solution.py:146
  5.8 0.4 collective-permute-start.1
  6.3 0.2 collective-permute-start
  6.5 1.8 %collective-permute-done.2 = bf16[4,8,1024]{2,1,0:T(8,128)(2,1)S(1)} collective-permute-done((bf16[4,8,1024]{2,1,0:T(8,128)(2,1)S(1)}, bf16[4,8,1024]{2,1,0:T(8,128)(2,1)S(1)}, u32[]{:S(2)}, u32[]{:S(2)}) %collective-permute-start.2) | collective-permute-done | bytes 65568 | tf_op jit(solution)/shard_map/ppermute | solution.py:146
  8.3 1.8 %collective-permute-done.1 = bf16[4,8,1024]{2,1,0:T(8,128)(2,1)S(1)} collective-permute-done((bf16[4,8,1024]{2,1,0:T(8,128)(2,1)S(1)}, bf16[4,8,1024]{2,1,0:T(8,128)(2,1)S(1)}, u32[]{:S(2)}, u32[]{:S(2)}) %collective-permute-start.1) | collective-permute-done | bytes 65568 | tf_op jit(solution)/shard_map/ppermute | solution.py:146
  10.1 0.4 collective-permute-done
  10.6 1.3 %collective-permute-start.8 = (bf16[128,1024]{1,0:T(8,128)(2,1)S(1)}, bf16[128,1024]{1,0:T(8,128)(2,1)S(1)}, u32[]{:S(2)}, u32[]{:S(2)}) collective-permute-start(bf16[128,1024]{1,0:T(8,128)(2,1)S(1)} %maximum_bitcast_fusion.near_ref), channel_id=1, source_target_pairs={{16,17},{20,21},{24,25},{28,29},{1,0},{5,4},{9,8},{13,12},{17,18},... | collective-permute-start | bytes 786440 | tf_op jit(solution)/shard_map/ppermute | solution.py:150
  11.9 2.7 %collective-permute-start.3 = (bf16[4,8,1024]{2,1,0:T(8,128)(2,1)S(1)}, bf16[4,8,1024]{2,1,0:T(8,128)(2,1)S(1)}, u32[]{:S(2)}, u32[]{:S(2)}) collective-permute-start(bf16[4,8,1024]{2,1,0:T(8,128)(2,1)S(1)} %get-tuple-element.38), channel_id=1, source_target_pairs={{0,16},{4,20},{8,24},{12,28},{16,0},{20,4},{24,8},{28,12},{1,17},{... | collective-permute-start | bytes 196616 | tf_op jit(solution)/shard_map/ppermute | solution.py:146
  14.6 1.3 %collective-permute-start.6 = (bf16[4,8,1024]{2,1,0:T(8,128)(2,1)S(1)}, bf16[4,8,1024]{2,1,0:T(8,128)(2,1)S(1)}, u32[]{:S(2)}, u32[]{:S(2)}) collective-permute-start(bf16[4,8,1024]{2,1,0:T(8,128)(2,1)S(1)} %get-tuple-element.39), channel_id=1, source_target_pairs={{0,28},{4,24},{8,20},{12,16},{16,12},{20,8},{24,4},{28,0},{1,29},{... | collective-permute-start | bytes 196616 | tf_op jit(solution)/shard_map/ppermute | solution.py:146
  15.9 2.6 %collective-permute-start.5 = (bf16[4,8,1024]{2,1,0:T(8,128)(2,1)S(1)}, bf16[4,8,1024]{2,1,0:T(8,128)(2,1)S(1)}, u32[]{:S(2)}, u32[]{:S(2)}) collective-permute-start(bf16[4,8,1024]{2,1,0:T(8,128)(2,1)S(1)} %get-tuple-element.40), channel_id=1, source_target_pairs={{0,24},{4,28},{8,16},{12,20},{16,8},{20,12},{24,0},{28,4},{1,25},{... | collective-permute-start | bytes 196616 | tf_op jit(solution)/shard_map/ppermute | solution.py:146
  18.4 0.1 collective-permute-start.4
  18.5 0.1 pad_add_fusion.at_ref
  18.6 0.0 collective-permute-done.3
  18.6 3.0 %collective-permute-done.6 = bf16[4,8,1024]{2,1,0:T(8,128)(2,1)S(1)} collective-permute-done((bf16[4,8,1024]{2,1,0:T(8,128)(2,1)S(1)}, bf16[4,8,1024]{2,1,0:T(8,128)(2,1)S(1)}, u32[]{:S(2)}, u32[]{:S(2)}) %collective-permute-start.6) | collective-permute-done | bytes 65568 | tf_op jit(solution)/shard_map/ppermute | solution.py:146
  21.6 1.0 %collective-permute-done.5 = bf16[4,8,1024]{2,1,0:T(8,128)(2,1)S(1)} collective-permute-done((bf16[4,8,1024]{2,1,0:T(8,128)(2,1)S(1)}, bf16[4,8,1024]{2,1,0:T(8,128)(2,1)S(1)}, u32[]{:S(2)}, u32[]{:S(2)}) %collective-permute-start.5) | collective-permute-done | bytes 65568 | tf_op jit(solution)/shard_map/ppermute | solution.py:146
  22.6 4.9 %collective-permute-done.4 = bf16[4,8,1024]{2,1,0:T(8,128)(2,1)S(1)} collective-permute-done((bf16[4,8,1024]{2,1,0:T(8,128)(2,1)S(1)}, bf16[4,8,1024]{2,1,0:T(8,128)(2,1)S(1)}, u32[]{:S(2)}, u32[]{:S(2)}) %collective-permute-start.4) | collective-permute-done | bytes 65568 | tf_op jit(solution)/shard_map/ppermute | solution.py:146
  27.6 2.6 %collective-permute-start.7 = (bf16[128,1024]{1,0:T(8,128)(2,1)S(1)}, bf16[128,1024]{1,0:T(8,128)(2,1)S(1)}, u32[]{:S(2)}, u32[]{:S(2)}) collective-permute-start(bf16[128,1024]{1,0:T(8,128)(2,1)S(1)} %maximum_bitcast_fusion.1.far_ref), channel_id=1, source_target_pairs={{0,1},{4,5},{8,9},{12,13},{1,2},{5,6},{9,10},{13,14},{17,16},{21,2... | collective-permute-start | bytes 786440 | tf_op jit(solution)/shard_map/ppermute | solution.py:151
  30.2 0.0 copy-start
  30.3 1.6 %copy-done = bf16[1024,1024]{1,0:T(8,128)(2,1)S(1)} copy-done((bf16[1024,1024]{1,0:T(8,128)(2,1)S(1)}, bf16[1024,1024]{1,0:T(8,128)(2,1)}, u32[]{:S(2)}) %copy-start) | copy-done | bytes 2097176
  31.8 0.0 copy-start.1
  31.8 1.0 %copy-done.1 = bf16[1024,256]{1,0:T(8,128)(2,1)S(1)} copy-done((bf16[1024,256]{1,0:T(8,128)(2,1)S(1)}, bf16[1024,256]{1,0:T(8,128)(2,1)}, u32[]{:S(2)}) %copy-start.1) | copy-done | bytes 524312
  32.9 0.0 copy-start.2
  32.9 0.7 %copy-done.2 = s32[1024,2]{0,1:T(2,128)S(1)} copy-done((s32[1024,2]{0,1:T(2,128)S(1)}, s32[1024,2]{0,1:T(2,128)}, u32[]{:S(2)}) %copy-start.2) | copy-done | bytes 8216
  33.6 0.0 copy-start.3
  33.6 0.7 %copy-done.3 = s32[1024]{0:T(1024)S(1)} copy-done((s32[1024]{0:T(1024)S(1)}, s32[1024]{0:T(1024)}, u32[]{:S(2)}) %copy-start.3) | copy-done | bytes 4120
  34.3 0.0 copy-start.4
  34.3 0.7 %copy-done.4 = s32[128,8]{0,1:T(8,128)S(1)} copy-done((s32[128,8]{0,1:T(8,128)S(1)}, s32[128,8]{0,1:T(8,128)}, u32[]{:S(2)}) %copy-start.4) | copy-done | bytes 4120
  35.0 0.9 %shard_map.86 = (s32[8,128]{1,0:T(8,128)S(1)}, f32[8,128]{1,0:T(8,128)S(1)}, f32[64,8,128]{2,1,0:T(8,128)S(1)}, bf16[1024,1024]{1,0:T(8,128)(2,1)S(1)}, bf16[1024,256]{1,0:T(8,128)(2,1)S(1)}) custom-call(s32[2]{0:T(128)S(1)} %pad_add_fusion.at_ref, s32[2,1024]{1,0:T(2,128)S(1)} %bitcast.32, s32[1,1024]{1,0:T(1,128)S(1)} %bitcast.33, s32[8,128]{1,0:T(8,128)S(1)} %bitcast.34, ...), custom_call_target="tpu_custom_call" | custom-call | flops 1000000 | bytes 5000000 | tf_op jit(solution)/shard_map/pallas_call | solution.py:384
  35.9 0.0 collective-permute-done.8.halo_ref
  35.9 0.0 copy-done.5
  35.9 4.7 %shard_map.87 = (f32[32,8,1024]{2,1,0:T(8,128)S(1)}, bf16[1032,8,256]{2,1,0:T(8,128)(2,1)S(1)}, f32[8,1152]{1,0:T(8,128)S(1)}) custom-call(s32[2]{0:T(128)S(1)} %pad_add_fusion.at_ref, bf16[128,1024]{1,0:T(8,128)(2,1)S(1)} %maximum_bitcast_fusion.near_ref, bf16[128,1024]{1,0:T(8,128)(2,1)S(1)} %maximum_bitcast_fusion.1.far_ref, ...), custom_call_target="tpu_custom_call" | custom-call | flops 4563402752 | bytes 8000000 | tf_op jit(solution)/shard_map/pallas_call | solution.py:406
  40.5 0.0 collective-permute-done.7.halo_ref
  40.6 2.1 %shard_map.88 = (bf16[1032,8,256]{2,1,0:T(8,128)(2,1)S(1)}, f32[2,8,128]{2,1,0:T(8,128)S(1)}) custom-call(s32[2]{0:T(128)S(1)} %pad_add_fusion.at_ref, bf16[128,1024]{1,0:T(8,128)(2,1)S(1)} %collective-permute-done.7.halo_ref, f32[32,8,1024]{2,1,0:T(8,128)S(1)} %get-tuple-element.25.own_ref, ...), custom_call_target="tpu_custom_call", output_to_operand_aliasing={{0}: (10, {})} | custom-call | flops 838860800 | bytes 4000000 | tf_op jit(solution)/shard_map/pallas_call | solution.py:429
  42.6 0.0 collective-permute-start.9
  42.6 2.5 %shard_map.89.refs_0_ = bf16[1024,8,256]{2,1,0:T(8,128)(2,1)} custom-call(s32[1024]{0:T(1024)S(1)} %bitcast.29, bf16[1032,8,256]{2,1,0:T(8,128)(2,1)S(1)} %get-tuple-element.31.table_ref), custom_call_target="tpu_custom_call" | custom-call | flops 1000000 | bytes 9000000 | tf_op jit(solution)/shard_map/pallas_call | solution.py:450
  45.1 2.0 %collective-permute-done.9 = f32[2,8,128]{2,1,0:T(8,128)S(1)} collective-permute-done((f32[2,8,128]{2,1,0:T(8,128)S(1)}, f32[2,8,128]{2,1,0:T(8,128)S(1)}, u32[]{:S(2)}, u32[]{:S(2)}) %collective-permute-start.9) | collective-permute-done | bytes 8224 | tf_op jit(solution)/shard_map/ppermute | solution.py:491
  47.2 0.2 collective-permute-start.10
  47.4 2.5 %shard_map.90.refs_0_ = bf16[1024,8,256]{2,1,0:T(8,128)(2,1)} custom-call(s32[1024]{0:T(1024)S(1)} %bitcast.30, bf16[1032,8,256]{2,1,0:T(8,128)(2,1)S(1)} %get-tuple-element.31.table_ref, bf16[1024,8,256]{2,1,0:T(8,128)(2,1)} %shard_map.89.refs_0_), custom_call_target="tpu_custom_call", output_to_operand_aliasing={{}: (2, {})} | custom-call | flops 1000000 | bytes 9000000 | tf_op jit(solution)/shard_map/pallas_call | solution.py:450
  49.8 1.0 %collective-permute-done.10 = f32[2,8,128]{2,1,0:T(8,128)S(1)} collective-permute-done((f32[2,8,128]{2,1,0:T(8,128)S(1)}, f32[2,8,128]{2,1,0:T(8,128)S(1)}, u32[]{:S(2)}, u32[]{:S(2)}) %collective-permute-start.10) | collective-permute-done | bytes 8224 | tf_op jit(solution)/shard_map/ppermute | solution.py:491
  50.8 1.0 %collective-permute-start.11 = (f32[2,8,128]{2,1,0:T(8,128)S(1)}, f32[2,8,128]{2,1,0:T(8,128)S(1)}, u32[]{:S(2)}, u32[]{:S(2)}) collective-permute-start(f32[2,8,128]{2,1,0:T(8,128)S(1)} %add.43), channel_id=1, source_target_pairs={{0,4},{4,0},{8,12},{12,8},{16,20},{20,16},{24,28},{28,24},{1,5},{5... | collective-permute-start | bytes 24584 | tf_op jit(solution)/shard_map/ppermute | solution.py:491
  51.8 1.7 %shard_map.91 = bf16[1024,8,256]{2,1,0:T(8,128)(2,1)} custom-call(s32[1024]{0:T(1024)S(1)} %bitcast.31, bf16[1032,8,256]{2,1,0:T(8,128)(2,1)S(1)} %get-tuple-element.31.table_ref, bf16[1024,8,256]{2,1,0:T(8,128)(2,1)} %shard_map.90.refs_0_), custom_call_target="tpu_custom_call", output_to_operand_aliasing={{}: (2, {})} | custom-call | flops 1000000 | bytes 6000000 | tf_op jit(solution)/shard_map/pallas_call | solution.py:450
  53.5 1.0 %collective-permute-done.11 = f32[2,8,128]{2,1,0:T(8,128)S(1)} collective-permute-done((f32[2,8,128]{2,1,0:T(8,128)S(1)}, f32[2,8,128]{2,1,0:T(8,128)S(1)}, u32[]{:S(2)}, u32[]{:S(2)}) %collective-permute-start.11) | collective-permute-done | bytes 8224 | tf_op jit(solution)/shard_map/ppermute | solution.py:491
  54.5 0.6 %divide_bitcast_fusion = f32[1024]{0:T(1024)} fusion(f32[2,8,128]{2,1,0:T(8,128)S(1)} %add.44), kind=kLoop, calls=%fused_computation.10 | loop fusion | flops 2048 | bytes 12288 | tf_op jit(solution)/shard_map/div | solution.py:534
  (5 shorter events, 0.1 us)
Async XLA Ops:
  0.6 35.2 %copy-start.5 = (f32[1,1024]{1,0:T(1,128)S(1)}, f32[1,1024]{1,0:T(1,128)}, u32[]{:S(2)}) copy-start(f32[1,1024]{1,0:T(1,128)} %constant.55.clone.weights_ref) | copy-start | bytes 12292
  1.8 6.4 %collective-permute-start.2 = (bf16[4,8,1024]{2,1,0:T(8,128)(2,1)S(1)}, bf16[4,8,1024]{2,1,0:T(8,128)(2,1)S(1)}, u32[]{:S(2)}, u32[]{:S(2)}) collective-permute-start(bf16[4,8,1024]{2,1,0:T(8,128)(2,1)S(1)} %get-tuple-element.42), channel_id=1, source_target_pairs={{0,12},{4,8},{8,4},{12,0},{16,28},{20,24},{24,20},{28,16},{1,13},{... | collective-permute-start | bytes 196616 | tf_op jit(solution)/shard_map/ppermute | solution.py:146
  5.8 4.3 %collective-permute-start.1 = (bf16[4,8,1024]{2,1,0:T(8,128)(2,1)S(1)}, bf16[4,8,1024]{2,1,0:T(8,128)(2,1)S(1)}, u32[]{:S(2)}, u32[]{:S(2)}) collective-permute-start(bf16[4,8,1024]{2,1,0:T(8,128)(2,1)S(1)} %get-tuple-element.43), channel_id=1, source_target_pairs={{0,8},{4,12},{8,0},{12,4},{16,24},{20,28},{24,16},{28,20},{1,9},{5... | collective-permute-start | bytes 196616 | tf_op jit(solution)/shard_map/ppermute | solution.py:146
  6.3 4.3 %collective-permute-start = (bf16[4,8,1024]{2,1,0:T(8,128)(2,1)S(1)}, bf16[4,8,1024]{2,1,0:T(8,128)(2,1)S(1)}, u32[]{:S(2)}, u32[]{:S(2)}) collective-permute-start(bf16[4,8,1024]{2,1,0:T(8,128)(2,1)S(1)} %get-tuple-element.44), channel_id=1, source_target_pairs={{0,4},{4,0},{8,12},{12,8},{16,20},{20,16},{24,28},{28,24},{1,5},{5... | collective-permute-start | bytes 196616 | tf_op jit(solution)/shard_map/ppermute | solution.py:146
  10.6 25.3 %collective-permute-start.8 = (bf16[128,1024]{1,0:T(8,128)(2,1)S(1)}, bf16[128,1024]{1,0:T(8,128)(2,1)S(1)}, u32[]{:S(2)}, u32[]{:S(2)}) collective-permute-start(bf16[128,1024]{1,0:T(8,128)(2,1)S(1)} %maximum_bitcast_fusion.near_ref), channel_id=1, source_target_pairs={{16,17},{20,21},{24,25},{28,29},{1,0},{5,4},{9,8},{13,12},{17,18},... | collective-permute-start | bytes 786440 | tf_op jit(solution)/shard_map/ppermute | solution.py:150
  11.9 6.7 %collective-permute-start.3 = (bf16[4,8,1024]{2,1,0:T(8,128)(2,1)S(1)}, bf16[4,8,1024]{2,1,0:T(8,128)(2,1)S(1)}, u32[]{:S(2)}, u32[]{:S(2)}) collective-permute-start(bf16[4,8,1024]{2,1,0:T(8,128)(2,1)S(1)} %get-tuple-element.38), channel_id=1, source_target_pairs={{0,16},{4,20},{8,24},{12,28},{16,0},{20,4},{24,8},{28,12},{1,17},{... | collective-permute-start | bytes 196616 | tf_op jit(solution)/shard_map/ppermute | solution.py:146
  14.6 7.1 %collective-permute-start.6 = (bf16[4,8,1024]{2,1,0:T(8,128)(2,1)S(1)}, bf16[4,8,1024]{2,1,0:T(8,128)(2,1)S(1)}, u32[]{:S(2)}, u32[]{:S(2)}) collective-permute-start(bf16[4,8,1024]{2,1,0:T(8,128)(2,1)S(1)} %get-tuple-element.39), channel_id=1, source_target_pairs={{0,28},{4,24},{8,20},{12,16},{16,12},{20,8},{24,4},{28,0},{1,29},{... | collective-permute-start | bytes 196616 | tf_op jit(solution)/shard_map/ppermute | solution.py:146
  15.9 6.8 %collective-permute-start.5 = (bf16[4,8,1024]{2,1,0:T(8,128)(2,1)S(1)}, bf16[4,8,1024]{2,1,0:T(8,128)(2,1)S(1)}, u32[]{:S(2)}, u32[]{:S(2)}) collective-permute-start(bf16[4,8,1024]{2,1,0:T(8,128)(2,1)S(1)} %get-tuple-element.40), channel_id=1, source_target_pairs={{0,24},{4,28},{8,16},{12,20},{16,8},{20,12},{24,0},{28,4},{1,25},{... | collective-permute-start | bytes 196616 | tf_op jit(solution)/shard_map/ppermute | solution.py:146
  18.4 9.2 %collective-permute-start.4 = (bf16[4,8,1024]{2,1,0:T(8,128)(2,1)S(1)}, bf16[4,8,1024]{2,1,0:T(8,128)(2,1)S(1)}, u32[]{:S(2)}, u32[]{:S(2)}) collective-permute-start(bf16[4,8,1024]{2,1,0:T(8,128)(2,1)S(1)} %get-tuple-element.41), channel_id=1, source_target_pairs={{0,20},{4,16},{8,28},{12,24},{16,4},{20,0},{24,12},{28,8},{1,21},{... | collective-permute-start | bytes 196616 | tf_op jit(solution)/shard_map/ppermute | solution.py:146
  27.6 12.9 %collective-permute-start.7 = (bf16[128,1024]{1,0:T(8,128)(2,1)S(1)}, bf16[128,1024]{1,0:T(8,128)(2,1)S(1)}, u32[]{:S(2)}, u32[]{:S(2)}) collective-permute-start(bf16[128,1024]{1,0:T(8,128)(2,1)S(1)} %maximum_bitcast_fusion.1.far_ref), channel_id=1, source_target_pairs={{0,1},{4,5},{8,9},{12,13},{1,2},{5,6},{9,10},{13,14},{17,16},{21,2... | collective-permute-start | bytes 786440 | tf_op jit(solution)/shard_map/ppermute | solution.py:151
  30.2 1.6 %copy-start = (bf16[1024,1024]{1,0:T(8,128)(2,1)S(1)}, bf16[1024,1024]{1,0:T(8,128)(2,1)}, u32[]{:S(2)}) copy-start(bf16[1024,1024]{1,0:T(8,128)(2,1)} %constant.53.clone.forward_ref) | copy-start | bytes 6291460
  31.8 1.0 %copy-start.1 = (bf16[1024,256]{1,0:T(8,128)(2,1)S(1)}, bf16[1024,256]{1,0:T(8,128)(2,1)}, u32[]{:S(2)}) copy-start(bf16[1024,256]{1,0:T(8,128)(2,1)} %constant.54.clone.inverse_ref) | copy-start | bytes 1572868
  32.9 0.7 %copy-start.2 = (s32[1024,2]{0,1:T(2,128)S(1)}, s32[1024,2]{0,1:T(2,128)}, u32[]{:S(2)}) copy-start(s32[1024,2]{0,1:T(2,128)} %param.8) | copy-start | bytes 24580
  33.6 0.7 %copy-start.3 = (s32[1024]{0:T(1024)S(1)}, s32[1024]{0:T(1024)}, u32[]{:S(2)}) copy-start(s32[1024]{0:T(1024)} %param.9) | copy-start | bytes 12292
  34.3 0.7 %copy-start.4 = (s32[128,8]{0,1:T(8,128)S(1)}, s32[128,8]{0,1:T(8,128)}, u32[]{:S(2)}) copy-start(s32[128,8]{0,1:T(8,128)} %param.10) | copy-start | bytes 12292
  42.6 4.6 %collective-permute-start.9 = (f32[2,8,128]{2,1,0:T(8,128)S(1)}, f32[2,8,128]{2,1,0:T(8,128)S(1)}, u32[]{:S(2)}, u32[]{:S(2)}) collective-permute-start(f32[2,8,128]{2,1,0:T(8,128)S(1)} %get-tuple-element.30), channel_id=1, source_target_pairs={{0,16},{4,20},{8,24},{12,28},{16,0},{20,4},{24,8},{28,12},{1,17},{... | collective-permute-start | bytes 24584 | tf_op jit(solution)/shard_map/ppermute | solution.py:491
  47.2 3.7 %collective-permute-start.10 = (f32[2,8,128]{2,1,0:T(8,128)S(1)}, f32[2,8,128]{2,1,0:T(8,128)S(1)}, u32[]{:S(2)}, u32[]{:S(2)}) collective-permute-start(f32[2,8,128]{2,1,0:T(8,128)S(1)} %add.42), channel_id=1, source_target_pairs={{0,8},{4,12},{8,0},{12,4},{16,24},{20,28},{24,16},{28,20},{1,9},{5... | collective-permute-start | bytes 24584 | tf_op jit(solution)/shard_map/ppermute | solution.py:491
  50.8 3.7 %collective-permute-start.11 = (f32[2,8,128]{2,1,0:T(8,128)S(1)}, f32[2,8,128]{2,1,0:T(8,128)S(1)}, u32[]{:S(2)}, u32[]{:S(2)}) collective-permute-start(f32[2,8,128]{2,1,0:T(8,128)S(1)} %add.43), channel_id=1, source_target_pairs={{0,4},{4,0},{8,12},{12,8},{16,20},{20,16},{24,28},{28,24},{1,5},{5... | collective-permute-start | bytes 24584 | tf_op jit(solution)/shard_map/ppermute | solution.py:491

commit v4 on v3

--- a/solution.py
+++ b/solution.py
@@ -147,9 +147,7 @@
     rows = half * events * share
     near = jnp.concatenate(pieces[:half], axis=0).reshape(rows, window)
     far = jnp.concatenate(pieces[half:], axis=0).reshape(rows, window)
-    near_halo = lax.ppermute(near, ("sta", "evt"), toward)
-    far_halo = lax.ppermute(far, ("sta", "evt"), away)
-    return (near, far, near_halo, far_halo), me
+    return near, far, toward, away
 
 
 def exchange_whole(waveforms):
@@ -231,28 +229,33 @@
 
 
 def prepare_kernel(
-    each, block, at_ref, events_ref, valid_ref, presence_ref, forward_ref, inverse_ref,
-    row_ref, count_ref, held_ref, forward_out, inverse_out, sems,
+    each, block, events_ref, valid_ref, presence_ref, forward_ref, inverse_ref,
+    row_ref, count_ref, held_ref, forward_out, inverse_out, events_in, valid_in, presence_in, sems,
 ):
     copies = [
-        pltpu.make_async_copy(forward_ref, forward_out, sems.at[0]),
-        pltpu.make_async_copy(inverse_ref, inverse_out, sems.at[1]),
+        pltpu.make_async_copy(events_ref, events_in, sems.at[0]),
+        pltpu.make_async_copy(valid_ref, valid_in, sems.at[1]),
+        pltpu.make_async_copy(presence_ref, presence_in, sems.at[2]),
+        pltpu.make_async_copy(forward_ref, forward_out, sems.at[3]),
+        pltpu.make_async_copy(inverse_ref, inverse_out, sems.at[4]),
     ]
     for copy in copies:
         copy.start()
-    me, start = at_ref[0], at_ref[1]
+    me, start = lax.axis_index("sta"), lax.axis_index("evt") * block
+    for copy in copies[:3]:
+        copy.wait()
     lines = row_ref.shape[0]
 
     def stacked(ref, line):
         return jnp.concatenate([ref[line:line + 1, i * LANES:(i + 1) * LANES] for i in range(lines)], axis=0)
 
-    first, second, valid = stacked(events_ref, 0), stacked(events_ref, 1), stacked(valid_ref, 0)
+    first, second, valid = stacked(events_in, 0), stacked(events_in, 1), stacked(valid_in, 0)
     rows = Rows(block)
     row = table_row(first - start, second - start, me, each, block, rows)
     row = jnp.where(valid > 0, row, rows.zero)
     row_ref[...] = jnp.clip(row, 0, rows.end - 1)
 
-    presence = presence_ref[...]
+    presence = presence_in[...]
     stations, events = presence.shape
     bits = jnp.zeros((1, events), jnp.int32)
     for s in range(stations):
@@ -269,7 +272,7 @@
     for i in range(held_ref.shape[0]):
         mine = jnp.where(lane == start - block // 2 + i, present, 0.0)
         held_ref[i] = jnp.broadcast_to(jnp.sum(mine, axis=1, keepdims=True), (stations, LANES))
-    for copy in copies:
+    for copy in copies[3:]:
         copy.wait()
 
 
@@ -309,37 +312,50 @@
         keep(table_ref, peaks, lagged, row + low)
 
 
-def first_kernel(
-    each, at_ref, near_ref, far_ref, halo_ref, presence_ref, forward_ref, inverse_ref, weights_ref,
-    spec_ref, table_ref, peak_ref, other_ref, lhs_ref,
+def own_kernel(
+    each, near_ref, far_ref, presence_ref, forward_ref, inverse_ref, weights_ref,
+    spec_ref, table_ref, peak_ref, lhs_ref,
 ):
     block, stations, window = spec_ref.shape
     band = block // 2
-    me = at_ref[0]
-    low_half = me * each < band
-    mine = jnp.where(low_half, 0, band)
+    me = lax.axis_index("sta")
+    mine = jnp.where(me * each < band, 0, band)
     for ref, place in ((near_ref, mine), (far_ref, band - mine)):
         scaled_spectra(
             ref, me, each, place, presence_ref, band + place, forward_ref, weights_ref, spec_ref
         )
-    edge = jnp.where(low_half, 3 * band, 0)
+    rows = Rows(block)
+    peaks = no_peaks(rows, stations)
+    own_pairs(spec_ref, inverse_ref, table_ref, peaks, lhs_ref)
+    table_ref[rows.zero] = jnp.zeros(table_ref.shape[1:], table_ref.dtype)
+    peak_ref[...] = jnp.concatenate(peaks, axis=1)
+
+
+def near_kernel(
+    each, halo_ref, own_ref, presence_ref, forward_ref, inverse_ref, weights_ref, own_peak_ref,
+    held_table_ref, table_ref, peak_ref, other_ref, lhs_ref,
+):
+    del held_table_ref
+    block, stations, window = own_ref.shape
+    band = block // 2
+    me = lax.axis_index("sta")
+    high = me * each < band
+    edge = jnp.where(high, 3 * band, 0)
     scaled_spectra(halo_ref, me, each, 0, presence_ref, edge, forward_ref, weights_ref, other_ref)
     rows = Rows(block)
     peaks = no_peaks(rows, stations)
-    own_pairs(spec_ref, inverse_ref, table_ref, peaks, lhs_ref)
-    halo_pairs(low_half, spec_ref, other_ref, inverse_ref, table_ref, peaks, lhs_ref, rows.near)
-    table_ref[rows.zero] = jnp.zeros(table_ref.shape[1:], table_ref.dtype)
-    peak_ref[...] = jnp.concatenate(peaks, axis=1)
+    halo_pairs(high, own_ref, other_ref, inverse_ref, table_ref, peaks, lhs_ref, rows.near)
+    peak_ref[...] = own_peak_ref[...] + jnp.concatenate(peaks, axis=1)
 
 
 def last_kernel(
-    each, at_ref, halo_ref, own_ref, presence_ref, forward_ref, inverse_ref, weights_ref, peak_ref, row_ref, count_ref,
+    each, halo_ref, own_ref, presence_ref, forward_ref, inverse_ref, weights_ref, peak_ref, row_ref, count_ref,
     held_table_ref, table_ref, sums_ref, other_ref, lhs_ref,
 ):
     del held_table_ref
     block, stations, window = own_ref.shape
     band = block // 2
-    me = at_ref[0]
+    me = lax.axis_index("sta")
     high = me * each >= band
     edge = jnp.where(high, 3 * band, 0)
     scaled_spectra(halo_ref, me, each, 0, presence_ref, edge, forward_ref, weights_ref, other_ref)
@@ -375,12 +391,12 @@
     )
 
 
-def prepare_call(at, pair_events, pair_valid, presence, tables, each, block):
+def prepare_call(pair_events, pair_valid, presence, tables, each, block):
     forward, inverse = tables[:2]
     pairs = pair_events.shape[0]
     stations = presence.shape[1]
     line = (pairs // LANES, LANES)
-    anywhere = pl.BlockSpec(memory_space=pl.ANY)
+    anywhere = pl.BlockSpec(memory_space=pltpu.HBM)
     return pl.pallas_call(
         functools.partial(prepare_kernel, each, block),
         out_shape=(
@@ -390,38 +406,63 @@
             jax.ShapeDtypeStruct(forward.shape, forward.dtype),
             jax.ShapeDtypeStruct(inverse.shape, inverse.dtype),
         ),
-        in_specs=[SMEM] + [VMEM] * 3 + [anywhere] * 2,
+        in_specs=[anywhere] * 5,
         out_specs=(VMEM,) * 5,
-        scratch_shapes=[pltpu.SemaphoreType.DMA((2,))],
+        scratch_shapes=[
+            pltpu.VMEM((2, pairs), jnp.int32),
+            pltpu.VMEM((1, pairs), jnp.int32),
+            pltpu.VMEM(presence.shape[::-1], jnp.int32),
+            pltpu.SemaphoreType.DMA((5,)),
+        ],
         compiler_params=PARAMS,
         cost_estimate=pl.CostEstimate(flops=1_000_000, bytes_accessed=5_000_000, transcendentals=0),
-    )(at, pair_events.T, pair_valid.reshape(1, pairs), presence.T, forward, inverse)
-
-
-def first_call(at, near, far, halo, presence, tables, each, block):
+    )(pair_events.T, pair_valid.reshape(1, pairs), presence.T, forward, inverse)
+
+
+def own_call(near, far, presence, tables, each, block):
     forward, inverse, weights = tables
     window, lags = inverse.shape
     stations = presence.shape[1]
     rows = Rows(block)
     return pl.pallas_call(
-        functools.partial(first_kernel, each),
+        functools.partial(own_kernel, each),
         out_shape=(
             jax.ShapeDtypeStruct((block, stations, window), jnp.float32),
             jax.ShapeDtypeStruct((rows.end, stations, lags), jnp.bfloat16),
             jax.ShapeDtypeStruct((stations, rows.lanes), jnp.float32),
         ),
-        in_specs=[SMEM] + [VMEM] * 7,
+        in_specs=[VMEM] * 6,
         out_specs=(VMEM,) * 3,
+        scratch_shapes=[pltpu.VMEM((rows.own * stations, window), jnp.bfloat16)],
+        compiler_params=PARAMS,
+        cost_estimate=cost(rows.own * stations, lags, window, near.shape[0] * 2, 8_000_000),
+    )(near, far, presence, forward, inverse, weights)
+
+
+def near_call(halo, own, presence, tables, peaks, table, each):
+    forward, inverse, weights = tables
+    window, lags = inverse.shape
+    block, stations = own.shape[:2]
+    pairs = triangle(block // 2)
+    return pl.pallas_call(
+        functools.partial(near_kernel, each),
+        out_shape=(
+            jax.ShapeDtypeStruct(table.shape, table.dtype),
+            jax.ShapeDtypeStruct(peaks.shape, peaks.dtype),
+        ),
+        in_specs=[VMEM] * 8,
+        out_specs=(VMEM,) * 2,
         scratch_shapes=[
             pltpu.VMEM((block // 2, stations, window), jnp.float32),
-            pltpu.VMEM((rows.own * stations, window), jnp.bfloat16),
+            pltpu.VMEM((pairs * stations, window), jnp.bfloat16),
         ],
+        input_output_aliases={7: 0},
         compiler_params=PARAMS,
-        cost_estimate=cost(rows.far * stations, lags, window, near.shape[0] * 3, 8_000_000),
-    )(at, near, far, halo, presence, forward, inverse, weights)
-
-
-def last_call(at, halo, own, presence, tables, peaks, row, count, table, each):
+        cost_estimate=cost(pairs * stations, lags, window, halo.shape[0], 4_000_000),
+    )(halo, own, presence, forward, inverse, weights, peaks, table)
+
+
+def last_call(halo, own, presence, tables, peaks, row, count, table, each):
     forward, inverse, weights = tables
     window, lags = inverse.shape
     block, stations = own.shape[:2]
@@ -432,16 +473,16 @@
             jax.ShapeDtypeStruct(table.shape, table.dtype),
             jax.ShapeDtypeStruct((2,) + row.shape, jnp.float32),
         ),
-        in_specs=[SMEM] + [VMEM] * 10,
+        in_specs=[VMEM] * 10,
         out_specs=(VMEM,) * 2,
         scratch_shapes=[
             pltpu.VMEM((block // 2, stations, window), jnp.float32),
             pltpu.VMEM((pairs * stations, window), jnp.bfloat16),
         ],
-        input_output_aliases={10: 0},
+        input_output_aliases={9: 0},
         compiler_params=PARAMS,
         cost_estimate=cost(pairs * stations, lags, window, halo.shape[0], 4_000_000),
-    )(at, halo, own, presence, forward, inverse, weights, peaks, row, count, table)
+    )(halo, own, presence, forward, inverse, weights, peaks, row, count, table)
 
 
 def pick_call(row, table, held, skip, steps):
@@ -473,15 +514,18 @@
     return jnp.where(high | (second < 0), outside, inside)
 
 
-def banded(waveforms, pair_events, pair_valid, presence, start, block, tables):
+def banded(waveforms, pair_events, pair_valid, presence, block, tables):
     each = waveforms.shape[0]
-    (near, far, near_halo, far_halo), me = exchange(waveforms, lax.axis_size("sta"))
-    at = jnp.stack([me, start]).astype(jnp.int32)
-    near, at = lax.optimization_barrier((near, at))
-    row, count, held, forward, inverse = prepare_call(at, pair_events, pair_valid, presence, tables, each, block)
+    near, far, toward, away = exchange(waveforms, lax.axis_size("sta"))
+    ready = prepare_call(pair_events, pair_valid, presence, tables, each, block)
+    far, ready = lax.optimization_barrier((far, ready))
+    near_halo = lax.ppermute(near, ("sta", "evt"), toward)
+    far_halo = lax.ppermute(far, ("sta", "evt"), away)
+    row, count, held, forward, inverse = ready
     tables = (forward, inverse, tables[2])
-    own, table, peaks = first_call(at, near, far, near_halo, held, tables, each, block)
-    table, sums = last_call(at, far_halo, own, held, tables, peaks, row, count, table, each)
+    own, table, peaks = own_call(near, far, held, tables, each, block)
+    table, peaks = near_call(near_halo, own, held, tables, peaks, table, each)
+    table, sums = last_call(far_halo, own, held, tables, peaks, row, count, table, each)
 
     row = row.reshape(-1)
     groups = row.shape[0] // LANES
@@ -497,8 +541,9 @@
     return correlation[0], sums
 
 
-def by_slot(waveforms, pair_events, pair_valid, presence, start, block, tables):
+def by_slot(waveforms, pair_events, pair_valid, presence, block, tables):
     share = presence.shape[1]
+    start = lax.axis_index("evt") * block
     traces = exchange_whole(waveforms)
     place = pair_events - start
     slot = jnp.where((place >= 0) & (place < block), 0, block) + place % block
@@ -526,9 +571,8 @@
     sta_count = lax.axis_size("sta")
     local_events, stations, window = waveforms.shape
     block = sta_count * local_events
-    start = lax.axis_index("evt") * block
     tables = spectral_tables(window, LAGS)
-    args = (waveforms, pair_events, pair_valid, presence, start, block, tables)
+    args = (waveforms, pair_events, pair_valid, presence, block, tables)
     dense = sta_count == 8 and presence.shape[0] == LANES and block * block <= pair_events.shape[0]
     correlation, sums = (banded if dense else by_slot)(*args)
     pair_peak = sums[0] / jnp.maximum(sums[1], 1.0)

time: 55.5 us -> 45.6 us (0.82)
  the two profiles are of different devices: /device:TPU:0 before, /device:TPU:4 now
where the time goes in v4:
time: 45.6 us; the launch traced here: 45.2 us
  starting transfers between devices  18.7 us (41%)
  Pallas kernels  13.3 us (29%)
  waiting for transfers between devices  5.94 us (13%)
  local copies, waits for them, and re-layouts  5.82 us (13%)
  between operations  0.79 us (2%)
  other arithmetic  0.68 us (1%)
    ppermute x7, starting transfers between devices, exchange(): lax.ppermute(piece, 'sta', [(i, i ^ j) for i in range(sta_count)])  11.3 us
    pallas_call x3, Pallas kernels, pick_call(): pl.pallas_call(functools.partial(pick_kernel, LANES, skip), grid=(steps,)...  6.67 us
    unnamed x12, local copies, waits for them, and re-layouts  4.71 us
    ppermute x3, starting transfers between devices, banded(): lax.ppermute(sums, 'sta', [(i, i ^ step) for i in range(lax.axis_size('st...  3.57 us
    pallas_call x1, Pallas kernels, own_call(): pl.pallas_call(functools.partial(own_kernel, each), out_shape=(jax.ShapeD...  3.23 us
    ppermute x3, waiting for transfers between devices, banded(): lax.ppermute(sums, 'sta', [(i, i ^ step) for i in range(lax.axis_size('st...  2.5 us
    ppermute x7, waiting for transfers between devices, exchange(): lax.ppermute(piece, 'sta', [(i, i ^ j) for i in range(sta_count)])  2.37 us
    ppermute x1, starting transfers between devices, banded(): near_halo = lax.ppermute(near, ('sta', 'evt'), toward)  1.92 us
  transfers between devices with their start and end apart: 12, of which 4 were waited for; matrix products, arithmetic and copies ran while one was open for 0% of the time, Pallas kernels for 26%

profile of v4, /device:TPU:4, one launch (start us, length us, event | category | flops | bytes accessed | tf_op | source)
XLA Modules:
  0.0 45.2 jit_solution(17054661583386390809)
XLA Ops:
  0.6 0.0 copy-start.2
  0.7 1.1 %dynamic-slice_bitcast_fusion.3 = (bf16[4,8,1024]{2,1,0:T(8,128)(2,1)S(1)}, bf16[4,8,1024]{2,1,0:T(8,128)(2,1)S(1)}, bf16[4,8,1024]{2,1,0:T(8,128)(2,1)S(1)}, bf...) fusion(bf16[4,8,8,1024]{3,2,1,0:T(8,128)(2,1)} %bitcast.33, ...), kind=kLoop, calls=%fused_computation.5 | loop fusion | bytes 1048608 | tf_op jit(solution)/shard_map/jit(dynamic_index_in_dim)/squeeze | solution.py:143
  1.8 2.6 %collective-permute-start.7 = (bf16[4,8,1024]{2,1,0:T(8,128)(2,1)S(1)}, bf16[4,8,1024]{2,1,0:T(8,128)(2,1)S(1)}, u32[]{:S(2)}, u32[]{:S(2)}) collective-permute-start(bf16[4,8,1024]{2,1,0:T(8,128)(2,1)S(1)} %get-tuple-element.51), channel_id=1, source_target_pairs={{0,12},{4,8},{8,4},{12,0},{16,28},{20,24},{24,20},{28,16},{1,13},{... | collective-permute-start | bytes 196616 | tf_op jit(solution)/shard_map/ppermute | solution.py:146
  4.4 0.4 collective-permute-start.6
  4.8 0.5 %collective-permute-start.5 = (bf16[4,8,1024]{2,1,0:T(8,128)(2,1)S(1)}, bf16[4,8,1024]{2,1,0:T(8,128)(2,1)S(1)}, u32[]{:S(2)}, u32[]{:S(2)}) collective-permute-start(bf16[4,8,1024]{2,1,0:T(8,128)(2,1)S(1)} %get-tuple-element.53), channel_id=1, source_target_pairs={{0,4},{4,0},{8,12},{12,8},{16,20},{20,16},{24,28},{28,24},{1,5},{5... | collective-permute-start | bytes 196616 | tf_op jit(solution)/shard_map/ppermute | solution.py:146
  5.4 4.5 %collective-permute-start.3 = (bf16[4,8,1024]{2,1,0:T(8,128)(2,1)S(1)}, bf16[4,8,1024]{2,1,0:T(8,128)(2,1)S(1)}, u32[]{:S(2)}, u32[]{:S(2)}) collective-permute-start(bf16[4,8,1024]{2,1,0:T(8,128)(2,1)S(1)} %get-tuple-element.54), channel_id=1, source_target_pairs={{0,28},{4,24},{8,20},{12,16},{16,12},{20,8},{24,4},{28,0},{1,29},{... | collective-permute-start | bytes 196616 | tf_op jit(solution)/shard_map/ppermute | solution.py:146
  9.9 0.2 collective-permute-start.2
  10.1 0.0 copy-start
  10.1 1.6 %copy-done = bf16[1024,1024]{1,0:T(8,128)(2,1)S(1)} copy-done((bf16[1024,1024]{1,0:T(8,128)(2,1)S(1)}, bf16[1024,1024]{1,0:T(8,128)(2,1)}, u32[]{:S(2)}) %copy-start) | copy-done | bytes 2097176
  11.7 0.0 copy-start.1
  11.7 1.0 %copy-done.1 = bf16[1024,256]{1,0:T(8,128)(2,1)S(1)} copy-done((bf16[1024,256]{1,0:T(8,128)(2,1)S(1)}, bf16[1024,256]{1,0:T(8,128)(2,1)}, u32[]{:S(2)}) %copy-start.1) | copy-done | bytes 524312
  12.7 0.0 copy-start.3
  12.7 0.7 %copy-done.3 = s32[1024,2]{0,1:T(2,128)S(1)} copy-done((s32[1024,2]{0,1:T(2,128)S(1)}, s32[1024,2]{0,1:T(2,128)}, u32[]{:S(2)}) %copy-start.3) | copy-done | bytes 8216
  13.4 0.0 copy-start.4
  13.4 0.7 %copy-done.4 = s32[1024]{0:T(1024)S(1)} copy-done((s32[1024]{0:T(1024)S(1)}, s32[1024]{0:T(1024)}, u32[]{:S(2)}) %copy-start.4) | copy-done | bytes 4120
  14.1 0.0 copy-start.5
  14.1 0.7 %copy-done.5 = s32[128,8]{0,1:T(8,128)S(1)} copy-done((s32[128,8]{0,1:T(8,128)S(1)}, s32[128,8]{0,1:T(8,128)}, u32[]{:S(2)}) %copy-start.5) | copy-done | bytes 4120
  14.8 0.4 shard_map.86
  15.2 0.0 collective-permute-done.7
  15.2 0.8 %collective-permute-start.1 = (bf16[4,8,1024]{2,1,0:T(8,128)(2,1)S(1)}, bf16[4,8,1024]{2,1,0:T(8,128)(2,1)S(1)}, u32[]{:S(2)}, u32[]{:S(2)}) collective-permute-start(bf16[4,8,1024]{2,1,0:T(8,128)(2,1)S(1)} %get-tuple-element.56), channel_id=1, source_target_pairs={{0,20},{4,16},{8,28},{12,24},{16,4},{20,0},{24,12},{28,8},{1,21},{... | collective-permute-start | bytes 196616 | tf_op jit(solution)/shard_map/ppermute | solution.py:146
  16.1 0.0 collective-permute-done.6
  16.1 2.1 %collective-permute-start = (bf16[4,8,1024]{2,1,0:T(8,128)(2,1)S(1)}, bf16[4,8,1024]{2,1,0:T(8,128)(2,1)S(1)}, u32[]{:S(2)}, u32[]{:S(2)}) collective-permute-start(bf16[4,8,1024]{2,1,0:T(8,128)(2,1)S(1)} %get-tuple-element.57), channel_id=1, source_target_pairs={{0,16},{4,20},{8,24},{12,28},{16,0},{20,4},{24,8},{28,12},{1,17},{... | collective-permute-start | bytes 196616 | tf_op jit(solution)/shard_map/ppermute | solution.py:146
  18.2 0.0 collective-permute-done.5
  18.2 1.9 %collective-permute-start.8 = (bf16[128,1024]{1,0:T(8,128)(2,1)S(1)}, bf16[128,1024]{1,0:T(8,128)(2,1)S(1)}, u32[]{:S(2)}, u32[]{:S(2)}) collective-permute-start(bf16[128,1024]{1,0:T(8,128)(2,1)S(1)} %maximum_bitcast_fusion.1.near_ref), channel_id=1, source_target_pairs={{16,17},{20,21},{24,25},{28,29},{1,0},{5,4},{9,8},{13,12},{17,18},... | collective-permute-start | bytes 786440 | tf_op jit(solution)/shard_map/ppermute | solution.py:522
  20.2 0.0 collective-permute-done.3
  20.2 0.0 collective-permute-done.2
  20.2 2.3 %collective-permute-done.1 = bf16[4,8,1024]{2,1,0:T(8,128)(2,1)S(1)} collective-permute-done((bf16[4,8,1024]{2,1,0:T(8,128)(2,1)S(1)}, bf16[4,8,1024]{2,1,0:T(8,128)(2,1)S(1)}, u32[]{:S(2)}, u32[]{:S(2)}) %collective-permute-start.1) | collective-permute-done | bytes 65568 | tf_op jit(solution)/shard_map/ppermute | solution.py:146
  22.5 0.0 collective-permute-done
  22.6 1.9 %collective-permute-start.4 = (bf16[128,1024]{1,0:T(8,128)(2,1)S(1)}, bf16[128,1024]{1,0:T(8,128)(2,1)S(1)}, u32[]{:S(2)}, u32[]{:S(2)}) collective-permute-start(bf16[128,1024]{1,0:T(8,128)(2,1)S(1)} %maximum_bitcast_fusion.far_ref), channel_id=1, source_target_pairs={{0,1},{4,5},{8,9},{12,13},{1,2},{5,6},{9,10},{13,14},{17,16},{21,2... | collective-permute-start | bytes 786440 | tf_op jit(solution)/shard_map/ppermute | solution.py:523
  24.5 0.0 copy-done.2
  24.5 3.2 %shard_map.87 = (f32[32,8,1024]{2,1,0:T(8,128)S(1)}, bf16[1032,8,256]{2,1,0:T(8,128)(2,1)S(1)}, f32[8,1152]{1,0:T(8,128)S(1)}) custom-call(bf16[128,1024]{1,0:T(8,128)(2,1)S(1)} %maximum_bitcast_fusion.1.near_ref, bf16[128,1024]{1,0:T(8,128)(2,1)S(1)} %maximum_bitcast_fusion.far_ref, f32[64,8,128]{2,1,0:T(8,128)S(1)} %get-tuple-element.32.presence_ref, ...), custom_call_target="tpu_custom_call" | custom-call | flops 2113929216 | bytes 8000000 | tf_op jit(solution)/shard_map/pallas_call | solution.py:427
  27.8 0.0 collective-permute-done.8.halo_ref
  27.8 1.4 %shard_map.88 = (bf16[1032,8,256]{2,1,0:T(8,128)(2,1)S(1)}, f32[8,1152]{1,0:T(8,128)S(1)}) custom-call(bf16[128,1024]{1,0:T(8,128)(2,1)S(1)} %collective-permute-done.8.halo_ref, f32[32,8,1024]{2,1,0:T(8,128)S(1)} %get-tuple-element.35.own_ref, f32[64,8,128]{2,1,0:T(8,128)S(1)} %get-tuple-element.32.presence_ref, ...), custom_call_target="tpu_custom_call", output_to_operand_aliasing={{0}: (7, {})} | custom-call | flops 838860800 | bytes 4000000 | tf_op jit(solution)/shard_map/pallas_call | solution.py:447
  29.2 1.1 %collective-permute-done.4.halo_ref = bf16[128,1024]{1,0:T(8,128)(2,1)S(1)} collective-permute-done((bf16[128,1024]{1,0:T(8,128)(2,1)S(1)}, bf16[128,1024]{1,0:T(8,128)(2,1)S(1)}, u32[]{:S(2)}, u32[]{:S(2)}) %collective-permute-start.4) | collective-permute-done | bytes 262176 | tf_op jit(solution)/shard_map/ppermute | solution.py:523
  30.3 1.5 %shard_map.89 = (bf16[1032,8,256]{2,1,0:T(8,128)(2,1)S(1)}, f32[2,8,128]{2,1,0:T(8,128)S(1)}) custom-call(bf16[128,1024]{1,0:T(8,128)(2,1)S(1)} %collective-permute-done.4.halo_ref, f32[32,8,1024]{2,1,0:T(8,128)S(1)} %get-tuple-element.35.own_ref, f32[64,8,128]{2,1,0:T(8,128)S(1)} %get-tuple-element.32.presence_ref, ...), custom_call_target="tpu_custom_call", output_to_operand_aliasing={{0}: (9, {})} | custom-call | flops 838860800 | bytes 4000000 | tf_op jit(solution)/shard_map/pallas_call | solution.py:470
  31.8 0.0 collective-permute-start.9
  31.8 2.5 %shard_map.90.refs_0_ = bf16[1024,8,256]{2,1,0:T(8,128)(2,1)} custom-call(s32[1024]{0:T(1024)S(1)} %bitcast.27, bf16[1032,8,256]{2,1,0:T(8,128)(2,1)S(1)} %get-tuple-element.43.table_ref), custom_call_target="tpu_custom_call" | custom-call | flops 1000000 | bytes 9000000 | tf_op jit(solution)/shard_map/pallas_call | solution.py:491
  34.3 2.0 %collective-permute-done.9 = f32[2,8,128]{2,1,0:T(8,128)S(1)} collective-permute-done((f32[2,8,128]{2,1,0:T(8,128)S(1)}, f32[2,8,128]{2,1,0:T(8,128)S(1)}, u32[]{:S(2)}, u32[]{:S(2)}) %collective-permute-start.9) | collective-permute-done | bytes 8224 | tf_op jit(solution)/shard_map/ppermute | solution.py:535
  36.4 2.1 %collective-permute-start.10 = (f32[2,8,128]{2,1,0:T(8,128)S(1)}, f32[2,8,128]{2,1,0:T(8,128)S(1)}, u32[]{:S(2)}, u32[]{:S(2)}) collective-permute-start(f32[2,8,128]{2,1,0:T(8,128)S(1)} %add.42), channel_id=1, source_target_pairs={{0,8},{4,12},{8,0},{12,4},{16,24},{20,28},{24,16},{28,20},{1,9},{5... | collective-permute-start | bytes 24584 | tf_op jit(solution)/shard_map/ppermute | solution.py:535
  38.4 2.5 %shard_map.91.refs_0_ = bf16[1024,8,256]{2,1,0:T(8,128)(2,1)} custom-call(s32[1024]{0:T(1024)S(1)} %bitcast.28, bf16[1032,8,256]{2,1,0:T(8,128)(2,1)S(1)} %get-tuple-element.43.table_ref, bf16[1024,8,256]{2,1,0:T(8,128)(2,1)} %shard_map.90.refs_0_), custom_call_target="tpu_custom_call", output_to_operand_aliasing={{}: (2, {})} | custom-call | flops 1000000 | bytes 9000000 | tf_op jit(solution)/shard_map/pallas_call | solution.py:491
  40.9 0.0 collective-permute-done.10
  40.9 1.5 %collective-permute-start.11 = (f32[2,8,128]{2,1,0:T(8,128)S(1)}, f32[2,8,128]{2,1,0:T(8,128)S(1)}, u32[]{:S(2)}, u32[]{:S(2)}) collective-permute-start(f32[2,8,128]{2,1,0:T(8,128)S(1)} %add.43), channel_id=1, source_target_pairs={{0,4},{4,0},{8,12},{12,8},{16,20},{20,16},{24,28},{28,24},{1,5},{5... | collective-permute-start | bytes 24584 | tf_op jit(solution)/shard_map/ppermute | solution.py:535
  42.4 1.7 %shard_map.92 = bf16[1024,8,256]{2,1,0:T(8,128)(2,1)} custom-call(s32[1024]{0:T(1024)S(1)} %bitcast.29, bf16[1032,8,256]{2,1,0:T(8,128)(2,1)S(1)} %get-tuple-element.43.table_ref, bf16[1024,8,256]{2,1,0:T(8,128)(2,1)} %shard_map.91.refs_0_), custom_call_target="tpu_custom_call", output_to_operand_aliasing={{}: (2, {})} | custom-call | flops 1000000 | bytes 6000000 | tf_op jit(solution)/shard_map/pallas_call | solution.py:491
  44.1 0.5 %collective-permute-done.11 = f32[2,8,128]{2,1,0:T(8,128)S(1)} collective-permute-done((f32[2,8,128]{2,1,0:T(8,128)S(1)}, f32[2,8,128]{2,1,0:T(8,128)S(1)}, u32[]{:S(2)}, u32[]{:S(2)}) %collective-permute-start.11) | collective-permute-done | bytes 8224 | tf_op jit(solution)/shard_map/ppermute | solution.py:535
  44.6 0.6 %divide_bitcast_fusion = f32[1024]{0:T(1024)} fusion(f32[2,8,128]{2,1,0:T(8,128)S(1)} %add.44), kind=kLoop, calls=%fused_computation.10 | loop fusion | flops 2048 | bytes 12288 | tf_op jit(solution)/shard_map/div | solution.py:578
  (5 shorter events, 0.1 us)
Async XLA Ops:
  0.6 23.9 %copy-start.2 = (f32[1,1024]{1,0:T(1,128)S(1)}, f32[1,1024]{1,0:T(1,128)}, u32[]{:S(2)}) copy-start(f32[1,1024]{1,0:T(1,128)} %constant.50.clone.weights_ref) | copy-start | bytes 12292
  1.8 13.4 %collective-permute-start.7 = (bf16[4,8,1024]{2,1,0:T(8,128)(2,1)S(1)}, bf16[4,8,1024]{2,1,0:T(8,128)(2,1)S(1)}, u32[]{:S(2)}, u32[]{:S(2)}) collective-permute-start(bf16[4,8,1024]{2,1,0:T(8,128)(2,1)S(1)} %get-tuple-element.51), channel_id=1, source_target_pairs={{0,12},{4,8},{8,4},{12,0},{16,28},{20,24},{24,20},{28,16},{1,13},{... | collective-permute-start | bytes 196616 | tf_op jit(solution)/shard_map/ppermute | solution.py:146
  4.4 11.7 %collective-permute-start.6 = (bf16[4,8,1024]{2,1,0:T(8,128)(2,1)S(1)}, bf16[4,8,1024]{2,1,0:T(8,128)(2,1)S(1)}, u32[]{:S(2)}, u32[]{:S(2)}) collective-permute-start(bf16[4,8,1024]{2,1,0:T(8,128)(2,1)S(1)} %get-tuple-element.52), channel_id=1, source_target_pairs={{0,8},{4,12},{8,0},{12,4},{16,24},{20,28},{24,16},{28,20},{1,9},{5... | collective-permute-start | bytes 196616 | tf_op jit(solution)/shard_map/ppermute | solution.py:146
  4.8 13.4 %collective-permute-start.5 = (bf16[4,8,1024]{2,1,0:T(8,128)(2,1)S(1)}, bf16[4,8,1024]{2,1,0:T(8,128)(2,1)S(1)}, u32[]{:S(2)}, u32[]{:S(2)}) collective-permute-start(bf16[4,8,1024]{2,1,0:T(8,128)(2,1)S(1)} %get-tuple-element.53), channel_id=1, source_target_pairs={{0,4},{4,0},{8,12},{12,8},{16,20},{20,16},{24,28},{28,24},{1,5},{5... | collective-permute-start | bytes 196616 | tf_op jit(solution)/shard_map/ppermute | solution.py:146
  5.4 14.8 %collective-permute-start.3 = (bf16[4,8,1024]{2,1,0:T(8,128)(2,1)S(1)}, bf16[4,8,1024]{2,1,0:T(8,128)(2,1)S(1)}, u32[]{:S(2)}, u32[]{:S(2)}) collective-permute-start(bf16[4,8,1024]{2,1,0:T(8,128)(2,1)S(1)} %get-tuple-element.54), channel_id=1, source_target_pairs={{0,28},{4,24},{8,20},{12,16},{16,12},{20,8},{24,4},{28,0},{1,29},{... | collective-permute-start | bytes 196616 | tf_op jit(solution)/shard_map/ppermute | solution.py:146
  9.9 10.3 %collective-permute-start.2 = (bf16[4,8,1024]{2,1,0:T(8,128)(2,1)S(1)}, bf16[4,8,1024]{2,1,0:T(8,128)(2,1)S(1)}, u32[]{:S(2)}, u32[]{:S(2)}) collective-permute-start(bf16[4,8,1024]{2,1,0:T(8,128)(2,1)S(1)} %get-tuple-element.55), channel_id=1, source_target_pairs={{0,24},{4,28},{8,16},{12,20},{16,8},{20,12},{24,0},{28,4},{1,25},{... | collective-permute-start | bytes 196616 | tf_op jit(solution)/shard_map/ppermute | solution.py:146
  10.1 1.6 %copy-start = (bf16[1024,1024]{1,0:T(8,128)(2,1)S(1)}, bf16[1024,1024]{1,0:T(8,128)(2,1)}, u32[]{:S(2)}) copy-start(bf16[1024,1024]{1,0:T(8,128)(2,1)} %constant.48.clone.forward_ref) | copy-start | bytes 6291460
  11.7 1.0 %copy-start.1 = (bf16[1024,256]{1,0:T(8,128)(2,1)S(1)}, bf16[1024,256]{1,0:T(8,128)(2,1)}, u32[]{:S(2)}) copy-start(bf16[1024,256]{1,0:T(8,128)(2,1)} %constant.49.clone.inverse_ref) | copy-start | bytes 1572868
  12.7 0.7 %copy-start.3 = (s32[1024,2]{0,1:T(2,128)S(1)}, s32[1024,2]{0,1:T(2,128)}, u32[]{:S(2)}) copy-start(s32[1024,2]{0,1:T(2,128)} %param.8) | copy-start | bytes 24580
  13.4 0.7 %copy-start.4 = (s32[1024]{0:T(1024)S(1)}, s32[1024]{0:T(1024)}, u32[]{:S(2)}) copy-start(s32[1024]{0:T(1024)} %param.9) | copy-start | bytes 12292
  14.1 0.7 %copy-start.5 = (s32[128,8]{0,1:T(8,128)S(1)}, s32[128,8]{0,1:T(8,128)}, u32[]{:S(2)}) copy-start(s32[128,8]{0,1:T(8,128)} %param.10) | copy-start | bytes 12292
  15.2 7.3 %collective-permute-start.1 = (bf16[4,8,1024]{2,1,0:T(8,128)(2,1)S(1)}, bf16[4,8,1024]{2,1,0:T(8,128)(2,1)S(1)}, u32[]{:S(2)}, u32[]{:S(2)}) collective-permute-start(bf16[4,8,1024]{2,1,0:T(8,128)(2,1)S(1)} %get-tuple-element.56), channel_id=1, source_target_pairs={{0,20},{4,16},{8,28},{12,24},{16,4},{20,0},{24,12},{28,8},{1,21},{... | collective-permute-start | bytes 196616 | tf_op jit(solution)/shard_map/ppermute | solution.py:146
  16.1 6.5 %collective-permute-start = (bf16[4,8,1024]{2,1,0:T(8,128)(2,1)S(1)}, bf16[4,8,1024]{2,1,0:T(8,128)(2,1)S(1)}, u32[]{:S(2)}, u32[]{:S(2)}) collective-permute-start(bf16[4,8,1024]{2,1,0:T(8,128)(2,1)S(1)} %get-tuple-element.57), channel_id=1, source_target_pairs={{0,16},{4,20},{8,24},{12,28},{16,0},{20,4},{24,8},{28,12},{1,17},{... | collective-permute-start | bytes 196616 | tf_op jit(solution)/shard_map/ppermute | solution.py:146
  18.2 9.5 %collective-permute-start.8 = (bf16[128,1024]{1,0:T(8,128)(2,1)S(1)}, bf16[128,1024]{1,0:T(8,128)(2,1)S(1)}, u32[]{:S(2)}, u32[]{:S(2)}) collective-permute-start(bf16[128,1024]{1,0:T(8,128)(2,1)S(1)} %maximum_bitcast_fusion.1.near_ref), channel_id=1, source_target_pairs={{16,17},{20,21},{24,25},{28,29},{1,0},{5,4},{9,8},{13,12},{17,18},... | collective-permute-start | bytes 786440 | tf_op jit(solution)/shard_map/ppermute | solution.py:522
  22.6 7.7 %collective-permute-start.4 = (bf16[128,1024]{1,0:T(8,128)(2,1)S(1)}, bf16[128,1024]{1,0:T(8,128)(2,1)S(1)}, u32[]{:S(2)}, u32[]{:S(2)}) collective-permute-start(bf16[128,1024]{1,0:T(8,128)(2,1)S(1)} %maximum_bitcast_fusion.far_ref), channel_id=1, source_target_pairs={{0,1},{4,5},{8,9},{12,13},{1,2},{5,6},{9,10},{13,14},{17,16},{21,2... | collective-permute-start | bytes 786440 | tf_op jit(solution)/shard_map/ppermute | solution.py:523
  31.8 4.6 %collective-permute-start.9 = (f32[2,8,128]{2,1,0:T(8,128)S(1)}, f32[2,8,128]{2,1,0:T(8,128)S(1)}, u32[]{:S(2)}, u32[]{:S(2)}) collective-permute-start(f32[2,8,128]{2,1,0:T(8,128)S(1)} %get-tuple-element.42), channel_id=1, source_target_pairs={{0,16},{4,20},{8,24},{12,28},{16,0},{20,4},{24,8},{28,12},{1,17},{... | collective-permute-start | bytes 24584 | tf_op jit(solution)/shard_map/ppermute | solution.py:535
  36.4 4.5 %collective-permute-start.10 = (f32[2,8,128]{2,1,0:T(8,128)S(1)}, f32[2,8,128]{2,1,0:T(8,128)S(1)}, u32[]{:S(2)}, u32[]{:S(2)}) collective-permute-start(f32[2,8,128]{2,1,0:T(8,128)S(1)} %add.42), channel_id=1, source_target_pairs={{0,8},{4,12},{8,0},{12,4},{16,24},{20,28},{24,16},{28,20},{1,9},{5... | collective-permute-start | bytes 24584 | tf_op jit(solution)/shard_map/ppermute | solution.py:535
  40.9 3.7 %collective-permute-start.11 = (f32[2,8,128]{2,1,0:T(8,128)S(1)}, f32[2,8,128]{2,1,0:T(8,128)S(1)}, u32[]{:S(2)}, u32[]{:S(2)}) collective-permute-start(f32[2,8,128]{2,1,0:T(8,128)S(1)} %add.43), channel_id=1, source_target_pairs={{0,4},{4,0},{8,12},{12,8},{16,20},{20,16},{24,28},{28,24},{1,5},{5... | collective-permute-start | bytes 24584 | tf_op jit(solution)/shard_map/ppermute | solution.py:535

commit v5 on v4

--- a/solution.py
+++ b/solution.py
@@ -24,11 +24,7 @@
     factor = np.where(bins == 0, 1.0, 2.0)[:, None]
     inverse = np.concatenate([factor * np.cos(lag_angle), -factor * np.sin(lag_angle)], axis=0)
     weights = np.concatenate([factor[:, 0], factor[:, 0]])[None, :]
-    return (
-        jnp.asarray(forward.astype(jnp.bfloat16)),
-        jnp.asarray(inverse.astype(jnp.bfloat16)),
-        jnp.asarray(weights.astype(np.float32)),
-    )
+    return forward.astype(jnp.bfloat16), inverse.astype(jnp.bfloat16), weights.astype(np.float32)
 
 
 def pair_kernel(
@@ -126,7 +122,7 @@
     )(slots, *traces, presence, forward, inverse, weights)
 
 
-def exchange(waveforms, sta_count):
+def exchange(waveforms, sta_count, tables):
     events, stations, window = waveforms.shape
     share = stations // sta_count
     blocks = waveforms.reshape(events, sta_count, share, window)
@@ -140,14 +136,22 @@
             for pairs, target in ((toward, e + step), (away, e - step)):
                 if 0 <= target < evt_count:
                     pairs.append((s * evt_count + e, s * evt_count + target))
-    pieces = [lax.dynamic_index_in_dim(blocks, me, axis=1, keepdims=False)]
-    for j in range(1, sta_count):
-        piece = lax.dynamic_index_in_dim(blocks, me ^ j, axis=1, keepdims=False)
-        pieces.append(lax.ppermute(piece, "sta", [(i, i ^ j) for i in range(sta_count)]))
+    def for_station(i):
+        return lax.dynamic_index_in_dim(blocks, i, axis=1, keepdims=False)
+
+    def swap(piece, j):
+        return lax.ppermute(piece, "sta", [(i, i ^ j) for i in range(sta_count)])
+
+    later = [swap(for_station(me ^ j), j) for j in range(half, sta_count)]
+    across = swap(jnp.stack([for_station(me ^ 2), for_station(me ^ 3)]), 2)
+    beside = swap(jnp.concatenate([for_station(me ^ 1), across[1]], axis=0), 1)
+    later[3], tables = lax.optimization_barrier((later[3], tables))
+    tables = bring_call(tables)
+    pieces = [for_station(me), beside[:events], across[0], beside[events:]] + later
     rows = half * events * share
     near = jnp.concatenate(pieces[:half], axis=0).reshape(rows, window)
     far = jnp.concatenate(pieces[half:], axis=0).reshape(rows, window)
-    return near, far, toward, away
+    return near, far, toward, away, tables
 
 
 def exchange_whole(waveforms):
@@ -189,11 +193,11 @@
     return jnp.concatenate([ra * rb + ia * ib, ra * ib - ia * rb], axis=1)
 
 
-def scaled_spectra(traces_ref, me, each, place, presence_ref, present, forward_ref, weights_ref, spec_ref):
+def scaled_spectra(traces_ref, me, each, place, presence_ref, present, tables_ref, weights_ref, spec_ref):
     stations, window = spec_ref.shape[1:]
     events = traces_ref.shape[0] // stations
     pieces = events // each
-    result = jnp.dot(traces_ref[...], forward_ref[...], preferred_element_type=jnp.float32)
+    result = jnp.dot(traces_ref[...], tables_ref[:, :window], preferred_element_type=jnp.float32)
     rounded = result.astype(jnp.bfloat16).astype(jnp.float32)
     energy = jnp.sum(jnp.square(rounded) * weights_ref[...], axis=1, keepdims=True) + 1e-06
     gain = jnp.broadcast_to(lax.rsqrt(energy), (events * stations, LANES)).reshape(events, stations, LANES)
@@ -229,33 +233,23 @@
 
 
 def prepare_kernel(
-    each, block, events_ref, valid_ref, presence_ref, forward_ref, inverse_ref,
-    row_ref, count_ref, held_ref, forward_out, inverse_out, events_in, valid_in, presence_in, sems,
+    each, block, packed_ref, row_ref, count_ref, held_ref,
 ):
-    copies = [
-        pltpu.make_async_copy(events_ref, events_in, sems.at[0]),
-        pltpu.make_async_copy(valid_ref, valid_in, sems.at[1]),
-        pltpu.make_async_copy(presence_ref, presence_in, sems.at[2]),
-        pltpu.make_async_copy(forward_ref, forward_out, sems.at[3]),
-        pltpu.make_async_copy(inverse_ref, inverse_out, sems.at[4]),
-    ]
-    for copy in copies:
-        copy.start()
     me, start = lax.axis_index("sta"), lax.axis_index("evt") * block
-    for copy in copies[:3]:
-        copy.wait()
     lines = row_ref.shape[0]
 
-    def stacked(ref, line):
-        return jnp.concatenate([ref[line:line + 1, i * LANES:(i + 1) * LANES] for i in range(lines)], axis=0)
-
-    first, second, valid = stacked(events_in, 0), stacked(events_in, 1), stacked(valid_in, 0)
+    def stacked(line):
+        return jnp.concatenate(
+            [packed_ref[line:line + 1, i * LANES:(i + 1) * LANES] for i in range(lines)], axis=0
+        )
+
+    first, second, valid = stacked(0), stacked(1), stacked(2)
     rows = Rows(block)
     row = table_row(first - start, second - start, me, each, block, rows)
     row = jnp.where(valid > 0, row, rows.zero)
     row_ref[...] = jnp.clip(row, 0, rows.end - 1)
 
-    presence = presence_in[...]
+    presence = packed_ref[3:, :LANES]
     stations, events = presence.shape
     bits = jnp.zeros((1, events), jnp.int32)
     for s in range(stations):
@@ -272,11 +266,15 @@
     for i in range(held_ref.shape[0]):
         mine = jnp.where(lane == start - block // 2 + i, present, 0.0)
         held_ref[i] = jnp.broadcast_to(jnp.sum(mine, axis=1, keepdims=True), (stations, LANES))
-    for copy in copies[3:]:
-        copy.wait()
-
-
-def own_pairs(spec_ref, inverse_ref, table_ref, peaks, lhs_ref):
+
+
+def bring_kernel(tables_ref, tables_out, sem):
+    copy = pltpu.make_async_copy(tables_ref, tables_out, sem)
+    copy.start()
+    copy.wait()
+
+
+def own_pairs(spec_ref, tables_ref, table_ref, peaks, lhs_ref):
     block, stations, window = spec_ref.shape
     half = window // 2
     pairs = own_list(block)
@@ -286,14 +284,14 @@
         held = {x: spec_ref[x] for x, _ in some}
         build(lhs_ref, low, some, lambda x: held[x], lambda y: spec_ref[y])
         rows = pl.ds(low * stations, len(some) * stations)
-        even = jnp.dot(lhs_ref[rows, :half], inverse_ref[:half], preferred_element_type=jnp.float32)
-        odd = jnp.dot(lhs_ref[rows, half:], inverse_ref[half:], preferred_element_type=jnp.float32)
+        even = jnp.dot(lhs_ref[rows, :half], tables_ref[:half, window:], preferred_element_type=jnp.float32)
+        odd = jnp.dot(lhs_ref[rows, half:], tables_ref[half:, window:], preferred_element_type=jnp.float32)
         keep(table_ref, peaks, even + odd, low)
         keep(table_ref, peaks, even - odd, len(pairs) + low)
 
 
-def halo_pairs(high, own_ref, spec_ref, inverse_ref, table_ref, peaks, lhs_ref, row):
-    band, stations = spec_ref.shape[:2]
+def halo_pairs(high, own_ref, spec_ref, tables_ref, table_ref, peaks, lhs_ref, row):
+    band, stations, window = spec_ref.shape
 
     def own(u):
         return own_ref[jnp.where(high, band + u, band - 1 - u)]
@@ -308,12 +306,12 @@
         held = {u: own(u) for u, _ in some}
         build(lhs_ref, low, some, lambda u: held[u], other)
         rows = pl.ds(low * stations, len(some) * stations)
-        lagged = jnp.dot(lhs_ref[rows, :], inverse_ref[...], preferred_element_type=jnp.float32)
+        lagged = jnp.dot(lhs_ref[rows, :], tables_ref[:, window:], preferred_element_type=jnp.float32)
         keep(table_ref, peaks, lagged, row + low)
 
 
 def own_kernel(
-    each, near_ref, far_ref, presence_ref, forward_ref, inverse_ref, weights_ref,
+    each, near_ref, far_ref, presence_ref, tables_ref, weights_ref,
     spec_ref, table_ref, peak_ref, lhs_ref,
 ):
     block, stations, window = spec_ref.shape
@@ -322,17 +320,17 @@
     mine = jnp.where(me * each < band, 0, band)
     for ref, place in ((near_ref, mine), (far_ref, band - mine)):
         scaled_spectra(
-            ref, me, each, place, presence_ref, band + place, forward_ref, weights_ref, spec_ref
+            ref, me, each, place, presence_ref, band + place, tables_ref, weights_ref, spec_ref
         )
     rows = Rows(block)
     peaks = no_peaks(rows, stations)
-    own_pairs(spec_ref, inverse_ref, table_ref, peaks, lhs_ref)
+    own_pairs(spec_ref, tables_ref, table_ref, peaks, lhs_ref)
     table_ref[rows.zero] = jnp.zeros(table_ref.shape[1:], table_ref.dtype)
     peak_ref[...] = jnp.concatenate(peaks, axis=1)
 
 
-def near_kernel(
-    each, halo_ref, own_ref, presence_ref, forward_ref, inverse_ref, weights_ref, own_peak_ref,
+def middle_kernel(
+    each, halo_ref, own_ref, presence_ref, tables_ref, weights_ref, own_peak_ref,
     held_table_ref, table_ref, peak_ref, other_ref, lhs_ref,
 ):
     del held_table_ref
@@ -341,15 +339,15 @@
     me = lax.axis_index("sta")
     high = me * each < band
     edge = jnp.where(high, 3 * band, 0)
-    scaled_spectra(halo_ref, me, each, 0, presence_ref, edge, forward_ref, weights_ref, other_ref)
+    scaled_spectra(halo_ref, me, each, 0, presence_ref, edge, tables_ref, weights_ref, other_ref)
     rows = Rows(block)
     peaks = no_peaks(rows, stations)
-    halo_pairs(high, own_ref, other_ref, inverse_ref, table_ref, peaks, lhs_ref, rows.near)
+    halo_pairs(high, own_ref, other_ref, tables_ref, table_ref, peaks, lhs_ref, rows.near)
     peak_ref[...] = own_peak_ref[...] + jnp.concatenate(peaks, axis=1)
 
 
 def last_kernel(
-    each, halo_ref, own_ref, presence_ref, forward_ref, inverse_ref, weights_ref, peak_ref, row_ref, count_ref,
+    each, halo_ref, own_ref, presence_ref, tables_ref, weights_ref, peak_ref, row_ref, count_ref,
     held_table_ref, table_ref, sums_ref, other_ref, lhs_ref,
 ):
     del held_table_ref
@@ -358,10 +356,10 @@
     me = lax.axis_index("sta")
     high = me * each >= band
     edge = jnp.where(high, 3 * band, 0)
-    scaled_spectra(halo_ref, me, each, 0, presence_ref, edge, forward_ref, weights_ref, other_ref)
+    scaled_spectra(halo_ref, me, each, 0, presence_ref, edge, tables_ref, weights_ref, other_ref)
     rows = Rows(block)
     peaks = no_peaks(rows, stations)
-    halo_pairs(high, own_ref, other_ref, inverse_ref, table_ref, peaks, lhs_ref, rows.far)
+    halo_pairs(high, own_ref, other_ref, tables_ref, table_ref, peaks, lhs_ref, rows.far)
     row = row_ref[...]
     lanes = row & (LANES - 1)
     total = jnp.zeros(row.shape, jnp.float32)
@@ -373,11 +371,18 @@
     sums_ref[1] = count_ref[...]
 
 
-def pick_kernel(group, skip, row_ref, table_ref, *refs):
-    out_ref = refs[-1]
-    base = (pl.program_id(0) + skip) * group
-    for j in range(group):
-        out_ref[j] = table_ref[row_ref[base + j]]
+def pick_kernel(start, group, row_ref, table_ref, *refs):
+    out_ref, picked_ref, sems = refs[-3:]
+    copies = []
+    for low in range(0, picked_ref.shape[0], group):
+        for i in range(low, low + group):
+            picked_ref[i] = table_ref[row_ref[start + i]]
+        copies.append(pltpu.make_async_copy(
+            picked_ref.at[pl.ds(low, group)], out_ref.at[pl.ds(start + low, group)], sems.at[low // group]
+        ))
+        copies[-1].start()
+    for copy in copies:
+        copy.wait()
 
 
 VMEM = pl.BlockSpec(memory_space=pltpu.VMEM)
@@ -391,37 +396,43 @@
     )
 
 
-def prepare_call(pair_events, pair_valid, presence, tables, each, block):
-    forward, inverse = tables[:2]
+def prepare_call(pair_events, pair_valid, presence, each, block):
     pairs = pair_events.shape[0]
-    stations = presence.shape[1]
+    events, stations = presence.shape
+    packed = jnp.concatenate(
+        [pair_events.T, pair_valid[None], jnp.pad(presence.T, ((0, 0), (0, pairs - events)))], axis=0
+    )
     line = (pairs // LANES, LANES)
-    anywhere = pl.BlockSpec(memory_space=pltpu.HBM)
     return pl.pallas_call(
         functools.partial(prepare_kernel, each, block),
         out_shape=(
             jax.ShapeDtypeStruct(line, jnp.int32),
             jax.ShapeDtypeStruct(line, jnp.float32),
             jax.ShapeDtypeStruct((2 * block, stations, LANES), jnp.float32),
-            jax.ShapeDtypeStruct(forward.shape, forward.dtype),
-            jax.ShapeDtypeStruct(inverse.shape, inverse.dtype),
         ),
-        in_specs=[anywhere] * 5,
-        out_specs=(VMEM,) * 5,
-        scratch_shapes=[
-            pltpu.VMEM((2, pairs), jnp.int32),
-            pltpu.VMEM((1, pairs), jnp.int32),
-            pltpu.VMEM(presence.shape[::-1], jnp.int32),
-            pltpu.SemaphoreType.DMA((5,)),
-        ],
+        in_specs=[VMEM],
+        out_specs=(VMEM,) * 3,
         compiler_params=PARAMS,
-        cost_estimate=pl.CostEstimate(flops=1_000_000, bytes_accessed=5_000_000, transcendentals=0),
-    )(pair_events.T, pair_valid.reshape(1, pairs), presence.T, forward, inverse)
+        cost_estimate=pl.CostEstimate(flops=1_000_000, bytes_accessed=1_000_000, transcendentals=0),
+    )(packed)
+
+
+def bring_call(tables):
+    return pl.pallas_call(
+        bring_kernel,
+        out_shape=jax.ShapeDtypeStruct(tables.shape, tables.dtype),
+        in_specs=[pl.BlockSpec(memory_space=pl.ANY)],
+        out_specs=VMEM,
+        scratch_shapes=[pltpu.SemaphoreType.DMA],
+        compiler_params=PARAMS,
+        cost_estimate=pl.CostEstimate(flops=0, bytes_accessed=5_000_000, transcendentals=0),
+    )(tables)
 
 
 def own_call(near, far, presence, tables, each, block):
-    forward, inverse, weights = tables
-    window, lags = inverse.shape
+    table_of, weights = tables
+    window = table_of.shape[0]
+    lags = table_of.shape[1] - window
     stations = presence.shape[1]
     rows = Rows(block)
     return pl.pallas_call(
@@ -431,40 +442,42 @@
             jax.ShapeDtypeStruct((rows.end, stations, lags), jnp.bfloat16),
             jax.ShapeDtypeStruct((stations, rows.lanes), jnp.float32),
         ),
-        in_specs=[VMEM] * 6,
+        in_specs=[VMEM] * 5,
         out_specs=(VMEM,) * 3,
         scratch_shapes=[pltpu.VMEM((rows.own * stations, window), jnp.bfloat16)],
         compiler_params=PARAMS,
         cost_estimate=cost(rows.own * stations, lags, window, near.shape[0] * 2, 8_000_000),
-    )(near, far, presence, forward, inverse, weights)
-
-
-def near_call(halo, own, presence, tables, peaks, table, each):
-    forward, inverse, weights = tables
-    window, lags = inverse.shape
+    )(near, far, presence, table_of, weights)
+
+
+def middle_call(halo, own, presence, tables, peaks, table, each):
+    table_of, weights = tables
+    window = table_of.shape[0]
+    lags = table_of.shape[1] - window
     block, stations = own.shape[:2]
     pairs = triangle(block // 2)
     return pl.pallas_call(
-        functools.partial(near_kernel, each),
+        functools.partial(middle_kernel, each),
         out_shape=(
             jax.ShapeDtypeStruct(table.shape, table.dtype),
             jax.ShapeDtypeStruct(peaks.shape, peaks.dtype),
         ),
-        in_specs=[VMEM] * 8,
+        in_specs=[VMEM] * 7,
         out_specs=(VMEM,) * 2,
         scratch_shapes=[
             pltpu.VMEM((block // 2, stations, window), jnp.float32),
             pltpu.VMEM((pairs * stations, window), jnp.bfloat16),
         ],
-        input_output_aliases={7: 0},
+        input_output_aliases={6: 0},
         compiler_params=PARAMS,
         cost_estimate=cost(pairs * stations, lags, window, halo.shape[0], 4_000_000),
-    )(halo, own, presence, forward, inverse, weights, peaks, table)
+    )(halo, own, presence, table_of, weights, peaks, table)
 
 
 def last_call(halo, own, presence, tables, peaks, row, count, table, each):
-    forward, inverse, weights = tables
-    window, lags = inverse.shape
+    table_of, weights = tables
+    window = table_of.shape[0]
+    lags = table_of.shape[1] - window
     block, stations = own.shape[:2]
     pairs = triangle(block // 2)
     return pl.pallas_call(
@@ -473,30 +486,33 @@
             jax.ShapeDtypeStruct(table.shape, table.dtype),
             jax.ShapeDtypeStruct((2,) + row.shape, jnp.float32),
         ),
-        in_specs=[VMEM] * 10,
+        in_specs=[VMEM] * 9,
         out_specs=(VMEM,) * 2,
         scratch_shapes=[
             pltpu.VMEM((block // 2, stations, window), jnp.float32),
             pltpu.VMEM((pairs * stations, window), jnp.bfloat16),
         ],
-        input_output_aliases={9: 0},
+        input_output_aliases={8: 0},
         compiler_params=PARAMS,
         cost_estimate=cost(pairs * stations, lags, window, halo.shape[0], 4_000_000),
-    )(halo, own, presence, forward, inverse, weights, peaks, row, count, table)
-
-
-def pick_call(row, table, held, skip, steps):
-    pairs = row.shape[0]
-    block = (LANES,) + table.shape[1:]
+    )(halo, own, presence, table_of, weights, peaks, row, count, table)
+
+
+def pick_call(row, table, held, start, count):
+    group = 64
+    anywhere = pl.BlockSpec(memory_space=pl.ANY)
     return pl.pallas_call(
-        functools.partial(pick_kernel, LANES, skip),
-        grid=(steps,),
-        out_shape=jax.ShapeDtypeStruct((pairs,) + table.shape[1:], table.dtype),
-        in_specs=[SMEM, VMEM] + [pl.BlockSpec(memory_space=pl.ANY)] * len(held),
-        out_specs=pl.BlockSpec(block, lambda i: (i + skip, 0, 0)),
+        functools.partial(pick_kernel, start, group),
+        out_shape=jax.ShapeDtypeStruct(row.shape + table.shape[1:], table.dtype),
+        in_specs=[SMEM, VMEM] + [anywhere] * len(held),
+        out_specs=anywhere,
+        scratch_shapes=[
+            pltpu.VMEM((count,) + table.shape[1:], table.dtype),
+            pltpu.SemaphoreType.DMA((count // group,)),
+        ],
         input_output_aliases={2: 0} if held else {},
         compiler_params=PARAMS,
-        cost_estimate=pl.CostEstimate(flops=1_000_000, bytes_accessed=3_000_000 * steps, transcendentals=0),
+        cost_estimate=pl.CostEstimate(flops=0, bytes_accessed=count * 20_000, transcendentals=0),
     )(row, table, *held)
 
 
@@ -514,17 +530,20 @@
     return jnp.where(high | (second < 0), outside, inside)
 
 
-def banded(waveforms, pair_events, pair_valid, presence, block, tables):
+def banded(waveforms, pair_events, pair_valid, presence, block):
     each = waveforms.shape[0]
-    near, far, toward, away = exchange(waveforms, lax.axis_size("sta"))
-    ready = prepare_call(pair_events, pair_valid, presence, tables, each, block)
-    far, ready = lax.optimization_barrier((far, ready))
-    near_halo = lax.ppermute(near, ("sta", "evt"), toward)
+    forward, inverse, weights = spectral_tables(waveforms.shape[2], LAGS)
+    tables = (jnp.asarray(np.concatenate([forward, inverse], axis=1)), jnp.asarray(weights))
+    near, far, toward, away, brought = exchange(waveforms, lax.axis_size("sta"), tables[0])
+    ready = prepare_call(pair_events, pair_valid, presence, each, block)
+    far, ready, brought = lax.optimization_barrier((far, ready, brought))
+    tables = (brought, tables[1])
+    near_tied, tables = lax.optimization_barrier((near, tables))
+    near_halo = lax.ppermute(near_tied, ("sta", "evt"), toward)
     far_halo = lax.ppermute(far, ("sta", "evt"), away)
-    row, count, held, forward, inverse = ready
-    tables = (forward, inverse, tables[2])
+    row, count, held = ready
     own, table, peaks = own_call(near, far, held, tables, each, block)
-    table, peaks = near_call(near_halo, own, held, tables, peaks, table, each)
+    table, peaks = middle_call(near_halo, own, held, tables, peaks, table, each)
     table, sums = last_call(far_halo, own, held, tables, peaks, row, count, table, each)
 
     row = row.reshape(-1)
@@ -534,14 +553,14 @@
     while step:
         arrived = lax.ppermute(sums, "sta", [(i, i ^ step) for i in range(lax.axis_size("sta"))])
         steps = -(-(groups - skip) // step.bit_length())
-        correlation = (pick_call(row, table, correlation, skip, steps),)
+        correlation = (pick_call(row, table, correlation, skip * LANES, steps * LANES),)
         sums, correlation = lax.optimization_barrier((sums + arrived, correlation))
         skip += steps
         step //= 2
     return correlation[0], sums
 
 
-def by_slot(waveforms, pair_events, pair_valid, presence, block, tables):
+def by_slot(waveforms, pair_events, pair_valid, presence, block):
     share = presence.shape[1]
     start = lax.axis_index("evt") * block
     traces = exchange_whole(waveforms)
@@ -562,6 +581,7 @@
         for i in (0, 1)
     )
     counts = jnp.sum(first * second, axis=1) * pair_valid.astype(jnp.float32)
+    tables = tuple(jnp.asarray(x) for x in spectral_tables(waveforms.shape[2], LAGS))
     correlation, peaks = pair_call(slots, traces, slot_presence, tables)
     sums = lax.psum(jnp.stack([peaks.reshape(-1), counts]), "sta")
     return correlation.reshape(-1, share, correlation.shape[1]), sums
@@ -571,8 +591,7 @@
     sta_count = lax.axis_size("sta")
     local_events, stations, window = waveforms.shape
     block = sta_count * local_events
-    tables = spectral_tables(window, LAGS)
-    args = (waveforms, pair_events, pair_valid, presence, block, tables)
+    args = (waveforms, pair_events, pair_valid, presence, block)
     dense = sta_count == 8 and presence.shape[0] == LANES and block * block <= pair_events.shape[0]
     correlation, sums = (banded if dense else by_slot)(*args)
     pair_peak = sums[0] / jnp.maximum(sums[1], 1.0)

time: 45.6 us -> 43.2 us (0.947)
  the two profiles are of different devices: /device:TPU:4 before, /device:TPU:0 now
where the time goes in v5:
time: 43.2 us; the launch traced here: 42.9 us
  starting transfers between devices  17.9 us (41%)
  Pallas kernels  11.8 us (27%)
  waiting for transfers between devices  7.99 us (18%)
  local copies, waits for them, and re-layouts  2.89 us (7%)
  other arithmetic  1.46 us (3%)
  between operations  0.86 us (2%)
    ppermute x6, starting transfers between devices, swap(): return lax.ppermute(piece, 'sta', [(i, i ^ j) for i in range(sta_count)])  12.3 us
    pallas_call x3, Pallas kernels, pick_call(): pl.pallas_call(functools.partial(pick_kernel, start, group), out_shape=ja...  5.32 us
    ppermute x3, waiting for transfers between devices, banded(): lax.ppermute(sums, 'sta', [(i, i ^ step) for i in range(lax.axis_size('st...  5.21 us
    pallas_call x1, Pallas kernels, own_call(): pl.pallas_call(functools.partial(own_kernel, each), out_shape=(jax.ShapeD...  3.12 us
    ppermute x1, starting transfers between devices, banded(): far_halo = lax.ppermute(far, ('sta', 'evt'), away)  3.05 us
    ppermute x6, waiting for transfers between devices, swap(): return lax.ppermute(piece, 'sta', [(i, i ^ j) for i in range(sta_count)])  2.78 us
    unnamed x4, local copies, waits for them, and re-layouts  1.74 us
    pallas_call x1, Pallas kernels, last_call(): pl.pallas_call(functools.partial(last_kernel, each), out_shape=(jax.Shape...  1.52 us
  transfers between devices with their start and end apart: 11, of which 5 were waited for; matrix products, arithmetic and copies ran while one was open for 2% of the time, Pallas kernels for 24%

profile of v5, /device:TPU:0, one launch (start us, length us, event | category | flops | bytes accessed | tf_op | source)
XLA Modules:
  0.0 42.9 jit_solution(1834907095198152151)
XLA Ops:
  0.7 0.0 copy-start.1
  0.7 1.1 %dynamic-slice_bitcast_fusion.3 = (bf16[4,8,1024]{2,1,0:T(8,128)(2,1)S(1)}, bf16[1,4,8,1024]{3,2,1,0:T(8,128)(2,1)S(1)}, bf16[1,4,8,1024]{3,2,1,0:T(8,128)(2,1)S...) fusion(bf16[4,8,8,1024]{3,2,1,0:T(8,128)(2,1)} %bitcast.34, ...), kind=kLoop, calls=%fused_computation.10 | loop fusion | bytes 1048608 | tf_op jit(solution)/shard_map/jit(dynamic_index_in_dim)/squeeze | solution.py:140
  1.8 3.1 %collective-permute-start.5 = (bf16[2,4,8,1024]{3,2,1,0:T(8,128)(2,1)S(1)}, bf16[2,4,8,1024]{3,2,1,0:T(8,128)(2,1)S(1)}, u32[]{:S(2)}, u32[]{:S(2)}) collective-permute-start(bf16[2,4,8,1024]{3,2,1,0:T(8,128)(2,1)S(1)} %pad_maximum_fusion), channel_id=1, source_target_pairs={{0,8},{4,12},{8,0},{12,4},{16,24},{20,28},{24,16},{28,20},{1,9},{5... | collective-permute-start | bytes 393224 | tf_op jit(solution)/shard_map/ppermute | solution.py:143
  4.9 3.4 %collective-permute-start.3 = (bf16[4,8,1024]{2,1,0:T(8,128)(2,1)S(1)}, bf16[4,8,1024]{2,1,0:T(8,128)(2,1)S(1)}, u32[]{:S(2)}, u32[]{:S(2)}) collective-permute-start(bf16[4,8,1024]{2,1,0:T(8,128)(2,1)S(1)} %get-tuple-element.58), channel_id=1, source_target_pairs={{0,28},{4,24},{8,20},{12,16},{16,12},{20,8},{24,4},{28,0},{1,29},{... | collective-permute-start | bytes 196616 | tf_op jit(solution)/shard_map/ppermute | solution.py:143
  8.3 1.3 %collective-permute-start.2 = (bf16[4,8,1024]{2,1,0:T(8,128)(2,1)S(1)}, bf16[4,8,1024]{2,1,0:T(8,128)(2,1)S(1)}, u32[]{:S(2)}, u32[]{:S(2)}) collective-permute-start(bf16[4,8,1024]{2,1,0:T(8,128)(2,1)S(1)} %get-tuple-element.59), channel_id=1, source_target_pairs={{0,24},{4,28},{8,16},{12,20},{16,8},{20,12},{24,0},{28,4},{1,25},{... | collective-permute-start | bytes 196616 | tf_op jit(solution)/shard_map/ppermute | solution.py:143
  9.7 0.8 %collective-permute-start.1 = (bf16[4,8,1024]{2,1,0:T(8,128)(2,1)S(1)}, bf16[4,8,1024]{2,1,0:T(8,128)(2,1)S(1)}, u32[]{:S(2)}, u32[]{:S(2)}) collective-permute-start(bf16[4,8,1024]{2,1,0:T(8,128)(2,1)S(1)} %get-tuple-element.60), channel_id=1, source_target_pairs={{0,20},{4,16},{8,28},{12,24},{16,4},{20,0},{24,12},{28,8},{1,21},{... | collective-permute-start | bytes 196616 | tf_op jit(solution)/shard_map/ppermute | solution.py:143
  10.4 2.1 %collective-permute-start = (bf16[4,8,1024]{2,1,0:T(8,128)(2,1)S(1)}, bf16[4,8,1024]{2,1,0:T(8,128)(2,1)S(1)}, u32[]{:S(2)}, u32[]{:S(2)}) collective-permute-start(bf16[4,8,1024]{2,1,0:T(8,128)(2,1)S(1)} %get-tuple-element.61), channel_id=1, source_target_pairs={{0,16},{4,20},{8,24},{12,28},{16,0},{20,4},{24,8},{28,12},{1,17},{... | collective-permute-start | bytes 196616 | tf_op jit(solution)/shard_map/ppermute | solution.py:143
  12.6 0.0 collective-permute-done.5
  12.6 1.6 %collective-permute-start.6 = (bf16[8,8,1024]{2,1,0:T(8,128)(2,1)S(1)}, bf16[8,8,1024]{2,1,0:T(8,128)(2,1)S(1)}, u32[]{:S(2)}, u32[]{:S(2)}) collective-permute-start(bf16[8,8,1024]{2,1,0:T(8,128)(2,1)S(1)} %pad_maximum_fusion.1), channel_id=1, source_target_pairs={{0,4},{4,0},{8,12},{12,8},{16,20},{20,16},{24,28},{28,24},{1,5},{5... | collective-permute-start | bytes 393224 | tf_op jit(solution)/shard_map/ppermute | solution.py:143
  14.2 0.7 %pad_add_fusion.packed_ref = s32[11,1024]{1,0:T(8,128)S(1)} fusion(s32[8,128]{1,0:T(8,128)} %bitcast.36, s32[1,1024]{1,0:T(1,128)} %bitcast.37, s32[2,1024]{1,0:T(2,128)} %bitcast.35), kind=kLoop, calls=%fused_computation.6 | loop fusion | flops 22528 | bytes 61440 | tf_op jit(solution)/shard_map/concatenate | solution.py:402
  14.9 0.2 shard_map.77
  15.1 0.0 collective-permute-done.3
  15.2 0.0 copy-start
  15.2 1.7 %copy-done = bf16[1024,1280]{1,0:T(8,128)(2,1)S(1)} copy-done((bf16[1024,1280]{1,0:T(8,128)(2,1)S(1)}, bf16[1024,1280]{1,0:T(8,128)(2,1)}, u32[]{:S(2)}) %copy-start) | copy-done | bytes 2621464
  16.9 0.2 shard_map.78.tables_ref
  17.1 0.0 collective-permute-done.2
  17.1 2.5 %collective-permute-done.1 = bf16[4,8,1024]{2,1,0:T(8,128)(2,1)S(1)} collective-permute-done((bf16[4,8,1024]{2,1,0:T(8,128)(2,1)S(1)}, bf16[4,8,1024]{2,1,0:T(8,128)(2,1)S(1)}, u32[]{:S(2)}, u32[]{:S(2)}) %collective-permute-start.1) | collective-permute-done | bytes 65568 | tf_op jit(solution)/shard_map/ppermute | solution.py:143
  19.6 0.3 collective-permute-done
  19.9 0.0 collective-permute-done.6
  20.0 1.3 %collective-permute-start.7 = (bf16[128,1024]{1,0:T(8,128)(2,1)S(1)}, bf16[128,1024]{1,0:T(8,128)(2,1)S(1)}, u32[]{:S(2)}, u32[]{:S(2)}) collective-permute-start(bf16[128,1024]{1,0:T(8,128)(2,1)S(1)} %maximum_bitcast_fusion.1.near_ref), channel_id=1, source_target_pairs={{16,17},{20,21},{24,25},{28,29},{1,0},{5,4},{9,8},{13,12},{17,18},... | collective-permute-start | bytes 786440 | tf_op jit(solution)/shard_map/ppermute | solution.py:542
  21.3 3.0 %collective-permute-start.4 = (bf16[128,1024]{1,0:T(8,128)(2,1)S(1)}, bf16[128,1024]{1,0:T(8,128)(2,1)S(1)}, u32[]{:S(2)}, u32[]{:S(2)}) collective-permute-start(bf16[128,1024]{1,0:T(8,128)(2,1)S(1)} %maximum_bitcast_fusion.far_ref), channel_id=1, source_target_pairs={{0,1},{4,5},{8,9},{12,13},{1,2},{5,6},{9,10},{13,14},{17,16},{21,2... | collective-permute-start | bytes 786440 | tf_op jit(solution)/shard_map/ppermute | solution.py:543
  24.3 0.0 copy-done.1
  24.3 3.1 %shard_map.79 = (f32[32,8,1024]{2,1,0:T(8,128)S(1)}, bf16[1032,8,256]{2,1,0:T(8,128)(2,1)S(1)}, f32[8,1152]{1,0:T(8,128)S(1)}) custom-call(bf16[128,1024]{1,0:T(8,128)(2,1)S(1)} %maximum_bitcast_fusion.1.near_ref, bf16[128,1024]{1,0:T(8,128)(2,1)S(1)} %maximum_bitcast_fusion.far_ref, f32[64,8,128]{2,1,0:T(8,128)S(1)} %get-tuple-element.34.presence_ref, ...), custom_call_target="tpu_custom_call" | custom-call | flops 2113929216 | bytes 8000000 | tf_op jit(solution)/shard_map/pallas_call | solution.py:438
  27.5 0.0 collective-permute-done.7.halo_ref
  27.5 1.4 %shard_map.80 = (bf16[1032,8,256]{2,1,0:T(8,128)(2,1)S(1)}, f32[8,1152]{1,0:T(8,128)S(1)}) custom-call(bf16[128,1024]{1,0:T(8,128)(2,1)S(1)} %collective-permute-done.7.halo_ref, f32[32,8,1024]{2,1,0:T(8,128)S(1)} %get-tuple-element.38.own_ref, f32[64,8,128]{2,1,0:T(8,128)S(1)} %get-tuple-element.34.presence_ref, ...), custom_call_target="tpu_custom_call", output_to_operand_aliasing={{0}: (6, {})} | custom-call | flops 838860800 | bytes 4000000 | tf_op jit(solution)/shard_map/pallas_call | solution.py:459
  28.9 0.0 collective-permute-done.4.halo_ref
  28.9 1.5 %shard_map.81 = (bf16[1032,8,256]{2,1,0:T(8,128)(2,1)S(1)}, f32[2,8,128]{2,1,0:T(8,128)S(1)}) custom-call(bf16[128,1024]{1,0:T(8,128)(2,1)S(1)} %collective-permute-done.4.halo_ref, f32[32,8,1024]{2,1,0:T(8,128)S(1)} %get-tuple-element.38.own_ref, f32[64,8,128]{2,1,0:T(8,128)S(1)} %get-tuple-element.34.presence_ref, ...), custom_call_target="tpu_custom_call", output_to_operand_aliasing={{0}: (8, {})} | custom-call | flops 838860800 | bytes 4000000 | tf_op jit(solution)/shard_map/pallas_call | solution.py:483
  30.4 0.0 collective-permute-start.8
  30.5 1.8 %shard_map.82.refs_0_ = bf16[1024,8,256]{2,1,0:T(8,128)(2,1)} custom-call(s32[1024]{0:T(1024)S(1)} %bitcast.31, bf16[1032,8,256]{2,1,0:T(8,128)(2,1)S(1)} %get-tuple-element.47.table_ref), custom_call_target="tpu_custom_call" | custom-call | bytes 7680000 | tf_op jit(solution)/shard_map/pallas_call | solution.py:504
  32.3 2.7 %collective-permute-done.8 = f32[2,8,128]{2,1,0:T(8,128)S(1)} collective-permute-done((f32[2,8,128]{2,1,0:T(8,128)S(1)}, f32[2,8,128]{2,1,0:T(8,128)S(1)}, u32[]{:S(2)}, u32[]{:S(2)}) %collective-permute-start.8) | collective-permute-done | bytes 8224 | tf_op jit(solution)/shard_map/ppermute | solution.py:554
  35.0 0.1 collective-permute-start.9
  35.1 1.8 %shard_map.83.refs_0_ = bf16[1024,8,256]{2,1,0:T(8,128)(2,1)} custom-call(s32[1024]{0:T(1024)S(1)} %bitcast.32, bf16[1032,8,256]{2,1,0:T(8,128)(2,1)S(1)} %get-tuple-element.47.table_ref, bf16[1024,8,256]{2,1,0:T(8,128)(2,1)} %shard_map.82.refs_0_), custom_call_target="tpu_custom_call", output_to_operand_aliasing={{}: (2, {})} | custom-call | bytes 7680000 | tf_op jit(solution)/shard_map/pallas_call | solution.py:504
  36.9 1.8 %collective-permute-done.9 = f32[2,8,128]{2,1,0:T(8,128)S(1)} collective-permute-done((f32[2,8,128]{2,1,0:T(8,128)S(1)}, f32[2,8,128]{2,1,0:T(8,128)S(1)}, u32[]{:S(2)}, u32[]{:S(2)}) %collective-permute-start.9) | collective-permute-done | bytes 8224 | tf_op jit(solution)/shard_map/ppermute | solution.py:554
  38.7 1.2 %collective-permute-start.10 = (f32[2,8,128]{2,1,0:T(8,128)S(1)}, f32[2,8,128]{2,1,0:T(8,128)S(1)}, u32[]{:S(2)}, u32[]{:S(2)}) collective-permute-start(f32[2,8,128]{2,1,0:T(8,128)S(1)} %add.45), channel_id=1, source_target_pairs={{0,4},{4,0},{8,12},{12,8},{16,20},{20,16},{24,28},{28,24},{1,5},{5... | collective-permute-start | bytes 24584 | tf_op jit(solution)/shard_map/ppermute | solution.py:554
  39.9 1.6 %shard_map.84 = bf16[1024,8,256]{2,1,0:T(8,128)(2,1)} custom-call(s32[1024]{0:T(1024)S(1)} %bitcast.33, bf16[1032,8,256]{2,1,0:T(8,128)(2,1)S(1)} %get-tuple-element.47.table_ref, bf16[1024,8,256]{2,1,0:T(8,128)(2,1)} %shard_map.83.refs_0_), custom_call_target="tpu_custom_call", output_to_operand_aliasing={{}: (2, {})} | custom-call | bytes 5120000 | tf_op jit(solution)/shard_map/pallas_call | solution.py:504
  41.6 0.8 %collective-permute-done.10 = f32[2,8,128]{2,1,0:T(8,128)S(1)} collective-permute-done((f32[2,8,128]{2,1,0:T(8,128)S(1)}, f32[2,8,128]{2,1,0:T(8,128)S(1)}, u32[]{:S(2)}, u32[]{:S(2)}) %collective-permute-start.10) | collective-permute-done | bytes 8224 | tf_op jit(solution)/shard_map/ppermute | solution.py:554
  42.3 0.6 %divide_bitcast_fusion = f32[1024]{0:T(1024)} fusion(f32[2,8,128]{2,1,0:T(8,128)S(1)} %add.46), kind=kLoop, calls=%fused_computation.15 | loop fusion | flops 2048 | bytes 12288 | tf_op jit(solution)/shard_map/div | solution.py:597
  (9 shorter events, 0.1 us)
Async XLA Ops:
  0.7 23.7 %copy-start.1 = (f32[1,1024]{1,0:T(1,128)S(1)}, f32[1,1024]{1,0:T(1,128)}, u32[]{:S(2)}) copy-start(f32[1,1024]{1,0:T(1,128)} %constant.48.clone.weights_ref) | copy-start | bytes 12292
  1.8 10.7 %collective-permute-start.5 = (bf16[2,4,8,1024]{3,2,1,0:T(8,128)(2,1)S(1)}, bf16[2,4,8,1024]{3,2,1,0:T(8,128)(2,1)S(1)}, u32[]{:S(2)}, u32[]{:S(2)}) collective-permute-start(bf16[2,4,8,1024]{3,2,1,0:T(8,128)(2,1)S(1)} %pad_maximum_fusion), channel_id=1, source_target_pairs={{0,8},{4,12},{8,0},{12,4},{16,24},{20,28},{24,16},{28,20},{1,9},{5... | collective-permute-start | bytes 393224 | tf_op jit(solution)/shard_map/ppermute | solution.py:143
  4.9 10.2 %collective-permute-start.3 = (bf16[4,8,1024]{2,1,0:T(8,128)(2,1)S(1)}, bf16[4,8,1024]{2,1,0:T(8,128)(2,1)S(1)}, u32[]{:S(2)}, u32[]{:S(2)}) collective-permute-start(bf16[4,8,1024]{2,1,0:T(8,128)(2,1)S(1)} %get-tuple-element.58), channel_id=1, source_target_pairs={{0,28},{4,24},{8,20},{12,16},{16,12},{20,8},{24,4},{28,0},{1,29},{... | collective-permute-start | bytes 196616 | tf_op jit(solution)/shard_map/ppermute | solution.py:143
  8.3 8.8 %collective-permute-start.2 = (bf16[4,8,1024]{2,1,0:T(8,128)(2,1)S(1)}, bf16[4,8,1024]{2,1,0:T(8,128)(2,1)S(1)}, u32[]{:S(2)}, u32[]{:S(2)}) collective-permute-start(bf16[4,8,1024]{2,1,0:T(8,128)(2,1)S(1)} %get-tuple-element.59), channel_id=1, source_target_pairs={{0,24},{4,28},{8,16},{12,20},{16,8},{20,12},{24,0},{28,4},{1,25},{... | collective-permute-start | bytes 196616 | tf_op jit(solution)/shard_map/ppermute | solution.py:143
  9.7 9.9 %collective-permute-start.1 = (bf16[4,8,1024]{2,1,0:T(8,128)(2,1)S(1)}, bf16[4,8,1024]{2,1,0:T(8,128)(2,1)S(1)}, u32[]{:S(2)}, u32[]{:S(2)}) collective-permute-start(bf16[4,8,1024]{2,1,0:T(8,128)(2,1)S(1)} %get-tuple-element.60), channel_id=1, source_target_pairs={{0,20},{4,16},{8,28},{12,24},{16,4},{20,0},{24,12},{28,8},{1,21},{... | collective-permute-start | bytes 196616 | tf_op jit(solution)/shard_map/ppermute | solution.py:143
  10.4 9.4 %collective-permute-start = (bf16[4,8,1024]{2,1,0:T(8,128)(2,1)S(1)}, bf16[4,8,1024]{2,1,0:T(8,128)(2,1)S(1)}, u32[]{:S(2)}, u32[]{:S(2)}) collective-permute-start(bf16[4,8,1024]{2,1,0:T(8,128)(2,1)S(1)} %get-tuple-element.61), channel_id=1, source_target_pairs={{0,16},{4,20},{8,24},{12,28},{16,0},{20,4},{24,8},{28,12},{1,17},{... | collective-permute-start | bytes 196616 | tf_op jit(solution)/shard_map/ppermute | solution.py:143
  12.6 7.3 %collective-permute-start.6 = (bf16[8,8,1024]{2,1,0:T(8,128)(2,1)S(1)}, bf16[8,8,1024]{2,1,0:T(8,128)(2,1)S(1)}, u32[]{:S(2)}, u32[]{:S(2)}) collective-permute-start(bf16[8,8,1024]{2,1,0:T(8,128)(2,1)S(1)} %pad_maximum_fusion.1), channel_id=1, source_target_pairs={{0,4},{4,0},{8,12},{12,8},{16,20},{20,16},{24,28},{28,24},{1,5},{5... | collective-permute-start | bytes 393224 | tf_op jit(solution)/shard_map/ppermute | solution.py:143
  15.2 1.7 %copy-start = (bf16[1024,1280]{1,0:T(8,128)(2,1)S(1)}, bf16[1024,1280]{1,0:T(8,128)(2,1)}, u32[]{:S(2)}) copy-start(bf16[1024,1280]{1,0:T(8,128)(2,1)} %constant.47.clone.tables_ref) | copy-start | bytes 7864324
  20.0 7.5 %collective-permute-start.7 = (bf16[128,1024]{1,0:T(8,128)(2,1)S(1)}, bf16[128,1024]{1,0:T(8,128)(2,1)S(1)}, u32[]{:S(2)}, u32[]{:S(2)}) collective-permute-start(bf16[128,1024]{1,0:T(8,128)(2,1)S(1)} %maximum_bitcast_fusion.1.near_ref), channel_id=1, source_target_pairs={{16,17},{20,21},{24,25},{28,29},{1,0},{5,4},{9,8},{13,12},{17,18},... | collective-permute-start | bytes 786440 | tf_op jit(solution)/shard_map/ppermute | solution.py:542
  21.3 7.6 %collective-permute-start.4 = (bf16[128,1024]{1,0:T(8,128)(2,1)S(1)}, bf16[128,1024]{1,0:T(8,128)(2,1)S(1)}, u32[]{:S(2)}, u32[]{:S(2)}) collective-permute-start(bf16[128,1024]{1,0:T(8,128)(2,1)S(1)} %maximum_bitcast_fusion.far_ref), channel_id=1, source_target_pairs={{0,1},{4,5},{8,9},{12,13},{1,2},{5,6},{9,10},{13,14},{17,16},{21,2... | collective-permute-start | bytes 786440 | tf_op jit(solution)/shard_map/ppermute | solution.py:543
  30.4 4.6 %collective-permute-start.8 = (f32[2,8,128]{2,1,0:T(8,128)S(1)}, f32[2,8,128]{2,1,0:T(8,128)S(1)}, u32[]{:S(2)}, u32[]{:S(2)}) collective-permute-start(f32[2,8,128]{2,1,0:T(8,128)S(1)} %get-tuple-element.46), channel_id=1, source_target_pairs={{0,16},{4,20},{8,24},{12,28},{16,0},{20,4},{24,8},{28,12},{1,17},{... | collective-permute-start | bytes 24584 | tf_op jit(solution)/shard_map/ppermute | solution.py:554
  35.0 3.7 %collective-permute-start.9 = (f32[2,8,128]{2,1,0:T(8,128)S(1)}, f32[2,8,128]{2,1,0:T(8,128)S(1)}, u32[]{:S(2)}, u32[]{:S(2)}) collective-permute-start(f32[2,8,128]{2,1,0:T(8,128)S(1)} %add.44), channel_id=1, source_target_pairs={{0,8},{4,12},{8,0},{12,4},{16,24},{20,28},{24,16},{28,20},{1,9},{5... | collective-permute-start | bytes 24584 | tf_op jit(solution)/shard_map/ppermute | solution.py:554
  38.7 3.7 %collective-permute-start.10 = (f32[2,8,128]{2,1,0:T(8,128)S(1)}, f32[2,8,128]{2,1,0:T(8,128)S(1)}, u32[]{:S(2)}, u32[]{:S(2)}) collective-permute-start(f32[2,8,128]{2,1,0:T(8,128)S(1)} %add.45), channel_id=1, source_target_pairs={{0,4},{4,0},{8,12},{12,8},{16,20},{20,16},{24,28},{28,24},{1,5},{5... | collective-permute-start | bytes 24584 | tf_op jit(solution)/shard_map/ppermute | solution.py:554

commit v6 on v5

--- a/solution.py
+++ b/solution.py
@@ -128,14 +128,7 @@
     blocks = waveforms.reshape(events, sta_count, share, window)
     me = lax.axis_index("sta")
     half = sta_count // 2
-    evt_count = lax.axis_size("evt")
-    toward, away = [], []
-    for e in range(evt_count):
-        for s in range(sta_count):
-            step = -1 if s < half else 1
-            for pairs, target in ((toward, e + step), (away, e - step)):
-                if 0 <= target < evt_count:
-                    pairs.append((s * evt_count + e, s * evt_count + target))
+
     def for_station(i):
         return lax.dynamic_index_in_dim(blocks, i, axis=1, keepdims=False)
 
@@ -151,7 +144,7 @@
     rows = half * events * share
     near = jnp.concatenate(pieces[:half], axis=0).reshape(rows, window)
     far = jnp.concatenate(pieces[half:], axis=0).reshape(rows, window)
-    return near, far, toward, away, tables
+    return near, far, tables
 
 
 def exchange_whole(waveforms):
@@ -180,9 +173,9 @@
     def __init__(self, block):
         self.own = len(own_list(block))
         self.zero = 2 * self.own
-        self.near = self.zero + 8
-        self.far = self.near + triangle(block // 2)
-        self.end = self.far + triangle(block // 2)
+        self.first = self.zero + 8
+        self.second = self.first + triangle(block // 2)
+        self.end = self.second + triangle(block // 2)
         self.lanes = -(-self.end // LANES) * LANES
 
 
@@ -233,9 +226,10 @@
 
 
 def prepare_kernel(
-    each, block, packed_ref, row_ref, count_ref, held_ref,
+    block, packed_ref, row_ref, count_ref, held_ref,
 ):
-    me, start = lax.axis_index("sta"), lax.axis_index("evt") * block
+    place = lax.axis_index("evt")
+    start = place * block
     lines = row_ref.shape[0]
 
     def stacked(line):
@@ -245,7 +239,7 @@
 
     first, second, valid = stacked(0), stacked(1), stacked(2)
     rows = Rows(block)
-    row = table_row(first - start, second - start, me, each, block, rows)
+    row = table_row(first - start, second - start, place, block, rows)
     row = jnp.where(valid > 0, row, rows.zero)
     row_ref[...] = jnp.clip(row, 0, rows.end - 1)
 
@@ -337,12 +331,12 @@
     block, stations, window = own_ref.shape
     band = block // 2
     me = lax.axis_index("sta")
-    high = me * each < band
+    high = lax.axis_index("evt") % 2 == 0
     edge = jnp.where(high, 3 * band, 0)
     scaled_spectra(halo_ref, me, each, 0, presence_ref, edge, tables_ref, weights_ref, other_ref)
     rows = Rows(block)
     peaks = no_peaks(rows, stations)
-    halo_pairs(high, own_ref, other_ref, tables_ref, table_ref, peaks, lhs_ref, rows.near)
+    halo_pairs(high, own_ref, other_ref, tables_ref, table_ref, peaks, lhs_ref, rows.first)
     peak_ref[...] = own_peak_ref[...] + jnp.concatenate(peaks, axis=1)
 
 
@@ -354,12 +348,12 @@
     block, stations, window = own_ref.shape
     band = block // 2
     me = lax.axis_index("sta")
-    high = me * each >= band
+    high = lax.axis_index("evt") % 2 == 1
     edge = jnp.where(high, 3 * band, 0)
     scaled_spectra(halo_ref, me, each, 0, presence_ref, edge, tables_ref, weights_ref, other_ref)
     rows = Rows(block)
     peaks = no_peaks(rows, stations)
-    halo_pairs(high, own_ref, other_ref, tables_ref, table_ref, peaks, lhs_ref, rows.far)
+    halo_pairs(high, own_ref, other_ref, tables_ref, table_ref, peaks, lhs_ref, rows.second)
     row = row_ref[...]
     lanes = row & (LANES - 1)
     total = jnp.zeros(row.shape, jnp.float32)
@@ -396,7 +390,7 @@
     )
 
 
-def prepare_call(pair_events, pair_valid, presence, each, block):
+def prepare_call(pair_events, pair_valid, presence, block):
     pairs = pair_events.shape[0]
     events, stations = presence.shape
     packed = jnp.concatenate(
@@ -404,7 +398,7 @@
     )
     line = (pairs // LANES, LANES)
     return pl.pallas_call(
-        functools.partial(prepare_kernel, each, block),
+        functools.partial(prepare_kernel, block),
         out_shape=(
             jax.ShapeDtypeStruct(line, jnp.int32),
             jax.ShapeDtypeStruct(line, jnp.float32),
@@ -516,7 +510,7 @@
     )(row, table, *held)
 
 
-def table_row(first, second, me, each, block, rows):
+def table_row(first, second, place, block, rows):
     band = block // 2
     low, apart = jnp.minimum(first, second), jnp.abs(first - second)
     past = jnp.maximum(low - band, 0)
@@ -525,8 +519,7 @@
     high = second >= block
     u = jnp.where(high, first - band, band - 1 - first)
     h = jnp.where(high, second - block, -1 - second)
-    near = jnp.where(high, 1, 0) == jnp.where(me * each < band, 1, 0)
-    outside = jnp.where(near, rows.near, rows.far) + (u * (u + 1) >> 1) + h
+    outside = jnp.where(jnp.where(high, 1, 0) == place % 2, rows.second, rows.first) + (u * (u + 1) >> 1) + h
     return jnp.where(high | (second < 0), outside, inside)
 
 
@@ -534,17 +527,24 @@
     each = waveforms.shape[0]
     forward, inverse, weights = spectral_tables(waveforms.shape[2], LAGS)
     tables = (jnp.asarray(np.concatenate([forward, inverse], axis=1)), jnp.asarray(weights))
-    near, far, toward, away, brought = exchange(waveforms, lax.axis_size("sta"), tables[0])
-    ready = prepare_call(pair_events, pair_valid, presence, each, block)
+    near, far, brought = exchange(waveforms, lax.axis_size("sta"), tables[0])
+    ready = prepare_call(pair_events, pair_valid, presence, block)
     far, ready, brought = lax.optimization_barrier((far, ready, brought))
     tables = (brought, tables[1])
-    near_tied, tables = lax.optimization_barrier((near, tables))
-    near_halo = lax.ppermute(near_tied, ("sta", "evt"), toward)
-    far_halo = lax.ppermute(far, ("sta", "evt"), away)
+    me, place = lax.axis_index("sta"), lax.axis_index("evt")
+    count = lax.axis_size("evt")
+    inward = (place % 2 == 0) == (me * each < block // 2)
+
+    def swapped(half, odd):
+        links = [(i, i + 1) for i in range(odd, count - 1, 2)]
+        return lax.ppermute(half, "evt", links + [(j, i) for i, j in links])
+
+    first_halo = swapped(jnp.where(inward, far, near), 0)
+    second_halo = swapped(jnp.where(inward, near, far), 1)
     row, count, held = ready
     own, table, peaks = own_call(near, far, held, tables, each, block)
-    table, peaks = middle_call(near_halo, own, held, tables, peaks, table, each)
-    table, sums = last_call(far_halo, own, held, tables, peaks, row, count, table, each)
+    table, peaks = middle_call(first_halo, own, held, tables, peaks, table, each)
+    table, sums = last_call(second_halo, own, held, tables, peaks, row, count, table, each)
 
     row = row.reshape(-1)
     groups = row.shape[0] // LANES

time: 43.2 us -> 40.6 us (0.940)
  the two profiles are of different devices: /device:TPU:0 before, /device:TPU:4 now
where the time goes in v6:
time: 40.6 us; the launch traced here: 40.4 us
  starting transfers between devices  15.5 us (38%)
  Pallas kernels  11.8 us (29%)
  waiting for transfers between devices  7.75 us (19%)
  local copies, waits for them, and re-layouts  2.89 us (7%)
  other arithmetic  1.52 us (4%)
  between operations  0.88 us (2%)
    ppermute x6, starting transfers between devices, swap(): return lax.ppermute(piece, 'sta', [(i, i ^ j) for i in range(sta_count)])  10.8 us
    pallas_call x3, Pallas kernels, pick_call(): pl.pallas_call(functools.partial(pick_kernel, start, group), out_shape=ja...  5.32 us
    ppermute x3, waiting for transfers between devices, banded(): lax.ppermute(sums, 'sta', [(i, i ^ step) for i in range(lax.axis_size('st...  4.43 us
    pallas_call x1, Pallas kernels, own_call(): pl.pallas_call(functools.partial(own_kernel, each), out_shape=(jax.ShapeD...  3.13 us
    ppermute x6, waiting for transfers between devices, swap(): return lax.ppermute(piece, 'sta', [(i, i ^ j) for i in range(sta_count)])  2.76 us
    ppermute x2, starting transfers between devices, swapped(): return lax.ppermute(half, 'evt', links + [(j, i) for i, j in links])  2.58 us
    ppermute x3, starting transfers between devices, banded(): lax.ppermute(sums, 'sta', [(i, i ^ step) for i in range(lax.axis_size('st...  2.11 us
    unnamed x4, local copies, waits for them, and re-layouts  1.74 us
  transfers between devices with their start and end apart: 11, of which 6 were waited for; matrix products, arithmetic and copies ran while one was open for 2% of the time, Pallas kernels for 25%

profile of v6, /device:TPU:4, one launch (start us, length us, event | category | flops | bytes accessed | tf_op | source)
XLA Modules:
  0.0 40.4 jit_solution(16025641474007389474)
XLA Ops:
  0.7 1.1 %dynamic-slice_bitcast_fusion.7 = (bf16[4,8,1024]{2,1,0:T(8,128)(2,1)S(1)}, bf16[4,8,1024]{2,1,0:T(8,128)(2,1)S(1)}, bf16[4,8,1024]{2,1,0:T(8,128)(2,1)S(1)}, bf...) fusion(bf16[4,8,8,1024]{3,2,1,0:T(8,128)(2,1)} %bitcast.38, ...), kind=kLoop, calls=%fused_computation.16 | loop fusion | bytes 1048608 | tf_op jit(solution)/shard_map/jit(dynamic_index_in_dim)/squeeze | solution.py:133
  1.8 0.0 copy-start.1
  1.8 1.6 %collective-permute-start = (bf16[2,4,8,1024]{3,2,1,0:T(8,128)(2,1)S(1)}, bf16[2,4,8,1024]{3,2,1,0:T(8,128)(2,1)S(1)}, u32[]{:S(2)}, u32[]{:S(2)}) collective-permute-start(bf16[2,4,8,1024]{3,2,1,0:T(8,128)(2,1)S(1)} %pad_maximum_fusion), channel_id=1, source_target_pairs={{0,8},{4,12},{8,0},{12,4},{16,24},{20,28},{24,16},{28,20},{1,9},{5... | collective-permute-start | bytes 393224 | tf_op jit(solution)/shard_map/ppermute | solution.py:136
  3.5 3.4 %collective-permute-start.5 = (bf16[4,8,1024]{2,1,0:T(8,128)(2,1)S(1)}, bf16[4,8,1024]{2,1,0:T(8,128)(2,1)S(1)}, u32[]{:S(2)}, u32[]{:S(2)}) collective-permute-start(bf16[4,8,1024]{2,1,0:T(8,128)(2,1)S(1)} %get-tuple-element.51), channel_id=1, source_target_pairs={{0,28},{4,24},{8,20},{12,16},{16,12},{20,8},{24,4},{28,0},{1,29},{... | collective-permute-start | bytes 196616 | tf_op jit(solution)/shard_map/ppermute | solution.py:136
  6.9 1.3 %collective-permute-start.4 = (bf16[4,8,1024]{2,1,0:T(8,128)(2,1)S(1)}, bf16[4,8,1024]{2,1,0:T(8,128)(2,1)S(1)}, u32[]{:S(2)}, u32[]{:S(2)}) collective-permute-start(bf16[4,8,1024]{2,1,0:T(8,128)(2,1)S(1)} %get-tuple-element.52), channel_id=1, source_target_pairs={{0,24},{4,28},{8,16},{12,20},{16,8},{20,12},{24,0},{28,4},{1,25},{... | collective-permute-start | bytes 196616 | tf_op jit(solution)/shard_map/ppermute | solution.py:136
  8.2 0.8 %collective-permute-start.3 = (bf16[4,8,1024]{2,1,0:T(8,128)(2,1)S(1)}, bf16[4,8,1024]{2,1,0:T(8,128)(2,1)S(1)}, u32[]{:S(2)}, u32[]{:S(2)}) collective-permute-start(bf16[4,8,1024]{2,1,0:T(8,128)(2,1)S(1)} %get-tuple-element.53), channel_id=1, source_target_pairs={{0,20},{4,16},{8,28},{12,24},{16,4},{20,0},{24,12},{28,8},{1,21},{... | collective-permute-start | bytes 196616 | tf_op jit(solution)/shard_map/ppermute | solution.py:136
  9.0 2.1 %collective-permute-start.2 = (bf16[4,8,1024]{2,1,0:T(8,128)(2,1)S(1)}, bf16[4,8,1024]{2,1,0:T(8,128)(2,1)S(1)}, u32[]{:S(2)}, u32[]{:S(2)}) collective-permute-start(bf16[4,8,1024]{2,1,0:T(8,128)(2,1)S(1)} %get-tuple-element.54), channel_id=1, source_target_pairs={{0,16},{4,20},{8,24},{12,28},{16,0},{20,4},{24,8},{28,12},{1,17},{... | collective-permute-start | bytes 196616 | tf_op jit(solution)/shard_map/ppermute | solution.py:136
  11.1 0.0 collective-permute-done
  11.2 1.6 %collective-permute-start.1 = (bf16[8,8,1024]{2,1,0:T(8,128)(2,1)S(1)}, bf16[8,8,1024]{2,1,0:T(8,128)(2,1)S(1)}, u32[]{:S(2)}, u32[]{:S(2)}) collective-permute-start(bf16[8,8,1024]{2,1,0:T(8,128)(2,1)S(1)} %pad_maximum_fusion.1), channel_id=1, source_target_pairs={{0,4},{4,0},{8,12},{12,8},{16,20},{20,16},{24,28},{28,24},{1,5},{5... | collective-permute-start | bytes 393224 | tf_op jit(solution)/shard_map/ppermute | solution.py:136
  12.7 0.7 %pad_add_fusion.packed_ref = s32[11,1024]{1,0:T(8,128)S(1)} fusion(s32[8,128]{1,0:T(8,128)} %bitcast.40, s32[1,1024]{1,0:T(1,128)} %bitcast.41, s32[2,1024]{1,0:T(2,128)} %bitcast.39), kind=kLoop, calls=%fused_computation.6 | loop fusion | flops 22528 | bytes 61440 | tf_op jit(solution)/shard_map/concatenate | solution.py:396
  13.5 0.2 shard_map.77
  13.7 0.0 collective-permute-done.5
  13.7 0.0 copy-start
  13.7 1.7 %copy-done = bf16[1024,1280]{1,0:T(8,128)(2,1)S(1)} copy-done((bf16[1024,1280]{1,0:T(8,128)(2,1)S(1)}, bf16[1024,1280]{1,0:T(8,128)(2,1)}, u32[]{:S(2)}) %copy-start) | copy-done | bytes 2621464
  15.5 0.2 shard_map.78.tables_ref
  15.7 0.0 collective-permute-done.4
  15.7 2.4 %collective-permute-done.3 = bf16[4,8,1024]{2,1,0:T(8,128)(2,1)S(1)} collective-permute-done((bf16[4,8,1024]{2,1,0:T(8,128)(2,1)S(1)}, bf16[4,8,1024]{2,1,0:T(8,128)(2,1)S(1)}, u32[]{:S(2)}, u32[]{:S(2)}) %collective-permute-start.3) | collective-permute-done | bytes 65568 | tf_op jit(solution)/shard_map/ppermute | solution.py:136
  18.1 0.3 collective-permute-done.2
  18.5 0.0 collective-permute-done.1
  18.5 0.1 broadcast_select_fusion
  18.6 0.1 collective-permute-start.7
  18.6 2.5 %collective-permute-start.6 = (bf16[128,1024]{1,0:T(8,128)(2,1)S(1)}, bf16[128,1024]{1,0:T(8,128)(2,1)S(1)}, u32[]{:S(2)}, u32[]{:S(2)}) collective-permute-start(bf16[128,1024]{1,0:T(8,128)(2,1)S(1)} %get-tuple-element.49), channel_id=1, source_target_pairs={{1,2},{2,1},{5,6},{6,5},{9,10},{10,9},{13,14},{14,13},{17,18},{18,... | collective-permute-start | bytes 786440 | tf_op jit(solution)/shard_map/ppermute | solution.py:540
  21.2 0.0 copy-done.1
  21.2 3.1 %shard_map.79 = (f32[32,8,1024]{2,1,0:T(8,128)S(1)}, bf16[1032,8,256]{2,1,0:T(8,128)(2,1)S(1)}, f32[8,1152]{1,0:T(8,128)S(1)}) custom-call(bf16[128,1024]{1,0:T(8,128)(2,1)S(1)} %maximum_bitcast_fusion.near_ref, bf16[128,1024]{1,0:T(8,128)(2,1)S(1)} %maximum_bitcast_fusion.1.far_ref, f32[64,8,128]{2,1,0:T(8,128)S(1)} %get-tuple-element.31.presence_ref, ...), custom_call_target="tpu_custom_call" | custom-call | flops 2113929216 | bytes 8000000 | tf_op jit(solution)/shard_map/pallas_call | solution.py:432
  24.3 0.0 collective-permute-done.7.halo_ref
  24.4 1.4 %shard_map.80 = (bf16[1032,8,256]{2,1,0:T(8,128)(2,1)S(1)}, f32[8,1152]{1,0:T(8,128)S(1)}) custom-call(bf16[128,1024]{1,0:T(8,128)(2,1)S(1)} %collective-permute-done.7.halo_ref, f32[32,8,1024]{2,1,0:T(8,128)S(1)} %get-tuple-element.33.own_ref, f32[64,8,128]{2,1,0:T(8,128)S(1)} %get-tuple-element.31.presence_ref, ...), custom_call_target="tpu_custom_call", output_to_operand_aliasing={{0}: (6, {})} | custom-call | flops 838860800 | bytes 4000000 | tf_op jit(solution)/shard_map/pallas_call | solution.py:453
  25.8 0.6 %collective-permute-done.6.halo_ref = bf16[128,1024]{1,0:T(8,128)(2,1)S(1)} collective-permute-done((bf16[128,1024]{1,0:T(8,128)(2,1)S(1)}, bf16[128,1024]{1,0:T(8,128)(2,1)S(1)}, u32[]{:S(2)}, u32[]{:S(2)}) %collective-permute-start.6) | collective-permute-done | bytes 262176 | tf_op jit(solution)/shard_map/ppermute | solution.py:540
  26.3 1.5 %shard_map.81 = (bf16[1032,8,256]{2,1,0:T(8,128)(2,1)S(1)}, f32[2,8,128]{2,1,0:T(8,128)S(1)}) custom-call(bf16[128,1024]{1,0:T(8,128)(2,1)S(1)} %collective-permute-done.6.halo_ref, f32[32,8,1024]{2,1,0:T(8,128)S(1)} %get-tuple-element.33.own_ref, f32[64,8,128]{2,1,0:T(8,128)S(1)} %get-tuple-element.31.presence_ref, ...), custom_call_target="tpu_custom_call", output_to_operand_aliasing={{0}: (8, {})} | custom-call | flops 838860800 | bytes 4000000 | tf_op jit(solution)/shard_map/pallas_call | solution.py:477
  27.9 0.2 collective-permute-start.8
  28.0 1.8 %shard_map.82.refs_0_ = bf16[1024,8,256]{2,1,0:T(8,128)(2,1)} custom-call(s32[1024]{0:T(1024)S(1)} %bitcast.35, bf16[1032,8,256]{2,1,0:T(8,128)(2,1)S(1)} %get-tuple-element.41.table_ref), custom_call_target="tpu_custom_call" | custom-call | bytes 7680000 | tf_op jit(solution)/shard_map/pallas_call | solution.py:498
  29.9 2.6 %collective-permute-done.8 = f32[2,8,128]{2,1,0:T(8,128)S(1)} collective-permute-done((f32[2,8,128]{2,1,0:T(8,128)S(1)}, f32[2,8,128]{2,1,0:T(8,128)S(1)}, u32[]{:S(2)}, u32[]{:S(2)}) %collective-permute-start.8) | collective-permute-done | bytes 8224 | tf_op jit(solution)/shard_map/ppermute | solution.py:554
  32.4 0.8 %collective-permute-start.9 = (f32[2,8,128]{2,1,0:T(8,128)S(1)}, f32[2,8,128]{2,1,0:T(8,128)S(1)}, u32[]{:S(2)}, u32[]{:S(2)}) collective-permute-start(f32[2,8,128]{2,1,0:T(8,128)S(1)} %add.49), channel_id=1, source_target_pairs={{0,8},{4,12},{8,0},{12,4},{16,24},{20,28},{24,16},{28,20},{1,9},{5... | collective-permute-start | bytes 24584 | tf_op jit(solution)/shard_map/ppermute | solution.py:554
  33.2 1.8 %shard_map.83.refs_0_ = bf16[1024,8,256]{2,1,0:T(8,128)(2,1)} custom-call(s32[1024]{0:T(1024)S(1)} %bitcast.36, bf16[1032,8,256]{2,1,0:T(8,128)(2,1)S(1)} %get-tuple-element.41.table_ref, bf16[1024,8,256]{2,1,0:T(8,128)(2,1)} %shard_map.82.refs_0_), custom_call_target="tpu_custom_call", output_to_operand_aliasing={{}: (2, {})} | custom-call | bytes 7680000 | tf_op jit(solution)/shard_map/pallas_call | solution.py:498
  35.1 1.0 %collective-permute-done.9 = f32[2,8,128]{2,1,0:T(8,128)S(1)} collective-permute-done((f32[2,8,128]{2,1,0:T(8,128)S(1)}, f32[2,8,128]{2,1,0:T(8,128)S(1)}, u32[]{:S(2)}, u32[]{:S(2)}) %collective-permute-start.9) | collective-permute-done | bytes 8224 | tf_op jit(solution)/shard_map/ppermute | solution.py:554
  36.1 1.2 %collective-permute-start.10 = (f32[2,8,128]{2,1,0:T(8,128)S(1)}, f32[2,8,128]{2,1,0:T(8,128)S(1)}, u32[]{:S(2)}, u32[]{:S(2)}) collective-permute-start(f32[2,8,128]{2,1,0:T(8,128)S(1)} %add.50), channel_id=1, source_target_pairs={{0,4},{4,0},{8,12},{12,8},{16,20},{20,16},{24,28},{28,24},{1,5},{5... | collective-permute-start | bytes 24584 | tf_op jit(solution)/shard_map/ppermute | solution.py:554
  37.3 1.6 %shard_map.84 = bf16[1024,8,256]{2,1,0:T(8,128)(2,1)} custom-call(s32[1024]{0:T(1024)S(1)} %bitcast.37, bf16[1032,8,256]{2,1,0:T(8,128)(2,1)S(1)} %get-tuple-element.41.table_ref, bf16[1024,8,256]{2,1,0:T(8,128)(2,1)} %shard_map.83.refs_0_), custom_call_target="tpu_custom_call", output_to_operand_aliasing={{}: (2, {})} | custom-call | bytes 5120000 | tf_op jit(solution)/shard_map/pallas_call | solution.py:498
  38.9 0.8 %collective-permute-done.10 = f32[2,8,128]{2,1,0:T(8,128)S(1)} collective-permute-done((f32[2,8,128]{2,1,0:T(8,128)S(1)}, f32[2,8,128]{2,1,0:T(8,128)S(1)}, u32[]{:S(2)}, u32[]{:S(2)}) %collective-permute-start.10) | collective-permute-done | bytes 8224 | tf_op jit(solution)/shard_map/ppermute | solution.py:554
  39.7 0.6 %divide_bitcast_fusion = f32[1024]{0:T(1024)} fusion(f32[2,8,128]{2,1,0:T(8,128)S(1)} %add.51), kind=kLoop, calls=%fused_computation.17 | loop fusion | flops 2048 | bytes 12288 | tf_op jit(solution)/shard_map/div | solution.py:597
  (9 shorter events, 0.1 us)
Async XLA Ops:
  1.8 19.4 %copy-start.1 = (f32[1,1024]{1,0:T(1,128)S(1)}, f32[1,1024]{1,0:T(1,128)}, u32[]{:S(2)}) copy-start(f32[1,1024]{1,0:T(1,128)} %constant.62.clone.weights_ref) | copy-start | bytes 12292
  1.8 9.3 %collective-permute-start = (bf16[2,4,8,1024]{3,2,1,0:T(8,128)(2,1)S(1)}, bf16[2,4,8,1024]{3,2,1,0:T(8,128)(2,1)S(1)}, u32[]{:S(2)}, u32[]{:S(2)}) collective-permute-start(bf16[2,4,8,1024]{3,2,1,0:T(8,128)(2,1)S(1)} %pad_maximum_fusion), channel_id=1, source_target_pairs={{0,8},{4,12},{8,0},{12,4},{16,24},{20,28},{24,16},{28,20},{1,9},{5... | collective-permute-start | bytes 393224 | tf_op jit(solution)/shard_map/ppermute | solution.py:136
  3.5 10.2 %collective-permute-start.5 = (bf16[4,8,1024]{2,1,0:T(8,128)(2,1)S(1)}, bf16[4,8,1024]{2,1,0:T(8,128)(2,1)S(1)}, u32[]{:S(2)}, u32[]{:S(2)}) collective-permute-start(bf16[4,8,1024]{2,1,0:T(8,128)(2,1)S(1)} %get-tuple-element.51), channel_id=1, source_target_pairs={{0,28},{4,24},{8,20},{12,16},{16,12},{20,8},{24,4},{28,0},{1,29},{... | collective-permute-start | bytes 196616 | tf_op jit(solution)/shard_map/ppermute | solution.py:136
  6.9 8.8 %collective-permute-start.4 = (bf16[4,8,1024]{2,1,0:T(8,128)(2,1)S(1)}, bf16[4,8,1024]{2,1,0:T(8,128)(2,1)S(1)}, u32[]{:S(2)}, u32[]{:S(2)}) collective-permute-start(bf16[4,8,1024]{2,1,0:T(8,128)(2,1)S(1)} %get-tuple-element.52), channel_id=1, source_target_pairs={{0,24},{4,28},{8,16},{12,20},{16,8},{20,12},{24,0},{28,4},{1,25},{... | collective-permute-start | bytes 196616 | tf_op jit(solution)/shard_map/ppermute | solution.py:136
  8.2 9.9 %collective-permute-start.3 = (bf16[4,8,1024]{2,1,0:T(8,128)(2,1)S(1)}, bf16[4,8,1024]{2,1,0:T(8,128)(2,1)S(1)}, u32[]{:S(2)}, u32[]{:S(2)}) collective-permute-start(bf16[4,8,1024]{2,1,0:T(8,128)(2,1)S(1)} %get-tuple-element.53), channel_id=1, source_target_pairs={{0,20},{4,16},{8,28},{12,24},{16,4},{20,0},{24,12},{28,8},{1,21},{... | collective-permute-start | bytes 196616 | tf_op jit(solution)/shard_map/ppermute | solution.py:136
  9.0 9.4 %collective-permute-start.2 = (bf16[4,8,1024]{2,1,0:T(8,128)(2,1)S(1)}, bf16[4,8,1024]{2,1,0:T(8,128)(2,1)S(1)}, u32[]{:S(2)}, u32[]{:S(2)}) collective-permute-start(bf16[4,8,1024]{2,1,0:T(8,128)(2,1)S(1)} %get-tuple-element.54), channel_id=1, source_target_pairs={{0,16},{4,20},{8,24},{12,28},{16,0},{20,4},{24,8},{28,12},{1,17},{... | collective-permute-start | bytes 196616 | tf_op jit(solution)/shard_map/ppermute | solution.py:136
  11.2 7.3 %collective-permute-start.1 = (bf16[8,8,1024]{2,1,0:T(8,128)(2,1)S(1)}, bf16[8,8,1024]{2,1,0:T(8,128)(2,1)S(1)}, u32[]{:S(2)}, u32[]{:S(2)}) collective-permute-start(bf16[8,8,1024]{2,1,0:T(8,128)(2,1)S(1)} %pad_maximum_fusion.1), channel_id=1, source_target_pairs={{0,4},{4,0},{8,12},{12,8},{16,20},{20,16},{24,28},{28,24},{1,5},{5... | collective-permute-start | bytes 393224 | tf_op jit(solution)/shard_map/ppermute | solution.py:136
  13.7 1.7 %copy-start = (bf16[1024,1280]{1,0:T(8,128)(2,1)S(1)}, bf16[1024,1280]{1,0:T(8,128)(2,1)}, u32[]{:S(2)}) copy-start(bf16[1024,1280]{1,0:T(8,128)(2,1)} %constant.61.clone.tables_ref) | copy-start | bytes 7864324
  18.6 5.8 %collective-permute-start.7 = (bf16[128,1024]{1,0:T(8,128)(2,1)S(1)}, bf16[128,1024]{1,0:T(8,128)(2,1)S(1)}, u32[]{:S(2)}, u32[]{:S(2)}) collective-permute-start(bf16[128,1024]{1,0:T(8,128)(2,1)S(1)} %get-tuple-element.48), channel_id=1, source_target_pairs={{0,1},{2,3},{1,0},{3,2},{4,5},{6,7},{5,4},{7,6},{8,9},{10,11},{9,8... | collective-permute-start | bytes 786440 | tf_op jit(solution)/shard_map/ppermute | solution.py:540
  18.6 7.7 %collective-permute-start.6 = (bf16[128,1024]{1,0:T(8,128)(2,1)S(1)}, bf16[128,1024]{1,0:T(8,128)(2,1)S(1)}, u32[]{:S(2)}, u32[]{:S(2)}) collective-permute-start(bf16[128,1024]{1,0:T(8,128)(2,1)S(1)} %get-tuple-element.49), channel_id=1, source_target_pairs={{1,2},{2,1},{5,6},{6,5},{9,10},{10,9},{13,14},{14,13},{17,18},{18,... | collective-permute-start | bytes 786440 | tf_op jit(solution)/shard_map/ppermute | solution.py:540
  27.9 4.6 %collective-permute-start.8 = (f32[2,8,128]{2,1,0:T(8,128)S(1)}, f32[2,8,128]{2,1,0:T(8,128)S(1)}, u32[]{:S(2)}, u32[]{:S(2)}) collective-permute-start(f32[2,8,128]{2,1,0:T(8,128)S(1)} %get-tuple-element.40), channel_id=1, source_target_pairs={{0,16},{4,20},{8,24},{12,28},{16,0},{20,4},{24,8},{28,12},{1,17},{... | collective-permute-start | bytes 24584 | tf_op jit(solution)/shard_map/ppermute | solution.py:554
  32.4 3.7 %collective-permute-start.9 = (f32[2,8,128]{2,1,0:T(8,128)S(1)}, f32[2,8,128]{2,1,0:T(8,128)S(1)}, u32[]{:S(2)}, u32[]{:S(2)}) collective-permute-start(f32[2,8,128]{2,1,0:T(8,128)S(1)} %add.49), channel_id=1, source_target_pairs={{0,8},{4,12},{8,0},{12,4},{16,24},{20,28},{24,16},{28,20},{1,9},{5... | collective-permute-start | bytes 24584 | tf_op jit(solution)/shard_map/ppermute | solution.py:554
  36.1 3.7 %collective-permute-start.10 = (f32[2,8,128]{2,1,0:T(8,128)S(1)}, f32[2,8,128]{2,1,0:T(8,128)S(1)}, u32[]{:S(2)}, u32[]{:S(2)}) collective-permute-start(f32[2,8,128]{2,1,0:T(8,128)S(1)} %add.50), channel_id=1, source_target_pairs={{0,4},{4,0},{8,12},{12,8},{16,20},{20,16},{24,28},{28,24},{1,5},{5... | collective-permute-start | bytes 24584 | tf_op jit(solution)/shard_map/ppermute | solution.py:554

commit v7 on v6

--- a/solution.py
+++ b/solution.py
@@ -547,17 +547,18 @@
     table, sums = last_call(second_halo, own, held, tables, peaks, row, count, table, each)
 
     row = row.reshape(-1)
-    groups = row.shape[0] // LANES
-    correlation = ()
-    step, skip = lax.axis_size("sta") // 2, 0
-    while step:
-        arrived = lax.ppermute(sums, "sta", [(i, i ^ step) for i in range(lax.axis_size("sta"))])
-        steps = -(-(groups - skip) // step.bit_length())
-        correlation = (pick_call(row, table, correlation, skip * LANES, steps * LANES),)
-        sums, correlation = lax.optimization_barrier((sums + arrived, correlation))
-        skip += steps
-        step //= 2
-    return correlation[0], sums
+    sta_count = lax.axis_size("sta")
+
+    def from_station(j):
+        return lax.ppermute(sums, "sta", [(i, i ^ j) for i in range(sta_count)])
+
+    split = row.shape[0] * 4 // 8
+    beside, across, aslant = from_station(1), from_station(2), from_station(3)
+    correlation = pick_call(row, table, (), 0, split)
+    sums, correlation = lax.optimization_barrier(((sums + beside) + (across + aslant), correlation))
+    arrived = from_station(4)
+    correlation = pick_call(row, table, (correlation,), split, row.shape[0] - split)
+    return correlation, sums + arrived
 
 
 def by_slot(waveforms, pair_events, pair_valid, presence, block):

time: 40.6 us -> 39.6 us (0.975)
  starting transfers between devices: 15.5 us -> 18 us
  waiting for transfers between devices: 7.75 us -> 5.52 us
  Pallas kernels: 11.8 us -> 10.5 us
    ppermute x3 -> x4, starting transfers between devices: 2.11 us -> 4.59 us  [from_station(): return lax.ppermute(sums, 'sta', [(i, i ^ j) for i in range(sta_count)])]
    ppermute x3 -> x4, waiting for transfers between devices: 4.43 us -> 2.2 us  [from_station(): return lax.ppermute(sums, 'sta', [(i, i ^ j) for i in range(sta_count)])]
    pallas_call x3 -> x2, Pallas kernels: 5.32 us -> 4.05 us  [pick_call(): pl.pallas_call(functools.partial(pick_kernel, start, group), out_shape=ja...]
  transfers between devices with their start and end apart: 11 -> 12, of which waited for: 6 -> 5; matrix products, arithmetic and copies ran while one was open for 2% -> 2% of each run, Pallas kernels for 25% -> 23%
where the time goes in v7:
time: 39.6 us; the launch traced here: 39.4 us
  starting transfers between devices  18 us (45%)
  Pallas kernels  10.5 us (27%)
  waiting for transfers between devices  5.52 us (14%)
  local copies, waits for them, and re-layouts  2.89 us (7%)
  other arithmetic  1.52 us (4%)
  between operations  0.89 us (2%)
    ppermute x6, starting transfers between devices, swap(): return lax.ppermute(piece, 'sta', [(i, i ^ j) for i in range(sta_count)])  10.8 us
    ppermute x4, starting transfers between devices, from_station(): return lax.ppermute(sums, 'sta', [(i, i ^ j) for i in range(sta_count)])  4.59 us
    pallas_call x2, Pallas kernels, pick_call(): pl.pallas_call(functools.partial(pick_kernel, start, group), out_shape=ja...  4.05 us
    pallas_call x1, Pallas kernels, own_call(): pl.pallas_call(functools.partial(own_kernel, each), out_shape=(jax.ShapeD...  3.13 us
    ppermute x6, waiting for transfers between devices, swap(): return lax.ppermute(piece, 'sta', [(i, i ^ j) for i in range(sta_count)])  2.76 us
    ppermute x2, starting transfers between devices, swapped(): return lax.ppermute(half, 'evt', links + [(j, i) for i, j in links])  2.58 us
    ppermute x4, waiting for transfers between devices, from_station(): return lax.ppermute(sums, 'sta', [(i, i ^ j) for i in range(sta_count)])  2.2 us
    unnamed x4, local copies, waits for them, and re-layouts  1.74 us
  transfers between devices with their start and end apart: 12, of which 5 were waited for; matrix products, arithmetic and copies ran while one was open for 2% of the time, Pallas kernels for 23%

profile of v7, /device:TPU:4, one launch (start us, length us, event | category | flops | bytes accessed | tf_op | source)
XLA Modules:
  0.0 39.4 jit_solution(14229603781896595183)
XLA Ops:
  0.7 1.1 %dynamic-slice_bitcast_fusion.3 = (bf16[4,8,1024]{2,1,0:T(8,128)(2,1)S(1)}, bf16[1,4,8,1024]{3,2,1,0:T(8,128)(2,1)S(1)}, bf16[1,4,8,1024]{3,2,1,0:T(8,128)(2,1)S...) fusion(bf16[4,8,8,1024]{3,2,1,0:T(8,128)(2,1)} %bitcast.37, ...), kind=kLoop, calls=%fused_computation.12 | loop fusion | bytes 1048608 | tf_op jit(solution)/shard_map/jit(dynamic_index_in_dim)/squeeze | solution.py:133
  1.8 0.0 copy-start.1
  1.8 1.6 %collective-permute-start.4 = (bf16[2,4,8,1024]{3,2,1,0:T(8,128)(2,1)S(1)}, bf16[2,4,8,1024]{3,2,1,0:T(8,128)(2,1)S(1)}, u32[]{:S(2)}, u32[]{:S(2)}) collective-permute-start(bf16[2,4,8,1024]{3,2,1,0:T(8,128)(2,1)S(1)} %pad_maximum_fusion), channel_id=1, source_target_pairs={{0,8},{4,12},{8,0},{12,4},{16,24},{20,28},{24,16},{28,20},{1,9},{5... | collective-permute-start | bytes 393224 | tf_op jit(solution)/shard_map/ppermute | solution.py:136
  3.5 3.4 %collective-permute-start.3 = (bf16[4,8,1024]{2,1,0:T(8,128)(2,1)S(1)}, bf16[4,8,1024]{2,1,0:T(8,128)(2,1)S(1)}, u32[]{:S(2)}, u32[]{:S(2)}) collective-permute-start(bf16[4,8,1024]{2,1,0:T(8,128)(2,1)S(1)} %get-tuple-element.46), channel_id=1, source_target_pairs={{0,28},{4,24},{8,20},{12,16},{16,12},{20,8},{24,4},{28,0},{1,29},{... | collective-permute-start | bytes 196616 | tf_op jit(solution)/shard_map/ppermute | solution.py:136
  6.9 1.3 %collective-permute-start.2 = (bf16[4,8,1024]{2,1,0:T(8,128)(2,1)S(1)}, bf16[4,8,1024]{2,1,0:T(8,128)(2,1)S(1)}, u32[]{:S(2)}, u32[]{:S(2)}) collective-permute-start(bf16[4,8,1024]{2,1,0:T(8,128)(2,1)S(1)} %get-tuple-element.47), channel_id=1, source_target_pairs={{0,24},{4,28},{8,16},{12,20},{16,8},{20,12},{24,0},{28,4},{1,25},{... | collective-permute-start | bytes 196616 | tf_op jit(solution)/shard_map/ppermute | solution.py:136
  8.2 0.8 %collective-permute-start.1 = (bf16[4,8,1024]{2,1,0:T(8,128)(2,1)S(1)}, bf16[4,8,1024]{2,1,0:T(8,128)(2,1)S(1)}, u32[]{:S(2)}, u32[]{:S(2)}) collective-permute-start(bf16[4,8,1024]{2,1,0:T(8,128)(2,1)S(1)} %get-tuple-element.48), channel_id=1, source_target_pairs={{0,20},{4,16},{8,28},{12,24},{16,4},{20,0},{24,12},{28,8},{1,21},{... | collective-permute-start | bytes 196616 | tf_op jit(solution)/shard_map/ppermute | solution.py:136
  9.0 2.1 %collective-permute-start = (bf16[4,8,1024]{2,1,0:T(8,128)(2,1)S(1)}, bf16[4,8,1024]{2,1,0:T(8,128)(2,1)S(1)}, u32[]{:S(2)}, u32[]{:S(2)}) collective-permute-start(bf16[4,8,1024]{2,1,0:T(8,128)(2,1)S(1)} %get-tuple-element.49), channel_id=1, source_target_pairs={{0,16},{4,20},{8,24},{12,28},{16,0},{20,4},{24,8},{28,12},{1,17},{... | collective-permute-start | bytes 196616 | tf_op jit(solution)/shard_map/ppermute | solution.py:136
  11.1 0.0 collective-permute-done.4
  11.2 1.6 %collective-permute-start.5 = (bf16[8,8,1024]{2,1,0:T(8,128)(2,1)S(1)}, bf16[8,8,1024]{2,1,0:T(8,128)(2,1)S(1)}, u32[]{:S(2)}, u32[]{:S(2)}) collective-permute-start(bf16[8,8,1024]{2,1,0:T(8,128)(2,1)S(1)} %pad_maximum_fusion.1), channel_id=1, source_target_pairs={{0,4},{4,0},{8,12},{12,8},{16,20},{20,16},{24,28},{28,24},{1,5},{5... | collective-permute-start | bytes 393224 | tf_op jit(solution)/shard_map/ppermute | solution.py:136
  12.7 0.7 %pad_add_fusion.packed_ref = s32[11,1024]{1,0:T(8,128)S(1)} fusion(s32[8,128]{1,0:T(8,128)} %bitcast.39, s32[1,1024]{1,0:T(1,128)} %bitcast.40, s32[2,1024]{1,0:T(2,128)} %bitcast.38), kind=kLoop, calls=%fused_computation.8 | loop fusion | flops 22528 | bytes 61440 | tf_op jit(solution)/shard_map/concatenate | solution.py:396
  13.5 0.2 shard_map.77
  13.7 0.0 collective-permute-done.3
  13.7 0.0 copy-start
  13.7 1.7 %copy-done = bf16[1024,1280]{1,0:T(8,128)(2,1)S(1)} copy-done((bf16[1024,1280]{1,0:T(8,128)(2,1)S(1)}, bf16[1024,1280]{1,0:T(8,128)(2,1)}, u32[]{:S(2)}) %copy-start) | copy-done | bytes 2621464
  15.5 0.2 shard_map.78.tables_ref
  15.7 0.0 collective-permute-done.2
  15.7 2.4 %collective-permute-done.1 = bf16[4,8,1024]{2,1,0:T(8,128)(2,1)S(1)} collective-permute-done((bf16[4,8,1024]{2,1,0:T(8,128)(2,1)S(1)}, bf16[4,8,1024]{2,1,0:T(8,128)(2,1)S(1)}, u32[]{:S(2)}, u32[]{:S(2)}) %collective-permute-start.1) | collective-permute-done | bytes 65568 | tf_op jit(solution)/shard_map/ppermute | solution.py:136
  18.1 0.3 collective-permute-done
  18.5 0.0 collective-permute-done.5
  18.5 0.1 broadcast_select_fusion
  18.6 0.1 collective-permute-start.7
  18.6 2.5 %collective-permute-start.6 = (bf16[128,1024]{1,0:T(8,128)(2,1)S(1)}, bf16[128,1024]{1,0:T(8,128)(2,1)S(1)}, u32[]{:S(2)}, u32[]{:S(2)}) collective-permute-start(bf16[128,1024]{1,0:T(8,128)(2,1)S(1)} %get-tuple-element.41), channel_id=1, source_target_pairs={{1,2},{2,1},{5,6},{6,5},{9,10},{10,9},{13,14},{14,13},{17,18},{18,... | collective-permute-start | bytes 786440 | tf_op jit(solution)/shard_map/ppermute | solution.py:540
  21.2 0.0 copy-done.1
  21.2 3.1 %shard_map.79 = (f32[32,8,1024]{2,1,0:T(8,128)S(1)}, bf16[1032,8,256]{2,1,0:T(8,128)(2,1)S(1)}, f32[8,1152]{1,0:T(8,128)S(1)}) custom-call(bf16[128,1024]{1,0:T(8,128)(2,1)S(1)} %maximum_bitcast_fusion.1.near_ref, bf16[128,1024]{1,0:T(8,128)(2,1)S(1)} %maximum_bitcast_fusion.far_ref, f32[64,8,128]{2,1,0:T(8,128)S(1)} %get-tuple-element.28.presence_ref, ...), custom_call_target="tpu_custom_call" | custom-call | flops 2113929216 | bytes 8000000 | tf_op jit(solution)/shard_map/pallas_call | solution.py:432
  24.3 0.0 collective-permute-done.7.halo_ref
  24.4 1.4 %shard_map.80 = (bf16[1032,8,256]{2,1,0:T(8,128)(2,1)S(1)}, f32[8,1152]{1,0:T(8,128)S(1)}) custom-call(bf16[128,1024]{1,0:T(8,128)(2,1)S(1)} %collective-permute-done.7.halo_ref, f32[32,8,1024]{2,1,0:T(8,128)S(1)} %get-tuple-element.30.own_ref, f32[64,8,128]{2,1,0:T(8,128)S(1)} %get-tuple-element.28.presence_ref, ...), custom_call_target="tpu_custom_call", output_to_operand_aliasing={{0}: (6, {})} | custom-call | flops 838860800 | bytes 4000000 | tf_op jit(solution)/shard_map/pallas_call | solution.py:453
  25.8 0.6 %collective-permute-done.6.halo_ref = bf16[128,1024]{1,0:T(8,128)(2,1)S(1)} collective-permute-done((bf16[128,1024]{1,0:T(8,128)(2,1)S(1)}, bf16[128,1024]{1,0:T(8,128)(2,1)S(1)}, u32[]{:S(2)}, u32[]{:S(2)}) %collective-permute-start.6) | collective-permute-done | bytes 262176 | tf_op jit(solution)/shard_map/ppermute | solution.py:540
  26.3 1.5 %shard_map.81 = (bf16[1032,8,256]{2,1,0:T(8,128)(2,1)S(1)}, f32[2,8,128]{2,1,0:T(8,128)S(1)}) custom-call(bf16[128,1024]{1,0:T(8,128)(2,1)S(1)} %collective-permute-done.6.halo_ref, f32[32,8,1024]{2,1,0:T(8,128)S(1)} %get-tuple-element.30.own_ref, f32[64,8,128]{2,1,0:T(8,128)S(1)} %get-tuple-element.28.presence_ref, ...), custom_call_target="tpu_custom_call", output_to_operand_aliasing={{0}: (8, {})} | custom-call | flops 838860800 | bytes 4000000 | tf_op jit(solution)/shard_map/pallas_call | solution.py:477
  27.9 0.0 collective-permute-start.10
  27.9 2.7 %collective-permute-start.9 = (f32[2,8,128]{2,1,0:T(8,128)S(1)}, f32[2,8,128]{2,1,0:T(8,128)S(1)}, u32[]{:S(2)}, u32[]{:S(2)}) collective-permute-start(f32[2,8,128]{2,1,0:T(8,128)S(1)} %get-tuple-element.37), channel_id=1, source_target_pairs={{0,8},{4,12},{8,0},{12,4},{16,24},{20,28},{24,16},{28,20},{1,9},{5... | collective-permute-start | bytes 24584 | tf_op jit(solution)/shard_map/ppermute | solution.py:553
  30.5 0.8 %collective-permute-start.8 = (f32[2,8,128]{2,1,0:T(8,128)S(1)}, f32[2,8,128]{2,1,0:T(8,128)S(1)}, u32[]{:S(2)}, u32[]{:S(2)}) collective-permute-start(f32[2,8,128]{2,1,0:T(8,128)S(1)} %get-tuple-element.37), channel_id=1, source_target_pairs={{0,4},{4,0},{8,12},{12,8},{16,20},{20,16},{24,28},{28,24},{1,5},{5... | collective-permute-start | bytes 24584 | tf_op jit(solution)/shard_map/ppermute | solution.py:553
  31.4 2.0 %shard_map.82.refs_0_ = bf16[1024,8,256]{2,1,0:T(8,128)(2,1)} custom-call(s32[1024]{0:T(1024)S(1)} %bitcast.35, bf16[1032,8,256]{2,1,0:T(8,128)(2,1)S(1)} %get-tuple-element.36.table_ref), custom_call_target="tpu_custom_call" | custom-call | bytes 10240000 | tf_op jit(solution)/shard_map/pallas_call | solution.py:498
  33.4 0.0 collective-permute-done.10
  33.4 0.0 collective-permute-done.9
  33.4 0.8 %collective-permute-done.8 = f32[2,8,128]{2,1,0:T(8,128)S(1)} collective-permute-done((f32[2,8,128]{2,1,0:T(8,128)S(1)}, f32[2,8,128]{2,1,0:T(8,128)S(1)}, u32[]{:S(2)}, u32[]{:S(2)}) %collective-permute-start.8) | collective-permute-done | bytes 8224 | tf_op jit(solution)/shard_map/ppermute | solution.py:553
  34.2 1.1 %collective-permute-start.11 = (f32[2,8,128]{2,1,0:T(8,128)S(1)}, f32[2,8,128]{2,1,0:T(8,128)S(1)}, u32[]{:S(2)}, u32[]{:S(2)}) collective-permute-start(f32[2,8,128]{2,1,0:T(8,128)S(1)} %add_add_fusion), channel_id=1, source_target_pairs={{0,16},{4,20},{8,24},{12,28},{16,0},{20,4},{24,8},{28,12},{1,17},{... | collective-permute-start | bytes 24584 | tf_op jit(solution)/shard_map/ppermute | solution.py:553
  35.3 2.0 %shard_map.83 = bf16[1024,8,256]{2,1,0:T(8,128)(2,1)} custom-call(s32[1024]{0:T(1024)S(1)} %bitcast.36, bf16[1032,8,256]{2,1,0:T(8,128)(2,1)S(1)} %get-tuple-element.36.table_ref, bf16[1024,8,256]{2,1,0:T(8,128)(2,1)} %shard_map.82.refs_0_), custom_call_target="tpu_custom_call", output_to_operand_aliasing={{}: (2, {})} | custom-call | bytes 10240000 | tf_op jit(solution)/shard_map/pallas_call | solution.py:498
  37.3 1.4 %collective-permute-done.11 = f32[2,8,128]{2,1,0:T(8,128)S(1)} collective-permute-done((f32[2,8,128]{2,1,0:T(8,128)S(1)}, f32[2,8,128]{2,1,0:T(8,128)S(1)}, u32[]{:S(2)}, u32[]{:S(2)}) %collective-permute-start.11) | collective-permute-done | bytes 8224 | tf_op jit(solution)/shard_map/ppermute | solution.py:553
  38.7 0.6 %fusion.1 = f32[1024]{0:T(1024)} fusion(f32[2,8,128]{2,1,0:T(8,128)S(1)} %add.55), kind=kLoop, calls=%fused_computation.20 | loop fusion | flops 2048 | bytes 12288 | tf_op jit(solution)/shard_map/div | solution.py:598
  (8 shorter events, 0.1 us)
Async XLA Ops:
  1.8 19.4 %copy-start.1 = (f32[1,1024]{1,0:T(1,128)S(1)}, f32[1,1024]{1,0:T(1,128)}, u32[]{:S(2)}) copy-start(f32[1,1024]{1,0:T(1,128)} %constant.62.clone.weights_ref) | copy-start | bytes 12292
  1.8 9.3 %collective-permute-start.4 = (bf16[2,4,8,1024]{3,2,1,0:T(8,128)(2,1)S(1)}, bf16[2,4,8,1024]{3,2,1,0:T(8,128)(2,1)S(1)}, u32[]{:S(2)}, u32[]{:S(2)}) collective-permute-start(bf16[2,4,8,1024]{3,2,1,0:T(8,128)(2,1)S(1)} %pad_maximum_fusion), channel_id=1, source_target_pairs={{0,8},{4,12},{8,0},{12,4},{16,24},{20,28},{24,16},{28,20},{1,9},{5... | collective-permute-start | bytes 393224 | tf_op jit(solution)/shard_map/ppermute | solution.py:136
  3.5 10.2 %collective-permute-start.3 = (bf16[4,8,1024]{2,1,0:T(8,128)(2,1)S(1)}, bf16[4,8,1024]{2,1,0:T(8,128)(2,1)S(1)}, u32[]{:S(2)}, u32[]{:S(2)}) collective-permute-start(bf16[4,8,1024]{2,1,0:T(8,128)(2,1)S(1)} %get-tuple-element.46), channel_id=1, source_target_pairs={{0,28},{4,24},{8,20},{12,16},{16,12},{20,8},{24,4},{28,0},{1,29},{... | collective-permute-start | bytes 196616 | tf_op jit(solution)/shard_map/ppermute | solution.py:136
  6.9 8.8 %collective-permute-start.2 = (bf16[4,8,1024]{2,1,0:T(8,128)(2,1)S(1)}, bf16[4,8,1024]{2,1,0:T(8,128)(2,1)S(1)}, u32[]{:S(2)}, u32[]{:S(2)}) collective-permute-start(bf16[4,8,1024]{2,1,0:T(8,128)(2,1)S(1)} %get-tuple-element.47), channel_id=1, source_target_pairs={{0,24},{4,28},{8,16},{12,20},{16,8},{20,12},{24,0},{28,4},{1,25},{... | collective-permute-start | bytes 196616 | tf_op jit(solution)/shard_map/ppermute | solution.py:136
  8.2 9.9 %collective-permute-start.1 = (bf16[4,8,1024]{2,1,0:T(8,128)(2,1)S(1)}, bf16[4,8,1024]{2,1,0:T(8,128)(2,1)S(1)}, u32[]{:S(2)}, u32[]{:S(2)}) collective-permute-start(bf16[4,8,1024]{2,1,0:T(8,128)(2,1)S(1)} %get-tuple-element.48), channel_id=1, source_target_pairs={{0,20},{4,16},{8,28},{12,24},{16,4},{20,0},{24,12},{28,8},{1,21},{... | collective-permute-start | bytes 196616 | tf_op jit(solution)/shard_map/ppermute | solution.py:136
  9.0 9.4 %collective-permute-start = (bf16[4,8,1024]{2,1,0:T(8,128)(2,1)S(1)}, bf16[4,8,1024]{2,1,0:T(8,128)(2,1)S(1)}, u32[]{:S(2)}, u32[]{:S(2)}) collective-permute-start(bf16[4,8,1024]{2,1,0:T(8,128)(2,1)S(1)} %get-tuple-element.49), channel_id=1, source_target_pairs={{0,16},{4,20},{8,24},{12,28},{16,0},{20,4},{24,8},{28,12},{1,17},{... | collective-permute-start | bytes 196616 | tf_op jit(solution)/shard_map/ppermute | solution.py:136
  11.2 7.3 %collective-permute-start.5 = (bf16[8,8,1024]{2,1,0:T(8,128)(2,1)S(1)}, bf16[8,8,1024]{2,1,0:T(8,128)(2,1)S(1)}, u32[]{:S(2)}, u32[]{:S(2)}) collective-permute-start(bf16[8,8,1024]{2,1,0:T(8,128)(2,1)S(1)} %pad_maximum_fusion.1), channel_id=1, source_target_pairs={{0,4},{4,0},{8,12},{12,8},{16,20},{20,16},{24,28},{28,24},{1,5},{5... | collective-permute-start | bytes 393224 | tf_op jit(solution)/shard_map/ppermute | solution.py:136
  13.7 1.7 %copy-start = (bf16[1024,1280]{1,0:T(8,128)(2,1)S(1)}, bf16[1024,1280]{1,0:T(8,128)(2,1)}, u32[]{:S(2)}) copy-start(bf16[1024,1280]{1,0:T(8,128)(2,1)} %constant.61.clone.tables_ref) | copy-start | bytes 7864324
  18.6 5.8 %collective-permute-start.7 = (bf16[128,1024]{1,0:T(8,128)(2,1)S(1)}, bf16[128,1024]{1,0:T(8,128)(2,1)S(1)}, u32[]{:S(2)}, u32[]{:S(2)}) collective-permute-start(bf16[128,1024]{1,0:T(8,128)(2,1)S(1)} %get-tuple-element.40), channel_id=1, source_target_pairs={{0,1},{2,3},{1,0},{3,2},{4,5},{6,7},{5,4},{7,6},{8,9},{10,11},{9,8... | collective-permute-start | bytes 786440 | tf_op jit(solution)/shard_map/ppermute | solution.py:540
  18.6 7.7 %collective-permute-start.6 = (bf16[128,1024]{1,0:T(8,128)(2,1)S(1)}, bf16[128,1024]{1,0:T(8,128)(2,1)S(1)}, u32[]{:S(2)}, u32[]{:S(2)}) collective-permute-start(bf16[128,1024]{1,0:T(8,128)(2,1)S(1)} %get-tuple-element.41), channel_id=1, source_target_pairs={{1,2},{2,1},{5,6},{6,5},{9,10},{10,9},{13,14},{14,13},{17,18},{18,... | collective-permute-start | bytes 786440 | tf_op jit(solution)/shard_map/ppermute | solution.py:540
  27.9 5.5 %collective-permute-start.10 = (f32[2,8,128]{2,1,0:T(8,128)S(1)}, f32[2,8,128]{2,1,0:T(8,128)S(1)}, u32[]{:S(2)}, u32[]{:S(2)}) collective-permute-start(f32[2,8,128]{2,1,0:T(8,128)S(1)} %get-tuple-element.37), channel_id=1, source_target_pairs={{0,12},{4,8},{8,4},{12,0},{16,28},{20,24},{24,20},{28,16},{1,13},{... | collective-permute-start | bytes 24584 | tf_op jit(solution)/shard_map/ppermute | solution.py:553
  27.9 5.5 %collective-permute-start.9 = (f32[2,8,128]{2,1,0:T(8,128)S(1)}, f32[2,8,128]{2,1,0:T(8,128)S(1)}, u32[]{:S(2)}, u32[]{:S(2)}) collective-permute-start(f32[2,8,128]{2,1,0:T(8,128)S(1)} %get-tuple-element.37), channel_id=1, source_target_pairs={{0,8},{4,12},{8,0},{12,4},{16,24},{20,28},{24,16},{28,20},{1,9},{5... | collective-permute-start | bytes 24584 | tf_op jit(solution)/shard_map/ppermute | solution.py:553
  30.5 3.7 %collective-permute-start.8 = (f32[2,8,128]{2,1,0:T(8,128)S(1)}, f32[2,8,128]{2,1,0:T(8,128)S(1)}, u32[]{:S(2)}, u32[]{:S(2)}) collective-permute-start(f32[2,8,128]{2,1,0:T(8,128)S(1)} %get-tuple-element.37), channel_id=1, source_target_pairs={{0,4},{4,0},{8,12},{12,8},{16,20},{20,16},{24,28},{28,24},{1,5},{5... | collective-permute-start | bytes 24584 | tf_op jit(solution)/shard_map/ppermute | solution.py:553
  34.2 4.5 %collective-permute-start.11 = (f32[2,8,128]{2,1,0:T(8,128)S(1)}, f32[2,8,128]{2,1,0:T(8,128)S(1)}, u32[]{:S(2)}, u32[]{:S(2)}) collective-permute-start(f32[2,8,128]{2,1,0:T(8,128)S(1)} %add_add_fusion), channel_id=1, source_target_pairs={{0,16},{4,20},{8,24},{12,28},{16,0},{20,4},{24,8},{28,12},{1,17},{... | collective-permute-start | bytes 24584 | tf_op jit(solution)/shard_map/ppermute | solution.py:553

commit v8 on v7

--- a/solution.py
+++ b/solution.py
@@ -186,12 +186,11 @@
     return jnp.concatenate([ra * rb + ia * ib, ra * ib - ia * rb], axis=1)
 
 
-def scaled_spectra(traces_ref, me, each, place, presence_ref, present, tables_ref, weights_ref, spec_ref):
+def scaled_spectra(spectra_ref, me, each, place, presence_ref, present, weights_ref, spec_ref):
     stations, window = spec_ref.shape[1:]
-    events = traces_ref.shape[0] // stations
+    events = spectra_ref.shape[0] // stations
     pieces = events // each
-    result = jnp.dot(traces_ref[...], tables_ref[:, :window], preferred_element_type=jnp.float32)
-    rounded = result.astype(jnp.bfloat16).astype(jnp.float32)
+    rounded = spectra_ref[...].astype(jnp.float32)
     energy = jnp.sum(jnp.square(rounded) * weights_ref[...], axis=1, keepdims=True) + 1e-06
     gain = jnp.broadcast_to(lax.rsqrt(energy), (events * stations, LANES)).reshape(events, stations, LANES)
     rounded = rounded.reshape(events, stations, window)
@@ -266,6 +265,14 @@
     copy = pltpu.make_async_copy(tables_ref, tables_out, sem)
     copy.start()
     copy.wait()
+
+
+def spectra_kernel(near_ref, far_ref, tables_ref, near_out, far_out):
+    window = tables_ref.shape[0]
+    traces = jnp.concatenate([near_ref[...], far_ref[...]], axis=0)
+    result = jnp.dot(traces, tables_ref[:, :window], preferred_element_type=jnp.float32).astype(jnp.bfloat16)
+    near_out[...] = result[:near_ref.shape[0]]
+    far_out[...] = result[near_ref.shape[0]:]
 
 
 def own_pairs(spec_ref, tables_ref, table_ref, peaks, lhs_ref):
@@ -314,7 +321,7 @@
     mine = jnp.where(me * each < band, 0, band)
     for ref, place in ((near_ref, mine), (far_ref, band - mine)):
         scaled_spectra(
-            ref, me, each, place, presence_ref, band + place, tables_ref, weights_ref, spec_ref
+            ref, me, each, place, presence_ref, band + place, weights_ref, spec_ref
         )
     rows = Rows(block)
     peaks = no_peaks(rows, stations)
@@ -333,7 +340,7 @@
     me = lax.axis_index("sta")
     high = lax.axis_index("evt") % 2 == 0
     edge = jnp.where(high, 3 * band, 0)
-    scaled_spectra(halo_ref, me, each, 0, presence_ref, edge, tables_ref, weights_ref, other_ref)
+    scaled_spectra(halo_ref, me, each, 0, presence_ref, edge, weights_ref, other_ref)
     rows = Rows(block)
     peaks = no_peaks(rows, stations)
     halo_pairs(high, own_ref, other_ref, tables_ref, table_ref, peaks, lhs_ref, rows.first)
@@ -350,7 +357,7 @@
     me = lax.axis_index("sta")
     high = lax.axis_index("evt") % 2 == 1
     edge = jnp.where(high, 3 * band, 0)
-    scaled_spectra(halo_ref, me, each, 0, presence_ref, edge, tables_ref, weights_ref, other_ref)
+    scaled_spectra(halo_ref, me, each, 0, presence_ref, edge, weights_ref, other_ref)
     rows = Rows(block)
     peaks = no_peaks(rows, stations)
     halo_pairs(high, own_ref, other_ref, tables_ref, table_ref, peaks, lhs_ref, rows.second)
@@ -421,6 +428,17 @@
         compiler_params=PARAMS,
         cost_estimate=pl.CostEstimate(flops=0, bytes_accessed=5_000_000, transcendentals=0),
     )(tables)
+
+
+def spectra_call(near, far, tables):
+    return pl.pallas_call(
+        spectra_kernel,
+        out_shape=tuple(jax.ShapeDtypeStruct(x.shape, x.dtype) for x in (near, far)),
+        in_specs=[VMEM] * 3,
+        out_specs=(VMEM,) * 2,
+        compiler_params=PARAMS,
+        cost_estimate=cost(0, 0, near.shape[1], 2 * near.shape[0], 3_000_000),
+    )(near, far, tables)
 
 
 def own_call(near, far, presence, tables, each, block):
@@ -531,6 +549,7 @@
     ready = prepare_call(pair_events, pair_valid, presence, block)
     far, ready, brought = lax.optimization_barrier((far, ready, brought))
     tables = (brought, tables[1])
+    near, far = spectra_call(near, far, brought)
     me, place = lax.axis_index("sta"), lax.axis_index("evt")
     count = lax.axis_size("evt")
     inward = (place % 2 == 0) == (me * each < block // 2)

time: 39.6 us -> 40 us (1.010)
  waiting for transfers between devices: 5.52 us -> 6.61 us
  Pallas kernels: 10.5 us -> 9.89 us
    ppermute x2, waiting for transfers between devices: 0.56 us -> 1.59 us  [swapped(): return lax.ppermute(half, 'evt', links + [(j, i) for i, j in links])]
    pallas_call x0 -> x1, Pallas kernels: none -> 0.73 us  [spectra_call(): pl.pallas_call(spectra_kernel, out_shape=tuple((jax.ShapeDtypeStruct(x.sh...]
    pallas_call x1, Pallas kernels: 3.13 us -> 2.53 us  [own_call(): pl.pallas_call(functools.partial(own_kernel, each), out_shape=(jax.ShapeD...]
  transfers between devices with their start and end apart: 12 -> 12, of which waited for: 5 -> 5; matrix products, arithmetic and copies ran while one was open for 2% -> 2% of each run, Pallas kernels for 23% -> 20%
where the time goes in v8:
time: 40 us; the launch traced here: 39.7 us
  starting transfers between devices  17.9 us (45%)
  Pallas kernels  9.89 us (25%)
  waiting for transfers between devices  6.61 us (17%)
  local copies, waits for them, and re-layouts  2.89 us (7%)
  other arithmetic  1.5 us (4%)
  between operations  0.89 us (2%)
    ppermute x6, starting transfers between devices, swap(): return lax.ppermute(piece, 'sta', [(i, i ^ j) for i in range(sta_count)])  10.8 us
    ppermute x4, starting transfers between devices, from_station(): return lax.ppermute(sums, 'sta', [(i, i ^ j) for i in range(sta_count)])  4.51 us
    pallas_call x2, Pallas kernels, pick_call(): pl.pallas_call(functools.partial(pick_kernel, start, group), out_shape=ja...  4.05 us
    ppermute x6, waiting for transfers between devices, swap(): return lax.ppermute(piece, 'sta', [(i, i ^ j) for i in range(sta_count)])  2.76 us
    ppermute x2, starting transfers between devices, swapped(): return lax.ppermute(half, 'evt', links + [(j, i) for i, j in links])  2.57 us
    pallas_call x1, Pallas kernels, own_call(): pl.pallas_call(functools.partial(own_kernel, each), out_shape=(jax.ShapeD...  2.53 us
    ppermute x4, waiting for transfers between devices, from_station(): return lax.ppermute(sums, 'sta', [(i, i ^ j) for i in range(sta_count)])  2.27 us
    unnamed x4, local copies, waits for them, and re-layouts  1.74 us
  transfers between devices with their start and end apart: 12, of which 5 were waited for; matrix products, arithmetic and copies ran while one was open for 2% of the time, Pallas kernels for 20%

profile of v8, /device:TPU:4, one launch (start us, length us, event | category | flops | bytes accessed | tf_op | source)
XLA Modules:
  0.0 39.7 jit_solution(16609097844973611072)
XLA Ops:
  0.7 1.1 %dynamic-slice_bitcast_fusion.3 = (bf16[4,8,1024]{2,1,0:T(8,128)(2,1)S(1)}, bf16[1,4,8,1024]{3,2,1,0:T(8,128)(2,1)S(1)}, bf16[1,4,8,1024]{3,2,1,0:T(8,128)(2,1)S...) fusion(bf16[4,8,8,1024]{3,2,1,0:T(8,128)(2,1)} %bitcast.33, ...), kind=kLoop, calls=%fused_computation.12 | loop fusion | bytes 1048608 | tf_op jit(solution)/shard_map/jit(dynamic_index_in_dim)/squeeze | solution.py:133
  1.8 1.6 %collective-permute-start.4 = (bf16[2,4,8,1024]{3,2,1,0:T(8,128)(2,1)S(1)}, bf16[2,4,8,1024]{3,2,1,0:T(8,128)(2,1)S(1)}, u32[]{:S(2)}, u32[]{:S(2)}) collective-permute-start(bf16[2,4,8,1024]{3,2,1,0:T(8,128)(2,1)S(1)} %pad_maximum_fusion), channel_id=1, source_target_pairs={{0,8},{4,12},{8,0},{12,4},{16,24},{20,28},{24,16},{28,20},{1,9},{5... | collective-permute-start | bytes 393224 | tf_op jit(solution)/shard_map/ppermute | solution.py:136
  3.5 3.4 %collective-permute-start.3 = (bf16[4,8,1024]{2,1,0:T(8,128)(2,1)S(1)}, bf16[4,8,1024]{2,1,0:T(8,128)(2,1)S(1)}, u32[]{:S(2)}, u32[]{:S(2)}) collective-permute-start(bf16[4,8,1024]{2,1,0:T(8,128)(2,1)S(1)} %get-tuple-element.50), channel_id=1, source_target_pairs={{0,28},{4,24},{8,20},{12,16},{16,12},{20,8},{24,4},{28,0},{1,29},{... | collective-permute-start | bytes 196616 | tf_op jit(solution)/shard_map/ppermute | solution.py:136
  6.9 1.3 %collective-permute-start.2 = (bf16[4,8,1024]{2,1,0:T(8,128)(2,1)S(1)}, bf16[4,8,1024]{2,1,0:T(8,128)(2,1)S(1)}, u32[]{:S(2)}, u32[]{:S(2)}) collective-permute-start(bf16[4,8,1024]{2,1,0:T(8,128)(2,1)S(1)} %get-tuple-element.51), channel_id=1, source_target_pairs={{0,24},{4,28},{8,16},{12,20},{16,8},{20,12},{24,0},{28,4},{1,25},{... | collective-permute-start | bytes 196616 | tf_op jit(solution)/shard_map/ppermute | solution.py:136
  8.2 0.8 %collective-permute-start.1 = (bf16[4,8,1024]{2,1,0:T(8,128)(2,1)S(1)}, bf16[4,8,1024]{2,1,0:T(8,128)(2,1)S(1)}, u32[]{:S(2)}, u32[]{:S(2)}) collective-permute-start(bf16[4,8,1024]{2,1,0:T(8,128)(2,1)S(1)} %get-tuple-element.52), channel_id=1, source_target_pairs={{0,20},{4,16},{8,28},{12,24},{16,4},{20,0},{24,12},{28,8},{1,21},{... | collective-permute-start | bytes 196616 | tf_op jit(solution)/shard_map/ppermute | solution.py:136
  9.0 2.1 %collective-permute-start = (bf16[4,8,1024]{2,1,0:T(8,128)(2,1)S(1)}, bf16[4,8,1024]{2,1,0:T(8,128)(2,1)S(1)}, u32[]{:S(2)}, u32[]{:S(2)}) collective-permute-start(bf16[4,8,1024]{2,1,0:T(8,128)(2,1)S(1)} %get-tuple-element.53), channel_id=1, source_target_pairs={{0,16},{4,20},{8,24},{12,28},{16,0},{20,4},{24,8},{28,12},{1,17},{... | collective-permute-start | bytes 196616 | tf_op jit(solution)/shard_map/ppermute | solution.py:136
  11.1 0.0 collective-permute-done.4
  11.2 1.6 %collective-permute-start.5 = (bf16[8,8,1024]{2,1,0:T(8,128)(2,1)S(1)}, bf16[8,8,1024]{2,1,0:T(8,128)(2,1)S(1)}, u32[]{:S(2)}, u32[]{:S(2)}) collective-permute-start(bf16[8,8,1024]{2,1,0:T(8,128)(2,1)S(1)} %pad_maximum_fusion.1), channel_id=1, source_target_pairs={{0,4},{4,0},{8,12},{12,8},{16,20},{20,16},{24,28},{28,24},{1,5},{5... | collective-permute-start | bytes 393224 | tf_op jit(solution)/shard_map/ppermute | solution.py:136
  12.7 0.7 %pad_add_fusion.packed_ref = s32[11,1024]{1,0:T(8,128)S(1)} fusion(s32[8,128]{1,0:T(8,128)} %bitcast.35, s32[1,1024]{1,0:T(1,128)} %bitcast.36, s32[2,1024]{1,0:T(2,128)} %bitcast.34), kind=kLoop, calls=%fused_computation.8 | loop fusion | flops 22528 | bytes 61440 | tf_op jit(solution)/shard_map/concatenate | solution.py:403
  13.5 0.2 shard_map.77
  13.7 0.0 collective-permute-done.3
  13.7 0.0 copy-start
  13.7 1.7 %copy-done = bf16[1024,1280]{1,0:T(8,128)(2,1)S(1)} copy-done((bf16[1024,1280]{1,0:T(8,128)(2,1)S(1)}, bf16[1024,1280]{1,0:T(8,128)(2,1)}, u32[]{:S(2)}) %copy-start) | copy-done | bytes 2621464
  15.5 0.0 copy-start.1
  15.5 0.2 shard_map.78.tables_ref
  15.7 0.0 collective-permute-done.2
  15.7 2.4 %collective-permute-done.1 = bf16[4,8,1024]{2,1,0:T(8,128)(2,1)S(1)} collective-permute-done((bf16[4,8,1024]{2,1,0:T(8,128)(2,1)S(1)}, bf16[4,8,1024]{2,1,0:T(8,128)(2,1)S(1)}, u32[]{:S(2)}, u32[]{:S(2)}) %collective-permute-start.1) | collective-permute-done | bytes 65568 | tf_op jit(solution)/shard_map/ppermute | solution.py:136
  18.1 0.3 collective-permute-done
  18.5 0.0 collective-permute-done.5
  18.5 0.7 %shard_map.79 = (bf16[128,1024]{1,0:T(8,128)(2,1)S(1)}, bf16[128,1024]{1,0:T(8,128)(2,1)S(1)}) custom-call(bf16[128,1024]{1,0:T(8,128)(2,1)S(1)} %maximum_bitcast_fusion.1.near_ref, bf16[128,1024]{1,0:T(8,128)(2,1)S(1)} %maximum_bitcast_fusion.far_ref, bf16[1024,1280]{1,0:T(8,128)(2,1)S(1)} %shard_map.78.tables_ref), custom_call_target="tpu_custom_call" | custom-call | flops 536870912 | bytes 3000000 | tf_op jit(solution)/shard_map/pallas_call | solution.py:434
  19.3 0.1 collective-permute-start.7
  19.4 2.5 %collective-permute-start.6 = (bf16[128,1024]{1,0:T(8,128)(2,1)S(1)}, bf16[128,1024]{1,0:T(8,128)(2,1)S(1)}, u32[]{:S(2)}, u32[]{:S(2)}) collective-permute-start(bf16[128,1024]{1,0:T(8,128)(2,1)S(1)} %get-tuple-element.45), channel_id=1, source_target_pairs={{1,2},{2,1},{5,6},{6,5},{9,10},{10,9},{13,14},{14,13},{17,18},{18,... | collective-permute-start | bytes 786440 | tf_op jit(solution)/shard_map/ppermute | solution.py:559
  21.9 0.0 copy-done.1
  21.9 2.5 %shard_map.80 = (f32[32,8,1024]{2,1,0:T(8,128)S(1)}, bf16[1032,8,256]{2,1,0:T(8,128)(2,1)S(1)}, f32[8,1152]{1,0:T(8,128)S(1)}) custom-call(bf16[128,1024]{1,0:T(8,128)(2,1)S(1)} %get-tuple-element.31.near_ref, bf16[128,1024]{1,0:T(8,128)(2,1)S(1)} %get-tuple-element.32.far_ref, f32[64,8,128]{2,1,0:T(8,128)S(1)} %get-tuple-element.33.presence_ref, ...), custom_call_target="tpu_custom_call" | custom-call | flops 2113929216 | bytes 8000000 | tf_op jit(solution)/shard_map/pallas_call | solution.py:450
  24.5 0.0 collective-permute-done.7.halo_ref
  24.5 1.0 %shard_map.81 = (bf16[1032,8,256]{2,1,0:T(8,128)(2,1)S(1)}, f32[8,1152]{1,0:T(8,128)S(1)}) custom-call(bf16[128,1024]{1,0:T(8,128)(2,1)S(1)} %collective-permute-done.7.halo_ref, f32[32,8,1024]{2,1,0:T(8,128)S(1)} %get-tuple-element.34.own_ref, f32[64,8,128]{2,1,0:T(8,128)S(1)} %get-tuple-element.33.presence_ref, ...), custom_call_target="tpu_custom_call", output_to_operand_aliasing={{0}: (6, {})} | custom-call | flops 838860800 | bytes 4000000 | tf_op jit(solution)/shard_map/pallas_call | solution.py:471
  25.5 1.6 %collective-permute-done.6.halo_ref = bf16[128,1024]{1,0:T(8,128)(2,1)S(1)} collective-permute-done((bf16[128,1024]{1,0:T(8,128)(2,1)S(1)}, bf16[128,1024]{1,0:T(8,128)(2,1)S(1)}, u32[]{:S(2)}, u32[]{:S(2)}) %collective-permute-start.6) | collective-permute-done | bytes 262176 | tf_op jit(solution)/shard_map/ppermute | solution.py:559
  27.1 1.1 %shard_map.82 = (bf16[1032,8,256]{2,1,0:T(8,128)(2,1)S(1)}, f32[2,8,128]{2,1,0:T(8,128)S(1)}) custom-call(bf16[128,1024]{1,0:T(8,128)(2,1)S(1)} %collective-permute-done.6.halo_ref, f32[32,8,1024]{2,1,0:T(8,128)S(1)} %get-tuple-element.34.own_ref, f32[64,8,128]{2,1,0:T(8,128)S(1)} %get-tuple-element.33.presence_ref, ...), custom_call_target="tpu_custom_call", output_to_operand_aliasing={{0}: (8, {})} | custom-call | flops 838860800 | bytes 4000000 | tf_op jit(solution)/shard_map/pallas_call | solution.py:495
  28.2 0.0 collective-permute-start.10
  28.3 2.6 %collective-permute-start.9 = (f32[2,8,128]{2,1,0:T(8,128)S(1)}, f32[2,8,128]{2,1,0:T(8,128)S(1)}, u32[]{:S(2)}, u32[]{:S(2)}) collective-permute-start(f32[2,8,128]{2,1,0:T(8,128)S(1)} %get-tuple-element.41), channel_id=1, source_target_pairs={{0,8},{4,12},{8,0},{12,4},{16,24},{20,28},{24,16},{28,20},{1,9},{5... | collective-permute-start | bytes 24584 | tf_op jit(solution)/shard_map/ppermute | solution.py:572
  30.9 0.8 %collective-permute-start.8 = (f32[2,8,128]{2,1,0:T(8,128)S(1)}, f32[2,8,128]{2,1,0:T(8,128)S(1)}, u32[]{:S(2)}, u32[]{:S(2)}) collective-permute-start(f32[2,8,128]{2,1,0:T(8,128)S(1)} %get-tuple-element.41), channel_id=1, source_target_pairs={{0,4},{4,0},{8,12},{12,8},{16,20},{20,16},{24,28},{28,24},{1,5},{5... | collective-permute-start | bytes 24584 | tf_op jit(solution)/shard_map/ppermute | solution.py:572
  31.7 2.0 %shard_map.83.refs_0_ = bf16[1024,8,256]{2,1,0:T(8,128)(2,1)} custom-call(s32[1024]{0:T(1024)S(1)} %bitcast.31, bf16[1032,8,256]{2,1,0:T(8,128)(2,1)S(1)} %get-tuple-element.40.table_ref), custom_call_target="tpu_custom_call" | custom-call | bytes 10240000 | tf_op jit(solution)/shard_map/pallas_call | solution.py:516
  33.8 0.0 collective-permute-done.10
  33.8 0.0 collective-permute-done.9
  33.8 0.8 %collective-permute-done.8 = f32[2,8,128]{2,1,0:T(8,128)S(1)} collective-permute-done((f32[2,8,128]{2,1,0:T(8,128)S(1)}, f32[2,8,128]{2,1,0:T(8,128)S(1)}, u32[]{:S(2)}, u32[]{:S(2)}) %collective-permute-start.8) | collective-permute-done | bytes 8224 | tf_op jit(solution)/shard_map/ppermute | solution.py:572
  34.6 1.0 %collective-permute-start.11 = (f32[2,8,128]{2,1,0:T(8,128)S(1)}, f32[2,8,128]{2,1,0:T(8,128)S(1)}, u32[]{:S(2)}, u32[]{:S(2)}) collective-permute-start(f32[2,8,128]{2,1,0:T(8,128)S(1)} %add_add_fusion), channel_id=1, source_target_pairs={{0,16},{4,20},{8,24},{12,28},{16,0},{20,4},{24,8},{28,12},{1,17},{... | collective-permute-start | bytes 24584 | tf_op jit(solution)/shard_map/ppermute | solution.py:572
  35.6 2.0 %shard_map.84 = bf16[1024,8,256]{2,1,0:T(8,128)(2,1)} custom-call(s32[1024]{0:T(1024)S(1)} %bitcast.32, bf16[1032,8,256]{2,1,0:T(8,128)(2,1)S(1)} %get-tuple-element.40.table_ref, bf16[1024,8,256]{2,1,0:T(8,128)(2,1)} %shard_map.83.refs_0_), custom_call_target="tpu_custom_call", output_to_operand_aliasing={{}: (2, {})} | custom-call | bytes 10240000 | tf_op jit(solution)/shard_map/pallas_call | solution.py:516
  37.6 1.5 %collective-permute-done.11 = f32[2,8,128]{2,1,0:T(8,128)S(1)} collective-permute-done((f32[2,8,128]{2,1,0:T(8,128)S(1)}, f32[2,8,128]{2,1,0:T(8,128)S(1)}, u32[]{:S(2)}, u32[]{:S(2)}) %collective-permute-start.11) | collective-permute-done | bytes 8224 | tf_op jit(solution)/shard_map/ppermute | solution.py:572
  39.1 0.6 %fusion.1 = f32[1024]{0:T(1024)} fusion(f32[2,8,128]{2,1,0:T(8,128)S(1)} %add.55), kind=kLoop, calls=%fused_computation.20 | loop fusion | flops 2048 | bytes 12288 | tf_op jit(solution)/shard_map/div | solution.py:617
  (9 shorter events, 0.2 us)
Async XLA Ops:
  1.8 9.3 %collective-permute-start.4 = (bf16[2,4,8,1024]{3,2,1,0:T(8,128)(2,1)S(1)}, bf16[2,4,8,1024]{3,2,1,0:T(8,128)(2,1)S(1)}, u32[]{:S(2)}, u32[]{:S(2)}) collective-permute-start(bf16[2,4,8,1024]{3,2,1,0:T(8,128)(2,1)S(1)} %pad_maximum_fusion), channel_id=1, source_target_pairs={{0,8},{4,12},{8,0},{12,4},{16,24},{20,28},{24,16},{28,20},{1,9},{5... | collective-permute-start | bytes 393224 | tf_op jit(solution)/shard_map/ppermute | solution.py:136
  3.5 10.2 %collective-permute-start.3 = (bf16[4,8,1024]{2,1,0:T(8,128)(2,1)S(1)}, bf16[4,8,1024]{2,1,0:T(8,128)(2,1)S(1)}, u32[]{:S(2)}, u32[]{:S(2)}) collective-permute-start(bf16[4,8,1024]{2,1,0:T(8,128)(2,1)S(1)} %get-tuple-element.50), channel_id=1, source_target_pairs={{0,28},{4,24},{8,20},{12,16},{16,12},{20,8},{24,4},{28,0},{1,29},{... | collective-permute-start | bytes 196616 | tf_op jit(solution)/shard_map/ppermute | solution.py:136
  6.9 8.8 %collective-permute-start.2 = (bf16[4,8,1024]{2,1,0:T(8,128)(2,1)S(1)}, bf16[4,8,1024]{2,1,0:T(8,128)(2,1)S(1)}, u32[]{:S(2)}, u32[]{:S(2)}) collective-permute-start(bf16[4,8,1024]{2,1,0:T(8,128)(2,1)S(1)} %get-tuple-element.51), channel_id=1, source_target_pairs={{0,24},{4,28},{8,16},{12,20},{16,8},{20,12},{24,0},{28,4},{1,25},{... | collective-permute-start | bytes 196616 | tf_op jit(solution)/shard_map/ppermute | solution.py:136
  8.2 9.9 %collective-permute-start.1 = (bf16[4,8,1024]{2,1,0:T(8,128)(2,1)S(1)}, bf16[4,8,1024]{2,1,0:T(8,128)(2,1)S(1)}, u32[]{:S(2)}, u32[]{:S(2)}) collective-permute-start(bf16[4,8,1024]{2,1,0:T(8,128)(2,1)S(1)} %get-tuple-element.52), channel_id=1, source_target_pairs={{0,20},{4,16},{8,28},{12,24},{16,4},{20,0},{24,12},{28,8},{1,21},{... | collective-permute-start | bytes 196616 | tf_op jit(solution)/shard_map/ppermute | solution.py:136
  9.0 9.4 %collective-permute-start = (bf16[4,8,1024]{2,1,0:T(8,128)(2,1)S(1)}, bf16[4,8,1024]{2,1,0:T(8,128)(2,1)S(1)}, u32[]{:S(2)}, u32[]{:S(2)}) collective-permute-start(bf16[4,8,1024]{2,1,0:T(8,128)(2,1)S(1)} %get-tuple-element.53), channel_id=1, source_target_pairs={{0,16},{4,20},{8,24},{12,28},{16,0},{20,4},{24,8},{28,12},{1,17},{... | collective-permute-start | bytes 196616 | tf_op jit(solution)/shard_map/ppermute | solution.py:136
  11.2 7.3 %collective-permute-start.5 = (bf16[8,8,1024]{2,1,0:T(8,128)(2,1)S(1)}, bf16[8,8,1024]{2,1,0:T(8,128)(2,1)S(1)}, u32[]{:S(2)}, u32[]{:S(2)}) collective-permute-start(bf16[8,8,1024]{2,1,0:T(8,128)(2,1)S(1)} %pad_maximum_fusion.1), channel_id=1, source_target_pairs={{0,4},{4,0},{8,12},{12,8},{16,20},{20,16},{24,28},{28,24},{1,5},{5... | collective-permute-start | bytes 393224 | tf_op jit(solution)/shard_map/ppermute | solution.py:136
  13.7 1.7 %copy-start = (bf16[1024,1280]{1,0:T(8,128)(2,1)S(1)}, bf16[1024,1280]{1,0:T(8,128)(2,1)}, u32[]{:S(2)}) copy-start(bf16[1024,1280]{1,0:T(8,128)(2,1)} %constant.61.clone.tables_ref) | copy-start | bytes 7864324
  15.5 6.4 %copy-start.1 = (f32[1,1024]{1,0:T(1,128)S(1)}, f32[1,1024]{1,0:T(1,128)}, u32[]{:S(2)}) copy-start(f32[1,1024]{1,0:T(1,128)} %constant.62.clone.weights_ref) | copy-start | bytes 12292
  19.3 5.1 %collective-permute-start.7 = (bf16[128,1024]{1,0:T(8,128)(2,1)S(1)}, bf16[128,1024]{1,0:T(8,128)(2,1)S(1)}, u32[]{:S(2)}, u32[]{:S(2)}) collective-permute-start(bf16[128,1024]{1,0:T(8,128)(2,1)S(1)} %get-tuple-element.44), channel_id=1, source_target_pairs={{0,1},{2,3},{1,0},{3,2},{4,5},{6,7},{5,4},{7,6},{8,9},{10,11},{9,8... | collective-permute-start | bytes 786440 | tf_op jit(solution)/shard_map/ppermute | solution.py:559
  19.4 7.7 %collective-permute-start.6 = (bf16[128,1024]{1,0:T(8,128)(2,1)S(1)}, bf16[128,1024]{1,0:T(8,128)(2,1)S(1)}, u32[]{:S(2)}, u32[]{:S(2)}) collective-permute-start(bf16[128,1024]{1,0:T(8,128)(2,1)S(1)} %get-tuple-element.45), channel_id=1, source_target_pairs={{1,2},{2,1},{5,6},{6,5},{9,10},{10,9},{13,14},{14,13},{17,18},{18,... | collective-permute-start | bytes 786440 | tf_op jit(solution)/shard_map/ppermute | solution.py:559
  28.2 5.5 %collective-permute-start.10 = (f32[2,8,128]{2,1,0:T(8,128)S(1)}, f32[2,8,128]{2,1,0:T(8,128)S(1)}, u32[]{:S(2)}, u32[]{:S(2)}) collective-permute-start(f32[2,8,128]{2,1,0:T(8,128)S(1)} %get-tuple-element.41), channel_id=1, source_target_pairs={{0,12},{4,8},{8,4},{12,0},{16,28},{20,24},{24,20},{28,16},{1,13},{... | collective-permute-start | bytes 24584 | tf_op jit(solution)/shard_map/ppermute | solution.py:572
  28.3 5.5 %collective-permute-start.9 = (f32[2,8,128]{2,1,0:T(8,128)S(1)}, f32[2,8,128]{2,1,0:T(8,128)S(1)}, u32[]{:S(2)}, u32[]{:S(2)}) collective-permute-start(f32[2,8,128]{2,1,0:T(8,128)S(1)} %get-tuple-element.41), channel_id=1, source_target_pairs={{0,8},{4,12},{8,0},{12,4},{16,24},{20,28},{24,16},{28,20},{1,9},{5... | collective-permute-start | bytes 24584 | tf_op jit(solution)/shard_map/ppermute | solution.py:572
  30.9 3.7 %collective-permute-start.8 = (f32[2,8,128]{2,1,0:T(8,128)S(1)}, f32[2,8,128]{2,1,0:T(8,128)S(1)}, u32[]{:S(2)}, u32[]{:S(2)}) collective-permute-start(f32[2,8,128]{2,1,0:T(8,128)S(1)} %get-tuple-element.41), channel_id=1, source_target_pairs={{0,4},{4,0},{8,12},{12,8},{16,20},{20,16},{24,28},{28,24},{1,5},{5... | collective-permute-start | bytes 24584 | tf_op jit(solution)/shard_map/ppermute | solution.py:572
  34.6 4.5 %collective-permute-start.11 = (f32[2,8,128]{2,1,0:T(8,128)S(1)}, f32[2,8,128]{2,1,0:T(8,128)S(1)}, u32[]{:S(2)}, u32[]{:S(2)}) collective-permute-start(f32[2,8,128]{2,1,0:T(8,128)S(1)} %add_add_fusion), channel_id=1, source_target_pairs={{0,16},{4,20},{8,24},{12,28},{16,0},{20,4},{24,8},{28,12},{1,17},{... | collective-permute-start | bytes 24584 | tf_op jit(solution)/shard_map/ppermute | solution.py:572

commit v9 on v7

--- a/solution.py
+++ b/solution.py
@@ -552,13 +552,13 @@
     def from_station(j):
         return lax.ppermute(sums, "sta", [(i, i ^ j) for i in range(sta_count)])
 
-    split = row.shape[0] * 4 // 8
+    split = row.shape[0] * 6 // 8
+    arrived = from_station(4)
+    correlation = pick_call(row, table, (), 0, split)
+    sums, correlation = lax.optimization_barrier((sums + arrived, correlation))
     beside, across, aslant = from_station(1), from_station(2), from_station(3)
-    correlation = pick_call(row, table, (), 0, split)
-    sums, correlation = lax.optimization_barrier(((sums + beside) + (across + aslant), correlation))
-    arrived = from_station(4)
     correlation = pick_call(row, table, (correlation,), split, row.shape[0] - split)
-    return correlation, sums + arrived
+    return correlation, (sums + beside) + (across + aslant)
 
 
 def by_slot(waveforms, pair_events, pair_valid, presence, block):

time: 39.6 us -> 39.6 us (level)
  waiting for transfers between devices: 5.52 us -> 6.48 us
  starting transfers between devices: 18 us -> 17.1 us
    ppermute x4, waiting for transfers between devices: 2.2 us -> 3.16 us  [from_station(): return lax.ppermute(sums, 'sta', [(i, i ^ j) for i in range(sta_count)])]
    ppermute x4, starting transfers between devices: 4.59 us -> 3.64 us  [from_station(): return lax.ppermute(sums, 'sta', [(i, i ^ j) for i in range(sta_count)])]
where the time goes in v9:
time: 39.6 us; the launch traced here: 39.4 us
  starting transfers between devices  17.1 us (43%)
  Pallas kernels  10.5 us (27%)
  waiting for transfers between devices  6.48 us (16%)
  local copies, waits for them, and re-layouts  2.89 us (7%)
  other arithmetic  1.52 us (4%)
  between operations  0.88 us (2%)
    ppermute x6, starting transfers between devices, swap(): return lax.ppermute(piece, 'sta', [(i, i ^ j) for i in range(sta_count)])  10.8 us
    pallas_call x2, Pallas kernels, pick_call(): pl.pallas_call(functools.partial(pick_kernel, start, group), out_shape=ja...  4.05 us
    ppermute x4, starting transfers between devices, from_station(): return lax.ppermute(sums, 'sta', [(i, i ^ j) for i in range(sta_count)])  3.64 us
    ppermute x4, waiting for transfers between devices, from_station(): return lax.ppermute(sums, 'sta', [(i, i ^ j) for i in range(sta_count)])  3.16 us
    pallas_call x1, Pallas kernels, own_call(): pl.pallas_call(functools.partial(own_kernel, each), out_shape=(jax.ShapeD...  3.13 us
    ppermute x6, waiting for transfers between devices, swap(): return lax.ppermute(piece, 'sta', [(i, i ^ j) for i in range(sta_count)])  2.76 us
    ppermute x2, starting transfers between devices, swapped(): return lax.ppermute(half, 'evt', links + [(j, i) for i, j in links])  2.58 us
    unnamed x4, local copies, waits for them, and re-layouts  1.74 us
  transfers between devices with their start and end apart: 12, of which 5 were waited for; matrix products, arithmetic and copies ran while one was open for 2% of the time, Pallas kernels for 23%

profile of v9, /device:TPU:4, one launch (start us, length us, event | category | flops | bytes accessed | tf_op | source)
XLA Modules:
  0.0 39.4 jit_solution(3864316398859163138)
XLA Ops:
  0.7 1.1 %dynamic-slice_bitcast_fusion.3 = (bf16[4,8,1024]{2,1,0:T(8,128)(2,1)S(1)}, bf16[1,4,8,1024]{3,2,1,0:T(8,128)(2,1)S(1)}, bf16[1,4,8,1024]{3,2,1,0:T(8,128)(2,1)S...) fusion(bf16[4,8,8,1024]{3,2,1,0:T(8,128)(2,1)} %bitcast.37, ...), kind=kLoop, calls=%fused_computation.12 | loop fusion | bytes 1048608 | tf_op jit(solution)/shard_map/jit(dynamic_index_in_dim)/squeeze | solution.py:133
  1.8 0.0 copy-start.1
  1.8 1.6 %collective-permute-start.4 = (bf16[2,4,8,1024]{3,2,1,0:T(8,128)(2,1)S(1)}, bf16[2,4,8,1024]{3,2,1,0:T(8,128)(2,1)S(1)}, u32[]{:S(2)}, u32[]{:S(2)}) collective-permute-start(bf16[2,4,8,1024]{3,2,1,0:T(8,128)(2,1)S(1)} %pad_maximum_fusion), channel_id=1, source_target_pairs={{0,8},{4,12},{8,0},{12,4},{16,24},{20,28},{24,16},{28,20},{1,9},{5... | collective-permute-start | bytes 393224 | tf_op jit(solution)/shard_map/ppermute | solution.py:136
  3.5 3.4 %collective-permute-start.3 = (bf16[4,8,1024]{2,1,0:T(8,128)(2,1)S(1)}, bf16[4,8,1024]{2,1,0:T(8,128)(2,1)S(1)}, u32[]{:S(2)}, u32[]{:S(2)}) collective-permute-start(bf16[4,8,1024]{2,1,0:T(8,128)(2,1)S(1)} %get-tuple-element.46), channel_id=1, source_target_pairs={{0,28},{4,24},{8,20},{12,16},{16,12},{20,8},{24,4},{28,0},{1,29},{... | collective-permute-start | bytes 196616 | tf_op jit(solution)/shard_map/ppermute | solution.py:136
  6.9 1.3 %collective-permute-start.2 = (bf16[4,8,1024]{2,1,0:T(8,128)(2,1)S(1)}, bf16[4,8,1024]{2,1,0:T(8,128)(2,1)S(1)}, u32[]{:S(2)}, u32[]{:S(2)}) collective-permute-start(bf16[4,8,1024]{2,1,0:T(8,128)(2,1)S(1)} %get-tuple-element.47), channel_id=1, source_target_pairs={{0,24},{4,28},{8,16},{12,20},{16,8},{20,12},{24,0},{28,4},{1,25},{... | collective-permute-start | bytes 196616 | tf_op jit(solution)/shard_map/ppermute | solution.py:136
  8.2 0.8 %collective-permute-start.1 = (bf16[4,8,1024]{2,1,0:T(8,128)(2,1)S(1)}, bf16[4,8,1024]{2,1,0:T(8,128)(2,1)S(1)}, u32[]{:S(2)}, u32[]{:S(2)}) collective-permute-start(bf16[4,8,1024]{2,1,0:T(8,128)(2,1)S(1)} %get-tuple-element.48), channel_id=1, source_target_pairs={{0,20},{4,16},{8,28},{12,24},{16,4},{20,0},{24,12},{28,8},{1,21},{... | collective-permute-start | bytes 196616 | tf_op jit(solution)/shard_map/ppermute | solution.py:136
  9.0 2.1 %collective-permute-start = (bf16[4,8,1024]{2,1,0:T(8,128)(2,1)S(1)}, bf16[4,8,1024]{2,1,0:T(8,128)(2,1)S(1)}, u32[]{:S(2)}, u32[]{:S(2)}) collective-permute-start(bf16[4,8,1024]{2,1,0:T(8,128)(2,1)S(1)} %get-tuple-element.49), channel_id=1, source_target_pairs={{0,16},{4,20},{8,24},{12,28},{16,0},{20,4},{24,8},{28,12},{1,17},{... | collective-permute-start | bytes 196616 | tf_op jit(solution)/shard_map/ppermute | solution.py:136
  11.1 0.0 collective-permute-done.4
  11.2 1.6 %collective-permute-start.5 = (bf16[8,8,1024]{2,1,0:T(8,128)(2,1)S(1)}, bf16[8,8,1024]{2,1,0:T(8,128)(2,1)S(1)}, u32[]{:S(2)}, u32[]{:S(2)}) collective-permute-start(bf16[8,8,1024]{2,1,0:T(8,128)(2,1)S(1)} %pad_maximum_fusion.1), channel_id=1, source_target_pairs={{0,4},{4,0},{8,12},{12,8},{16,20},{20,16},{24,28},{28,24},{1,5},{5... | collective-permute-start | bytes 393224 | tf_op jit(solution)/shard_map/ppermute | solution.py:136
  12.7 0.7 %pad_add_fusion.packed_ref = s32[11,1024]{1,0:T(8,128)S(1)} fusion(s32[8,128]{1,0:T(8,128)} %bitcast.39, s32[1,1024]{1,0:T(1,128)} %bitcast.40, s32[2,1024]{1,0:T(2,128)} %bitcast.38), kind=kLoop, calls=%fused_computation.8 | loop fusion | flops 22528 | bytes 61440 | tf_op jit(solution)/shard_map/concatenate | solution.py:396
  13.5 0.2 shard_map.77
  13.7 0.0 collective-permute-done.3
  13.7 0.0 copy-start
  13.7 1.7 %copy-done = bf16[1024,1280]{1,0:T(8,128)(2,1)S(1)} copy-done((bf16[1024,1280]{1,0:T(8,128)(2,1)S(1)}, bf16[1024,1280]{1,0:T(8,128)(2,1)}, u32[]{:S(2)}) %copy-start) | copy-done | bytes 2621464
  15.5 0.2 shard_map.78.tables_ref
  15.7 0.0 collective-permute-done.2
  15.7 2.4 %collective-permute-done.1 = bf16[4,8,1024]{2,1,0:T(8,128)(2,1)S(1)} collective-permute-done((bf16[4,8,1024]{2,1,0:T(8,128)(2,1)S(1)}, bf16[4,8,1024]{2,1,0:T(8,128)(2,1)S(1)}, u32[]{:S(2)}, u32[]{:S(2)}) %collective-permute-start.1) | collective-permute-done | bytes 65568 | tf_op jit(solution)/shard_map/ppermute | solution.py:136
  18.1 0.3 collective-permute-done
  18.5 0.0 collective-permute-done.5
  18.5 0.1 broadcast_select_fusion
  18.6 0.1 collective-permute-start.7
  18.6 2.5 %collective-permute-start.6 = (bf16[128,1024]{1,0:T(8,128)(2,1)S(1)}, bf16[128,1024]{1,0:T(8,128)(2,1)S(1)}, u32[]{:S(2)}, u32[]{:S(2)}) collective-permute-start(bf16[128,1024]{1,0:T(8,128)(2,1)S(1)} %get-tuple-element.41), channel_id=1, source_target_pairs={{1,2},{2,1},{5,6},{6,5},{9,10},{10,9},{13,14},{14,13},{17,18},{18,... | collective-permute-start | bytes 786440 | tf_op jit(solution)/shard_map/ppermute | solution.py:540
  21.2 0.0 copy-done.1
  21.2 3.1 %shard_map.79 = (f32[32,8,1024]{2,1,0:T(8,128)S(1)}, bf16[1032,8,256]{2,1,0:T(8,128)(2,1)S(1)}, f32[8,1152]{1,0:T(8,128)S(1)}) custom-call(bf16[128,1024]{1,0:T(8,128)(2,1)S(1)} %maximum_bitcast_fusion.1.near_ref, bf16[128,1024]{1,0:T(8,128)(2,1)S(1)} %maximum_bitcast_fusion.far_ref, f32[64,8,128]{2,1,0:T(8,128)S(1)} %get-tuple-element.28.presence_ref, ...), custom_call_target="tpu_custom_call" | custom-call | flops 2113929216 | bytes 8000000 | tf_op jit(solution)/shard_map/pallas_call | solution.py:432
  24.3 0.0 collective-permute-done.7.halo_ref
  24.4 1.4 %shard_map.80 = (bf16[1032,8,256]{2,1,0:T(8,128)(2,1)S(1)}, f32[8,1152]{1,0:T(8,128)S(1)}) custom-call(bf16[128,1024]{1,0:T(8,128)(2,1)S(1)} %collective-permute-done.7.halo_ref, f32[32,8,1024]{2,1,0:T(8,128)S(1)} %get-tuple-element.30.own_ref, f32[64,8,128]{2,1,0:T(8,128)S(1)} %get-tuple-element.28.presence_ref, ...), custom_call_target="tpu_custom_call", output_to_operand_aliasing={{0}: (6, {})} | custom-call | flops 838860800 | bytes 4000000 | tf_op jit(solution)/shard_map/pallas_call | solution.py:453
  25.8 0.6 %collective-permute-done.6.halo_ref = bf16[128,1024]{1,0:T(8,128)(2,1)S(1)} collective-permute-done((bf16[128,1024]{1,0:T(8,128)(2,1)S(1)}, bf16[128,1024]{1,0:T(8,128)(2,1)S(1)}, u32[]{:S(2)}, u32[]{:S(2)}) %collective-permute-start.6) | collective-permute-done | bytes 262176 | tf_op jit(solution)/shard_map/ppermute | solution.py:540
  26.3 1.5 %shard_map.81 = (bf16[1032,8,256]{2,1,0:T(8,128)(2,1)S(1)}, f32[2,8,128]{2,1,0:T(8,128)S(1)}) custom-call(bf16[128,1024]{1,0:T(8,128)(2,1)S(1)} %collective-permute-done.6.halo_ref, f32[32,8,1024]{2,1,0:T(8,128)S(1)} %get-tuple-element.30.own_ref, f32[64,8,128]{2,1,0:T(8,128)S(1)} %get-tuple-element.28.presence_ref, ...), custom_call_target="tpu_custom_call", output_to_operand_aliasing={{0}: (8, {})} | custom-call | flops 838860800 | bytes 4000000 | tf_op jit(solution)/shard_map/pallas_call | solution.py:477
  27.9 0.2 collective-permute-start.8
  28.0 2.4 %shard_map.82.refs_0_ = bf16[1024,8,256]{2,1,0:T(8,128)(2,1)} custom-call(s32[1024]{0:T(1024)S(1)} %bitcast.35, bf16[1032,8,256]{2,1,0:T(8,128)(2,1)S(1)} %get-tuple-element.36.table_ref), custom_call_target="tpu_custom_call" | custom-call | bytes 15360000 | tf_op jit(solution)/shard_map/pallas_call | solution.py:498
  30.4 2.0 %collective-permute-done.8 = f32[2,8,128]{2,1,0:T(8,128)S(1)} collective-permute-done((f32[2,8,128]{2,1,0:T(8,128)S(1)}, f32[2,8,128]{2,1,0:T(8,128)S(1)}, u32[]{:S(2)}, u32[]{:S(2)}) %collective-permute-start.8) | collective-permute-done | bytes 8224 | tf_op jit(solution)/shard_map/ppermute | solution.py:553
  32.4 1.5 %collective-permute-start.11 = (f32[2,8,128]{2,1,0:T(8,128)S(1)}, f32[2,8,128]{2,1,0:T(8,128)S(1)}, u32[]{:S(2)}, u32[]{:S(2)}) collective-permute-start(f32[2,8,128]{2,1,0:T(8,128)S(1)} %add.52), channel_id=1, source_target_pairs={{0,12},{4,8},{8,4},{12,0},{16,28},{20,24},{24,20},{28,16},{1,13},{... | collective-permute-start | bytes 24584 | tf_op jit(solution)/shard_map/ppermute | solution.py:553
  34.0 1.1 %collective-permute-start.10 = (f32[2,8,128]{2,1,0:T(8,128)S(1)}, f32[2,8,128]{2,1,0:T(8,128)S(1)}, u32[]{:S(2)}, u32[]{:S(2)}) collective-permute-start(f32[2,8,128]{2,1,0:T(8,128)S(1)} %add.52), channel_id=1, source_target_pairs={{0,8},{4,12},{8,0},{12,4},{16,24},{20,28},{24,16},{28,20},{1,9},{5... | collective-permute-start | bytes 24584 | tf_op jit(solution)/shard_map/ppermute | solution.py:553
  35.1 0.8 %collective-permute-start.9 = (f32[2,8,128]{2,1,0:T(8,128)S(1)}, f32[2,8,128]{2,1,0:T(8,128)S(1)}, u32[]{:S(2)}, u32[]{:S(2)}) collective-permute-start(f32[2,8,128]{2,1,0:T(8,128)S(1)} %add.52), channel_id=1, source_target_pairs={{0,4},{4,0},{8,12},{12,8},{16,20},{20,16},{24,28},{28,24},{1,5},{5... | collective-permute-start | bytes 24584 | tf_op jit(solution)/shard_map/ppermute | solution.py:553
  35.9 1.6 %shard_map.83 = bf16[1024,8,256]{2,1,0:T(8,128)(2,1)} custom-call(s32[1024]{0:T(1024)S(1)} %bitcast.36, bf16[1032,8,256]{2,1,0:T(8,128)(2,1)S(1)} %get-tuple-element.36.table_ref, bf16[1024,8,256]{2,1,0:T(8,128)(2,1)} %shard_map.82.refs_0_), custom_call_target="tpu_custom_call", output_to_operand_aliasing={{}: (2, {})} | custom-call | bytes 5120000 | tf_op jit(solution)/shard_map/pallas_call | solution.py:498
  37.6 0.0 collective-permute-done.11
  37.6 0.0 collective-permute-done.10
  37.6 1.1 %collective-permute-done.9 = f32[2,8,128]{2,1,0:T(8,128)S(1)} collective-permute-done((f32[2,8,128]{2,1,0:T(8,128)S(1)}, f32[2,8,128]{2,1,0:T(8,128)S(1)}, u32[]{:S(2)}, u32[]{:S(2)}) %collective-permute-start.9) | collective-permute-done | bytes 8224 | tf_op jit(solution)/shard_map/ppermute | solution.py:553
  38.7 0.6 %fusion.1 = f32[1024]{0:T(1024)} fusion(f32[2,8,128]{2,1,0:T(8,128)S(1)} %add_add_fusion), kind=kLoop, calls=%fused_computation.20 | loop fusion | flops 2048 | bytes 12288 | tf_op jit(solution)/shard_map/div | solution.py:598
  (8 shorter events, 0.1 us)
Async XLA Ops:
  1.8 19.4 %copy-start.1 = (f32[1,1024]{1,0:T(1,128)S(1)}, f32[1,1024]{1,0:T(1,128)}, u32[]{:S(2)}) copy-start(f32[1,1024]{1,0:T(1,128)} %constant.62.clone.weights_ref) | copy-start | bytes 12292
  1.8 9.3 %collective-permute-start.4 = (bf16[2,4,8,1024]{3,2,1,0:T(8,128)(2,1)S(1)}, bf16[2,4,8,1024]{3,2,1,0:T(8,128)(2,1)S(1)}, u32[]{:S(2)}, u32[]{:S(2)}) collective-permute-start(bf16[2,4,8,1024]{3,2,1,0:T(8,128)(2,1)S(1)} %pad_maximum_fusion), channel_id=1, source_target_pairs={{0,8},{4,12},{8,0},{12,4},{16,24},{20,28},{24,16},{28,20},{1,9},{5... | collective-permute-start | bytes 393224 | tf_op jit(solution)/shard_map/ppermute | solution.py:136
  3.5 10.2 %collective-permute-start.3 = (bf16[4,8,1024]{2,1,0:T(8,128)(2,1)S(1)}, bf16[4,8,1024]{2,1,0:T(8,128)(2,1)S(1)}, u32[]{:S(2)}, u32[]{:S(2)}) collective-permute-start(bf16[4,8,1024]{2,1,0:T(8,128)(2,1)S(1)} %get-tuple-element.46), channel_id=1, source_target_pairs={{0,28},{4,24},{8,20},{12,16},{16,12},{20,8},{24,4},{28,0},{1,29},{... | collective-permute-start | bytes 196616 | tf_op jit(solution)/shard_map/ppermute | solution.py:136
  6.9 8.8 %collective-permute-start.2 = (bf16[4,8,1024]{2,1,0:T(8,128)(2,1)S(1)}, bf16[4,8,1024]{2,1,0:T(8,128)(2,1)S(1)}, u32[]{:S(2)}, u32[]{:S(2)}) collective-permute-start(bf16[4,8,1024]{2,1,0:T(8,128)(2,1)S(1)} %get-tuple-element.47), channel_id=1, source_target_pairs={{0,24},{4,28},{8,16},{12,20},{16,8},{20,12},{24,0},{28,4},{1,25},{... | collective-permute-start | bytes 196616 | tf_op jit(solution)/shard_map/ppermute | solution.py:136
  8.2 9.9 %collective-permute-start.1 = (bf16[4,8,1024]{2,1,0:T(8,128)(2,1)S(1)}, bf16[4,8,1024]{2,1,0:T(8,128)(2,1)S(1)}, u32[]{:S(2)}, u32[]{:S(2)}) collective-permute-start(bf16[4,8,1024]{2,1,0:T(8,128)(2,1)S(1)} %get-tuple-element.48), channel_id=1, source_target_pairs={{0,20},{4,16},{8,28},{12,24},{16,4},{20,0},{24,12},{28,8},{1,21},{... | collective-permute-start | bytes 196616 | tf_op jit(solution)/shard_map/ppermute | solution.py:136
  9.0 9.4 %collective-permute-start = (bf16[4,8,1024]{2,1,0:T(8,128)(2,1)S(1)}, bf16[4,8,1024]{2,1,0:T(8,128)(2,1)S(1)}, u32[]{:S(2)}, u32[]{:S(2)}) collective-permute-start(bf16[4,8,1024]{2,1,0:T(8,128)(2,1)S(1)} %get-tuple-element.49), channel_id=1, source_target_pairs={{0,16},{4,20},{8,24},{12,28},{16,0},{20,4},{24,8},{28,12},{1,17},{... | collective-permute-start | bytes 196616 | tf_op jit(solution)/shard_map/ppermute | solution.py:136
  11.2 7.3 %collective-permute-start.5 = (bf16[8,8,1024]{2,1,0:T(8,128)(2,1)S(1)}, bf16[8,8,1024]{2,1,0:T(8,128)(2,1)S(1)}, u32[]{:S(2)}, u32[]{:S(2)}) collective-permute-start(bf16[8,8,1024]{2,1,0:T(8,128)(2,1)S(1)} %pad_maximum_fusion.1), channel_id=1, source_target_pairs={{0,4},{4,0},{8,12},{12,8},{16,20},{20,16},{24,28},{28,24},{1,5},{5... | collective-permute-start | bytes 393224 | tf_op jit(solution)/shard_map/ppermute | solution.py:136
  13.7 1.7 %copy-start = (bf16[1024,1280]{1,0:T(8,128)(2,1)S(1)}, bf16[1024,1280]{1,0:T(8,128)(2,1)}, u32[]{:S(2)}) copy-start(bf16[1024,1280]{1,0:T(8,128)(2,1)} %constant.61.clone.tables_ref) | copy-start | bytes 7864324
  18.6 5.8 %collective-permute-start.7 = (bf16[128,1024]{1,0:T(8,128)(2,1)S(1)}, bf16[128,1024]{1,0:T(8,128)(2,1)S(1)}, u32[]{:S(2)}, u32[]{:S(2)}) collective-permute-start(bf16[128,1024]{1,0:T(8,128)(2,1)S(1)} %get-tuple-element.40), channel_id=1, source_target_pairs={{0,1},{2,3},{1,0},{3,2},{4,5},{6,7},{5,4},{7,6},{8,9},{10,11},{9,8... | collective-permute-start | bytes 786440 | tf_op jit(solution)/shard_map/ppermute | solution.py:540
  18.6 7.7 %collective-permute-start.6 = (bf16[128,1024]{1,0:T(8,128)(2,1)S(1)}, bf16[128,1024]{1,0:T(8,128)(2,1)S(1)}, u32[]{:S(2)}, u32[]{:S(2)}) collective-permute-start(bf16[128,1024]{1,0:T(8,128)(2,1)S(1)} %get-tuple-element.41), channel_id=1, source_target_pairs={{1,2},{2,1},{5,6},{6,5},{9,10},{10,9},{13,14},{14,13},{17,18},{18,... | collective-permute-start | bytes 786440 | tf_op jit(solution)/shard_map/ppermute | solution.py:540
  27.9 4.6 %collective-permute-start.8 = (f32[2,8,128]{2,1,0:T(8,128)S(1)}, f32[2,8,128]{2,1,0:T(8,128)S(1)}, u32[]{:S(2)}, u32[]{:S(2)}) collective-permute-start(f32[2,8,128]{2,1,0:T(8,128)S(1)} %get-tuple-element.37), channel_id=1, source_target_pairs={{0,16},{4,20},{8,24},{12,28},{16,0},{20,4},{24,8},{28,12},{1,17},{... | collective-permute-start | bytes 24584 | tf_op jit(solution)/shard_map/ppermute | solution.py:553
  32.4 5.1 %collective-permute-start.11 = (f32[2,8,128]{2,1,0:T(8,128)S(1)}, f32[2,8,128]{2,1,0:T(8,128)S(1)}, u32[]{:S(2)}, u32[]{:S(2)}) collective-permute-start(f32[2,8,128]{2,1,0:T(8,128)S(1)} %add.52), channel_id=1, source_target_pairs={{0,12},{4,8},{8,4},{12,0},{16,28},{20,24},{24,20},{28,16},{1,13},{... | collective-permute-start | bytes 24584 | tf_op jit(solution)/shard_map/ppermute | solution.py:553
  34.0 3.7 %collective-permute-start.10 = (f32[2,8,128]{2,1,0:T(8,128)S(1)}, f32[2,8,128]{2,1,0:T(8,128)S(1)}, u32[]{:S(2)}, u32[]{:S(2)}) collective-permute-start(f32[2,8,128]{2,1,0:T(8,128)S(1)} %add.52), channel_id=1, source_target_pairs={{0,8},{4,12},{8,0},{12,4},{16,24},{20,28},{24,16},{28,20},{1,9},{5... | collective-permute-start | bytes 24584 | tf_op jit(solution)/shard_map/ppermute | solution.py:553
  35.1 3.7 %collective-permute-start.9 = (f32[2,8,128]{2,1,0:T(8,128)S(1)}, f32[2,8,128]{2,1,0:T(8,128)S(1)}, u32[]{:S(2)}, u32[]{:S(2)}) collective-permute-start(f32[2,8,128]{2,1,0:T(8,128)S(1)} %add.52), channel_id=1, source_target_pairs={{0,4},{4,0},{8,12},{12,8},{16,20},{20,16},{24,28},{28,24},{1,5},{5... | collective-permute-start | bytes 24584 | tf_op jit(solution)/shard_map/ppermute | solution.py:553

commit v10 on v9

--- a/solution.py
+++ b/solution.py
@@ -138,12 +138,12 @@
     later = [swap(for_station(me ^ j), j) for j in range(half, sta_count)]
     across = swap(jnp.stack([for_station(me ^ 2), for_station(me ^ 3)]), 2)
     beside = swap(jnp.concatenate([for_station(me ^ 1), across[1]], axis=0), 1)
-    later[3], tables = lax.optimization_barrier((later[3], tables))
+    later[0], tables = lax.optimization_barrier((later[0], tables))
     tables = bring_call(tables)
     pieces = [for_station(me), beside[:events], across[0], beside[events:]] + later
     rows = half * events * share
-    near = jnp.concatenate(pieces[:half], axis=0).reshape(rows, window)
-    far = jnp.concatenate(pieces[half:], axis=0).reshape(rows, window)
+    near = jnp.concatenate(pieces[:half][::-1], axis=0).reshape(rows, window)
+    far = jnp.concatenate(pieces[half:][::-1], axis=0).reshape(rows, window)
     return near, far, tables
 
 
@@ -196,7 +196,7 @@
     gain = jnp.broadcast_to(lax.rsqrt(energy), (events * stations, LANES)).reshape(events, stations, LANES)
     rounded = rounded.reshape(events, stations, window)
     for j in range(pieces):
-        shift = ((me ^ j) & (pieces - 1)) * each
+        shift = ((me ^ (pieces - 1 - j)) & (pieces - 1)) * each
         piece = slice(j * each, (j + 1) * each)
         scale = gain[piece] * presence_ref[pl.ds(present + shift, each)]
         scale = jnp.concatenate([scale] * (window // LANES), axis=2)

time: 39.6 us -> 39.3 us (level)
  waiting for transfers between devices: 6.48 us -> 3.63 us
  starting transfers between devices: 17.1 us -> 19.4 us
    ppermute x4, waiting for transfers between devices: 3.16 us -> 0.8 us  [from_station(): return lax.ppermute(sums, 'sta', [(i, i ^ j) for i in range(sta_count)])]
    ppermute x4, starting transfers between devices: 3.64 us -> 5.97 us  [from_station(): return lax.ppermute(sums, 'sta', [(i, i ^ j) for i in range(sta_count)])]
    ppermute x6, waiting for transfers between devices: 2.76 us -> 2.26 us  [swap(): return lax.ppermute(piece, 'sta', [(i, i ^ j) for i in range(sta_count)])]
where the time goes in v10:
time: 39.3 us; the launch traced here: 38.8 us
  starting transfers between devices  19.4 us (49%)
  Pallas kernels  10.5 us (27%)
  waiting for transfers between devices  3.63 us (9%)
  local copies, waits for them, and re-layouts  2.89 us (7%)
  other arithmetic  1.52 us (4%)
  between operations  0.87 us (2%)
    ppermute x6, starting transfers between devices, swap(): return lax.ppermute(piece, 'sta', [(i, i ^ j) for i in range(sta_count)])  10.8 us
    ppermute x4, starting transfers between devices, from_station(): return lax.ppermute(sums, 'sta', [(i, i ^ j) for i in range(sta_count)])  5.97 us
    pallas_call x2, Pallas kernels, pick_call(): pl.pallas_call(functools.partial(pick_kernel, start, group), out_shape=ja...  4.05 us
    pallas_call x1, Pallas kernels, own_call(): pl.pallas_call(functools.partial(own_kernel, each), out_shape=(jax.ShapeD...  3.11 us
    ppermute x2, starting transfers between devices, swapped(): return lax.ppermute(half, 'evt', links + [(j, i) for i, j in links])  2.58 us
    ppermute x6, waiting for transfers between devices, swap(): return lax.ppermute(piece, 'sta', [(i, i ^ j) for i in range(sta_count)])  2.26 us
    unnamed x4, local copies, waits for them, and re-layouts  1.74 us
    pallas_call x1, Pallas kernels, last_call(): pl.pallas_call(functools.partial(last_kernel, each), out_shape=(jax.Shape...  1.52 us
  transfers between devices with their start and end apart: 12, of which 5 were waited for; matrix products, arithmetic and copies ran while one was open for 2% of the time, Pallas kernels for 23%

profile of v10, /device:TPU:4, one launch (start us, length us, event | category | flops | bytes accessed | tf_op | source)
XLA Modules:
  0.0 38.8 jit_solution(10641408844662779727)
XLA Ops:
  0.7 1.1 %dynamic-slice_bitcast_fusion.3 = (bf16[4,8,1024]{2,1,0:T(8,128)(2,1)S(1)}, bf16[4,8,1024]{2,1,0:T(8,128)(2,1)S(1)}, bf16[1,4,8,1024]{3,2,1,0:T(8,128)(2,1)S(1)}...) fusion(bf16[4,8,8,1024]{3,2,1,0:T(8,128)(2,1)} %bitcast.37, ...), kind=kLoop, calls=%fused_computation.12 | loop fusion | bytes 1048608 | tf_op jit(solution)/shard_map/jit(dynamic_index_in_dim)/squeeze | solution.py:133
  1.8 0.0 copy-start.1
  1.8 1.6 %collective-permute-start.4 = (bf16[2,4,8,1024]{3,2,1,0:T(8,128)(2,1)S(1)}, bf16[2,4,8,1024]{3,2,1,0:T(8,128)(2,1)S(1)}, u32[]{:S(2)}, u32[]{:S(2)}) collective-permute-start(bf16[2,4,8,1024]{3,2,1,0:T(8,128)(2,1)S(1)} %pad_maximum_fusion), channel_id=1, source_target_pairs={{0,8},{4,12},{8,0},{12,4},{16,24},{20,28},{24,16},{28,20},{1,9},{5... | collective-permute-start | bytes 393224 | tf_op jit(solution)/shard_map/ppermute | solution.py:136
  3.5 2.6 %collective-permute-start.3 = (bf16[4,8,1024]{2,1,0:T(8,128)(2,1)S(1)}, bf16[4,8,1024]{2,1,0:T(8,128)(2,1)S(1)}, u32[]{:S(2)}, u32[]{:S(2)}) collective-permute-start(bf16[4,8,1024]{2,1,0:T(8,128)(2,1)S(1)} %get-tuple-element.46), channel_id=1, source_target_pairs={{0,16},{4,20},{8,24},{12,28},{16,0},{20,4},{24,8},{28,12},{1,17},{... | collective-permute-start | bytes 196616 | tf_op jit(solution)/shard_map/ppermute | solution.py:136
  6.1 1.3 %collective-permute-start.2 = (bf16[4,8,1024]{2,1,0:T(8,128)(2,1)S(1)}, bf16[4,8,1024]{2,1,0:T(8,128)(2,1)S(1)}, u32[]{:S(2)}, u32[]{:S(2)}) collective-permute-start(bf16[4,8,1024]{2,1,0:T(8,128)(2,1)S(1)} %get-tuple-element.47), channel_id=1, source_target_pairs={{0,20},{4,16},{8,28},{12,24},{16,4},{20,0},{24,12},{28,8},{1,21},{... | collective-permute-start | bytes 196616 | tf_op jit(solution)/shard_map/ppermute | solution.py:136
  7.3 2.5 %collective-permute-start.1 = (bf16[4,8,1024]{2,1,0:T(8,128)(2,1)S(1)}, bf16[4,8,1024]{2,1,0:T(8,128)(2,1)S(1)}, u32[]{:S(2)}, u32[]{:S(2)}) collective-permute-start(bf16[4,8,1024]{2,1,0:T(8,128)(2,1)S(1)} %get-tuple-element.48), channel_id=1, source_target_pairs={{0,24},{4,28},{8,16},{12,20},{16,8},{20,12},{24,0},{28,4},{1,25},{... | collective-permute-start | bytes 196616 | tf_op jit(solution)/shard_map/ppermute | solution.py:136
  9.8 1.3 %collective-permute-start = (bf16[4,8,1024]{2,1,0:T(8,128)(2,1)S(1)}, bf16[4,8,1024]{2,1,0:T(8,128)(2,1)S(1)}, u32[]{:S(2)}, u32[]{:S(2)}) collective-permute-start(bf16[4,8,1024]{2,1,0:T(8,128)(2,1)S(1)} %get-tuple-element.49), channel_id=1, source_target_pairs={{0,28},{4,24},{8,20},{12,16},{16,12},{20,8},{24,4},{28,0},{1,29},{... | collective-permute-start | bytes 196616 | tf_op jit(solution)/shard_map/ppermute | solution.py:136
  11.1 0.0 collective-permute-done.4
  11.2 1.6 %collective-permute-start.5 = (bf16[8,8,1024]{2,1,0:T(8,128)(2,1)S(1)}, bf16[8,8,1024]{2,1,0:T(8,128)(2,1)S(1)}, u32[]{:S(2)}, u32[]{:S(2)}) collective-permute-start(bf16[8,8,1024]{2,1,0:T(8,128)(2,1)S(1)} %pad_maximum_fusion.1), channel_id=1, source_target_pairs={{0,4},{4,0},{8,12},{12,8},{16,20},{20,16},{24,28},{28,24},{1,5},{5... | collective-permute-start | bytes 393224 | tf_op jit(solution)/shard_map/ppermute | solution.py:136
  12.7 0.7 %pad_add_fusion.packed_ref = s32[11,1024]{1,0:T(8,128)S(1)} fusion(s32[8,128]{1,0:T(8,128)} %bitcast.39, s32[1,1024]{1,0:T(1,128)} %bitcast.40, s32[2,1024]{1,0:T(2,128)} %bitcast.38), kind=kLoop, calls=%fused_computation.8 | loop fusion | flops 22528 | bytes 61440 | tf_op jit(solution)/shard_map/concatenate | solution.py:396
  13.5 0.2 shard_map.77
  13.7 0.0 collective-permute-done.3
  13.7 0.0 copy-start
  13.7 1.7 %copy-done = bf16[1024,1280]{1,0:T(8,128)(2,1)S(1)} copy-done((bf16[1024,1280]{1,0:T(8,128)(2,1)S(1)}, bf16[1024,1280]{1,0:T(8,128)(2,1)}, u32[]{:S(2)}) %copy-start) | copy-done | bytes 2621464
  15.5 0.2 shard_map.78.tables_ref
  15.7 1.6 %collective-permute-done.2 = bf16[4,8,1024]{2,1,0:T(8,128)(2,1)S(1)} collective-permute-done((bf16[4,8,1024]{2,1,0:T(8,128)(2,1)S(1)}, bf16[4,8,1024]{2,1,0:T(8,128)(2,1)S(1)}, u32[]{:S(2)}, u32[]{:S(2)}) %collective-permute-start.2) | collective-permute-done | bytes 65568 | tf_op jit(solution)/shard_map/ppermute | solution.py:136
  17.3 0.0 collective-permute-done.1
  17.3 0.0 collective-permute-done
  17.3 0.6 %collective-permute-done.5 = bf16[8,8,1024]{2,1,0:T(8,128)(2,1)S(1)} collective-permute-done((bf16[8,8,1024]{2,1,0:T(8,128)(2,1)S(1)}, bf16[8,8,1024]{2,1,0:T(8,128)(2,1)S(1)}, u32[]{:S(2)}, u32[]{:S(2)}) %collective-permute-start.5) | collective-permute-done | bytes 131104 | tf_op jit(solution)/shard_map/ppermute | solution.py:136
  18.0 0.1 broadcast_select_fusion
  18.0 0.1 collective-permute-start.7
  18.1 2.5 %collective-permute-start.6 = (bf16[128,1024]{1,0:T(8,128)(2,1)S(1)}, bf16[128,1024]{1,0:T(8,128)(2,1)S(1)}, u32[]{:S(2)}, u32[]{:S(2)}) collective-permute-start(bf16[128,1024]{1,0:T(8,128)(2,1)S(1)} %get-tuple-element.41), channel_id=1, source_target_pairs={{1,2},{2,1},{5,6},{6,5},{9,10},{10,9},{13,14},{14,13},{17,18},{18,... | collective-permute-start | bytes 786440 | tf_op jit(solution)/shard_map/ppermute | solution.py:540
  20.7 0.0 copy-done.1
  20.7 3.1 %shard_map.79 = (f32[32,8,1024]{2,1,0:T(8,128)S(1)}, bf16[1032,8,256]{2,1,0:T(8,128)(2,1)S(1)}, f32[8,1152]{1,0:T(8,128)S(1)}) custom-call(bf16[128,1024]{1,0:T(8,128)(2,1)S(1)} %maximum_bitcast_fusion.1.near_ref, bf16[128,1024]{1,0:T(8,128)(2,1)S(1)} %maximum_bitcast_fusion.far_ref, f32[64,8,128]{2,1,0:T(8,128)S(1)} %get-tuple-element.28.presence_ref, ...), custom_call_target="tpu_custom_call" | custom-call | flops 2113929216 | bytes 8000000 | tf_op jit(solution)/shard_map/pallas_call | solution.py:432
  23.8 0.0 collective-permute-done.7.halo_ref
  23.8 1.4 %shard_map.80 = (bf16[1032,8,256]{2,1,0:T(8,128)(2,1)S(1)}, f32[8,1152]{1,0:T(8,128)S(1)}) custom-call(bf16[128,1024]{1,0:T(8,128)(2,1)S(1)} %collective-permute-done.7.halo_ref, f32[32,8,1024]{2,1,0:T(8,128)S(1)} %get-tuple-element.30.own_ref, f32[64,8,128]{2,1,0:T(8,128)S(1)} %get-tuple-element.28.presence_ref, ...), custom_call_target="tpu_custom_call", output_to_operand_aliasing={{0}: (6, {})} | custom-call | flops 838860800 | bytes 4000000 | tf_op jit(solution)/shard_map/pallas_call | solution.py:453
  25.2 0.6 %collective-permute-done.6.halo_ref = bf16[128,1024]{1,0:T(8,128)(2,1)S(1)} collective-permute-done((bf16[128,1024]{1,0:T(8,128)(2,1)S(1)}, bf16[128,1024]{1,0:T(8,128)(2,1)S(1)}, u32[]{:S(2)}, u32[]{:S(2)}) %collective-permute-start.6) | collective-permute-done | bytes 262176 | tf_op jit(solution)/shard_map/ppermute | solution.py:540
  25.8 1.5 %shard_map.81 = (bf16[1032,8,256]{2,1,0:T(8,128)(2,1)S(1)}, f32[2,8,128]{2,1,0:T(8,128)S(1)}) custom-call(bf16[128,1024]{1,0:T(8,128)(2,1)S(1)} %collective-permute-done.6.halo_ref, f32[32,8,1024]{2,1,0:T(8,128)S(1)} %get-tuple-element.30.own_ref, f32[64,8,128]{2,1,0:T(8,128)S(1)} %get-tuple-element.28.presence_ref, ...), custom_call_target="tpu_custom_call", output_to_operand_aliasing={{0}: (8, {})} | custom-call | flops 838860800 | bytes 4000000 | tf_op jit(solution)/shard_map/pallas_call | solution.py:477
  27.3 2.4 %collective-permute-start.8 = (f32[2,8,128]{2,1,0:T(8,128)S(1)}, f32[2,8,128]{2,1,0:T(8,128)S(1)}, u32[]{:S(2)}, u32[]{:S(2)}) collective-permute-start(f32[2,8,128]{2,1,0:T(8,128)S(1)} %get-tuple-element.37), channel_id=1, source_target_pairs={{0,16},{4,20},{8,24},{12,28},{16,0},{20,4},{24,8},{28,12},{1,17},{... | collective-permute-start | bytes 24584 | tf_op jit(solution)/shard_map/ppermute | solution.py:553
  29.7 2.4 %shard_map.82.refs_0_ = bf16[1024,8,256]{2,1,0:T(8,128)(2,1)} custom-call(s32[1024]{0:T(1024)S(1)} %bitcast.35, bf16[1032,8,256]{2,1,0:T(8,128)(2,1)S(1)} %get-tuple-element.36.table_ref), custom_call_target="tpu_custom_call" | custom-call | bytes 15360000 | tf_op jit(solution)/shard_map/pallas_call | solution.py:498
  32.2 0.0 collective-permute-done.8
  32.2 2.1 %collective-permute-start.11 = (f32[2,8,128]{2,1,0:T(8,128)S(1)}, f32[2,8,128]{2,1,0:T(8,128)S(1)}, u32[]{:S(2)}, u32[]{:S(2)}) collective-permute-start(f32[2,8,128]{2,1,0:T(8,128)S(1)} %add.52), channel_id=1, source_target_pairs={{0,12},{4,8},{8,4},{12,0},{16,28},{20,24},{24,20},{28,16},{1,13},{... | collective-permute-start | bytes 24584 | tf_op jit(solution)/shard_map/ppermute | solution.py:553
  34.3 0.2 collective-permute-start.10
  34.5 1.2 %collective-permute-start.9 = (f32[2,8,128]{2,1,0:T(8,128)S(1)}, f32[2,8,128]{2,1,0:T(8,128)S(1)}, u32[]{:S(2)}, u32[]{:S(2)}) collective-permute-start(f32[2,8,128]{2,1,0:T(8,128)S(1)} %add.52), channel_id=1, source_target_pairs={{0,4},{4,0},{8,12},{12,8},{16,20},{20,16},{24,28},{28,24},{1,5},{5... | collective-permute-start | bytes 24584 | tf_op jit(solution)/shard_map/ppermute | solution.py:553
  35.7 1.6 %shard_map.83 = bf16[1024,8,256]{2,1,0:T(8,128)(2,1)} custom-call(s32[1024]{0:T(1024)S(1)} %bitcast.36, bf16[1032,8,256]{2,1,0:T(8,128)(2,1)S(1)} %get-tuple-element.36.table_ref, bf16[1024,8,256]{2,1,0:T(8,128)(2,1)} %shard_map.82.refs_0_), custom_call_target="tpu_custom_call", output_to_operand_aliasing={{}: (2, {})} | custom-call | bytes 5120000 | tf_op jit(solution)/shard_map/pallas_call | solution.py:498
  37.4 0.0 collective-permute-done.11
  37.4 0.6 %collective-permute-done.10 = f32[2,8,128]{2,1,0:T(8,128)S(1)} collective-permute-done((f32[2,8,128]{2,1,0:T(8,128)S(1)}, f32[2,8,128]{2,1,0:T(8,128)S(1)}, u32[]{:S(2)}, u32[]{:S(2)}) %collective-permute-start.10) | collective-permute-done | bytes 8224 | tf_op jit(solution)/shard_map/ppermute | solution.py:553
  38.0 0.2 collective-permute-done.9
  38.2 0.6 %fusion.1 = f32[1024]{0:T(1024)} fusion(f32[2,8,128]{2,1,0:T(8,128)S(1)} %add_add_fusion), kind=kLoop, calls=%fused_computation.20 | loop fusion | flops 2048 | bytes 12288 | tf_op jit(solution)/shard_map/div | solution.py:598
  (8 shorter events, 0.1 us)
Async XLA Ops:
  1.8 18.9 %copy-start.1 = (f32[1,1024]{1,0:T(1,128)S(1)}, f32[1,1024]{1,0:T(1,128)}, u32[]{:S(2)}) copy-start(f32[1,1024]{1,0:T(1,128)} %constant.62.clone.weights_ref) | copy-start | bytes 12292
  1.8 9.3 %collective-permute-start.4 = (bf16[2,4,8,1024]{3,2,1,0:T(8,128)(2,1)S(1)}, bf16[2,4,8,1024]{3,2,1,0:T(8,128)(2,1)S(1)}, u32[]{:S(2)}, u32[]{:S(2)}) collective-permute-start(bf16[2,4,8,1024]{3,2,1,0:T(8,128)(2,1)S(1)} %pad_maximum_fusion), channel_id=1, source_target_pairs={{0,8},{4,12},{8,0},{12,4},{16,24},{20,28},{24,16},{28,20},{1,9},{5... | collective-permute-start | bytes 393224 | tf_op jit(solution)/shard_map/ppermute | solution.py:136
  3.5 10.2 %collective-permute-start.3 = (bf16[4,8,1024]{2,1,0:T(8,128)(2,1)S(1)}, bf16[4,8,1024]{2,1,0:T(8,128)(2,1)S(1)}, u32[]{:S(2)}, u32[]{:S(2)}) collective-permute-start(bf16[4,8,1024]{2,1,0:T(8,128)(2,1)S(1)} %get-tuple-element.46), channel_id=1, source_target_pairs={{0,16},{4,20},{8,24},{12,28},{16,0},{20,4},{24,8},{28,12},{1,17},{... | collective-permute-start | bytes 196616 | tf_op jit(solution)/shard_map/ppermute | solution.py:136
  6.1 11.2 %collective-permute-start.2 = (bf16[4,8,1024]{2,1,0:T(8,128)(2,1)S(1)}, bf16[4,8,1024]{2,1,0:T(8,128)(2,1)S(1)}, u32[]{:S(2)}, u32[]{:S(2)}) collective-permute-start(bf16[4,8,1024]{2,1,0:T(8,128)(2,1)S(1)} %get-tuple-element.47), channel_id=1, source_target_pairs={{0,20},{4,16},{8,28},{12,24},{16,4},{20,0},{24,12},{28,8},{1,21},{... | collective-permute-start | bytes 196616 | tf_op jit(solution)/shard_map/ppermute | solution.py:136
  7.3 9.9 %collective-permute-start.1 = (bf16[4,8,1024]{2,1,0:T(8,128)(2,1)S(1)}, bf16[4,8,1024]{2,1,0:T(8,128)(2,1)S(1)}, u32[]{:S(2)}, u32[]{:S(2)}) collective-permute-start(bf16[4,8,1024]{2,1,0:T(8,128)(2,1)S(1)} %get-tuple-element.48), channel_id=1, source_target_pairs={{0,24},{4,28},{8,16},{12,20},{16,8},{20,12},{24,0},{28,4},{1,25},{... | collective-permute-start | bytes 196616 | tf_op jit(solution)/shard_map/ppermute | solution.py:136
  9.8 7.5 %collective-permute-start = (bf16[4,8,1024]{2,1,0:T(8,128)(2,1)S(1)}, bf16[4,8,1024]{2,1,0:T(8,128)(2,1)S(1)}, u32[]{:S(2)}, u32[]{:S(2)}) collective-permute-start(bf16[4,8,1024]{2,1,0:T(8,128)(2,1)S(1)} %get-tuple-element.49), channel_id=1, source_target_pairs={{0,28},{4,24},{8,20},{12,16},{16,12},{20,8},{24,4},{28,0},{1,29},{... | collective-permute-start | bytes 196616 | tf_op jit(solution)/shard_map/ppermute | solution.py:136
  11.2 6.8 %collective-permute-start.5 = (bf16[8,8,1024]{2,1,0:T(8,128)(2,1)S(1)}, bf16[8,8,1024]{2,1,0:T(8,128)(2,1)S(1)}, u32[]{:S(2)}, u32[]{:S(2)}) collective-permute-start(bf16[8,8,1024]{2,1,0:T(8,128)(2,1)S(1)} %pad_maximum_fusion.1), channel_id=1, source_target_pairs={{0,4},{4,0},{8,12},{12,8},{16,20},{20,16},{24,28},{28,24},{1,5},{5... | collective-permute-start | bytes 393224 | tf_op jit(solution)/shard_map/ppermute | solution.py:136
  13.7 1.7 %copy-start = (bf16[1024,1280]{1,0:T(8,128)(2,1)S(1)}, bf16[1024,1280]{1,0:T(8,128)(2,1)}, u32[]{:S(2)}) copy-start(bf16[1024,1280]{1,0:T(8,128)(2,1)} %constant.61.clone.tables_ref) | copy-start | bytes 7864324
  18.0 5.8 %collective-permute-start.7 = (bf16[128,1024]{1,0:T(8,128)(2,1)S(1)}, bf16[128,1024]{1,0:T(8,128)(2,1)S(1)}, u32[]{:S(2)}, u32[]{:S(2)}) collective-permute-start(bf16[128,1024]{1,0:T(8,128)(2,1)S(1)} %get-tuple-element.40), channel_id=1, source_target_pairs={{0,1},{2,3},{1,0},{3,2},{4,5},{6,7},{5,4},{7,6},{8,9},{10,11},{9,8... | collective-permute-start | bytes 786440 | tf_op jit(solution)/shard_map/ppermute | solution.py:540
  18.1 7.7 %collective-permute-start.6 = (bf16[128,1024]{1,0:T(8,128)(2,1)S(1)}, bf16[128,1024]{1,0:T(8,128)(2,1)S(1)}, u32[]{:S(2)}, u32[]{:S(2)}) collective-permute-start(bf16[128,1024]{1,0:T(8,128)(2,1)S(1)} %get-tuple-element.41), channel_id=1, source_target_pairs={{1,2},{2,1},{5,6},{6,5},{9,10},{10,9},{13,14},{14,13},{17,18},{18,... | collective-permute-start | bytes 786440 | tf_op jit(solution)/shard_map/ppermute | solution.py:540
  27.3 4.8 %collective-permute-start.8 = (f32[2,8,128]{2,1,0:T(8,128)S(1)}, f32[2,8,128]{2,1,0:T(8,128)S(1)}, u32[]{:S(2)}, u32[]{:S(2)}) collective-permute-start(f32[2,8,128]{2,1,0:T(8,128)S(1)} %get-tuple-element.37), channel_id=1, source_target_pairs={{0,16},{4,20},{8,24},{12,28},{16,0},{20,4},{24,8},{28,12},{1,17},{... | collective-permute-start | bytes 24584 | tf_op jit(solution)/shard_map/ppermute | solution.py:553
  32.2 5.2 %collective-permute-start.11 = (f32[2,8,128]{2,1,0:T(8,128)S(1)}, f32[2,8,128]{2,1,0:T(8,128)S(1)}, u32[]{:S(2)}, u32[]{:S(2)}) collective-permute-start(f32[2,8,128]{2,1,0:T(8,128)S(1)} %add.52), channel_id=1, source_target_pairs={{0,12},{4,8},{8,4},{12,0},{16,28},{20,24},{24,20},{28,16},{1,13},{... | collective-permute-start | bytes 24584 | tf_op jit(solution)/shard_map/ppermute | solution.py:553
  34.3 3.7 %collective-permute-start.10 = (f32[2,8,128]{2,1,0:T(8,128)S(1)}, f32[2,8,128]{2,1,0:T(8,128)S(1)}, u32[]{:S(2)}, u32[]{:S(2)}) collective-permute-start(f32[2,8,128]{2,1,0:T(8,128)S(1)} %add.52), channel_id=1, source_target_pairs={{0,8},{4,12},{8,0},{12,4},{16,24},{20,28},{24,16},{28,20},{1,9},{5... | collective-permute-start | bytes 24584 | tf_op jit(solution)/shard_map/ppermute | solution.py:553
  34.5 3.7 %collective-permute-start.9 = (f32[2,8,128]{2,1,0:T(8,128)S(1)}, f32[2,8,128]{2,1,0:T(8,128)S(1)}, u32[]{:S(2)}, u32[]{:S(2)}) collective-permute-start(f32[2,8,128]{2,1,0:T(8,128)S(1)} %add.52), channel_id=1, source_target_pairs={{0,4},{4,0},{8,12},{12,8},{16,20},{20,16},{24,28},{28,24},{1,5},{5... | collective-permute-start | bytes 24584 | tf_op jit(solution)/shard_map/ppermute | solution.py:553
